TPU v7x, 32 devices: a whole 2x2x4 slice. The times are simulated.
32 devices in a mesh: dp: 8 (over y, x, core), tensor: 4 (over z).
Axes of the slice: x: 2, y: 2, z: 4, core: 2. Of those that a mesh axis runs over, the one named last changes fastest.
Arguments:
- latent: bfloat16 [4608, 512], P('dp'), may hold values from -6 to 6
- q_nope: bfloat16 [4608, 2048], P('dp', 'tensor'), may hold values from -6 to 6
- q_rope: bfloat16 [4608, 1024], P('dp', 'tensor'), may hold values from -40 to 40
- k_rope: bfloat16 [4608, 64], P('dp'), may hold values from -4.5 to 4.5
- grad_out: bfloat16 [4608, 2048], P('dp', 'tensor'), may hold values from -6 to 6
- offsets: int32 [8], P('dp'), may hold values from 1 to 575
- weight: bfloat16 [256, 16, 512], P(None, 'tensor'), may hold values from -0.25 to 0.25
- basis: float32 [512, 512], replicated, may hold values from -1 to 1
- first_moment: float32 [256, 16, 512], P('dp', 'tensor'), may hold values from -30 to 30
- second_rot: float32 [256, 16, 512], P('dp', 'tensor'), may hold values from 1 to 400
- second_plain: float32 [256, 16, 512], P('dp', 'tensor'), may hold values from 1 to 400
Outputs:
- grad_latent: bfloat16 [4608, 512], P(('dp', 'tensor'))
- new_weight: bfloat16 [256, 16, 512], P(None, 'tensor')
- new_first: float32 [256, 16, 512], P('dp', 'tensor')
- new_second: float32 [256, 16, 512], P('dp', 'tensor')
- new_plain: float32 [256, 16, 512], P('dp', 'tensor')
All inputs are finite; a program needn't handle non-finite values.
Results may differ from a plain program's by a relative error of at most 0.011.
Values may be sent and summed in bfloat16 or wider, within the bound.
No kernel may reach another device: no remote copies, remote signals or barrier semaphores. Data moves between devices by JAX's collectives and lax.ppermute only.
A program may use at most 64 MiB of HBM per device.

v0:
```python
import jax
import jax.numpy as jnp
from jax import lax
from jax.sharding import PartitionSpec as P

beta_first = 0.9
beta_second = 0.95
epsilon = 1e-08
learn_rate = 0.002
decay_rate = 0.1
blend_share = 0.5


def attend_back(
    query_main, query_side, key_side, key_main, value_rows, out_grads, visible, score_scale
):
    f32 = jnp.float32
    scores = (
        jnp.einsum("ihd,jhd->hij", query_main, key_main, preferred_element_type=f32)
        + jnp.einsum("ihe,je->hij", query_side, key_side, preferred_element_type=f32)
    ) * score_scale
    masked = jnp.where(visible[None], scores, -jnp.inf)
    row_max = jnp.max(masked, axis=-1, keepdims=True)
    exp_terms = jnp.where(visible[None], jnp.exp(masked - row_max), 0.0)
    attn_probs = exp_terms / jnp.sum(exp_terms, axis=-1, keepdims=True)
    probs_low = attn_probs.astype(jnp.bfloat16)
    attended = jnp.einsum("hij,jhd->ihd", probs_low, value_rows, preferred_element_type=f32)
    row_delta = jnp.sum(out_grads.astype(f32) * attended, axis=-1)
    grad_probs = jnp.einsum("ihd,jhd->hij", out_grads, value_rows, preferred_element_type=f32)
    grad_scores = (
        attn_probs * (grad_probs - jnp.transpose(row_delta)[:, :, None]) * score_scale
    ).astype(jnp.bfloat16)
    grad_keys = jnp.einsum("hij,ihd->jhd", grad_scores, query_main, preferred_element_type=f32)
    grad_values = jnp.einsum("hij,ihd->jhd", probs_low, out_grads, preferred_element_type=f32)
    return jnp.concatenate([grad_keys, grad_values], axis=-1).astype(jnp.bfloat16)


def local(
    latent,
    q_nope,
    q_rope,
    k_rope,
    grad_out,
    offsets,
    weight,
    basis,
    first_moment,
    second_rot,
    second_plain,
):
    f32 = jnp.float32
    highest = lax.Precision.HIGHEST
    seq_len = latent.shape[0]
    width_rows, head_count, latent_dim = weight.shape
    head_dim = width_rows // 2
    rope_dim = k_rope.shape[1]
    score_scale = float(head_dim + rope_dim) ** (-0.5)
    positions = jnp.arange(seq_len, dtype=jnp.int32)
    visible = positions[None, :] <= jnp.maximum(positions[:, None], offsets[0] - 1)
    query_main = q_nope.reshape(seq_len, head_count, head_dim)
    query_side = q_rope.reshape(seq_len, head_count, rope_dim)
    out_grads = grad_out.reshape(seq_len, head_count, head_dim)
    key_value = jnp.einsum("tc,rhc->thr", latent, weight, preferred_element_type=f32).astype(
        jnp.bfloat16
    )
    key_main = key_value[:, :, :head_dim]
    value_rows = key_value[:, :, head_dim:]
    slab_rows = width_rows // lax.axis_size("dp")
    grad_kv = attend_back(
        query_main, query_side, k_rope, key_main, value_rows, out_grads, visible, score_scale
    )
    slab_grad = lax.psum_scatter(
        jnp.einsum("thr,tc->rhc", grad_kv, latent, preferred_element_type=f32),
        "dp",
        scatter_dimension=0,
        tiled=True,
    )
    partial_value = jnp.einsum("thr,rhc->tc", grad_kv, weight, preferred_element_type=f32)
    grad_latent = lax.psum_scatter(partial_value, "tensor", scatter_dimension=0, tiled=True).astype(
        jnp.bfloat16
    )
    own_rows = lax.dynamic_slice_in_dim(
        weight, lax.axis_index("dp") * slab_rows, slab_rows, 0
    ).astype(f32)
    rotated = jnp.einsum("rhc,ce->rhe", slab_grad, basis, precision=highest)
    moment = beta_first * first_moment + (1.0 - beta_first) * rotated
    rotated_sq = beta_second * second_rot + (1.0 - beta_second) * rotated * rotated
    plain_sq = beta_second * second_plain + (1.0 - beta_second) * slab_grad * slab_grad
    stacked = jnp.stack([moment / (jnp.sqrt(rotated_sq) + epsilon), moment])
    turned = jnp.einsum("srhe,ce->srhc", stacked, basis, precision=highest)
    direction = blend_share * turned[0] + blend_share * turned[1] / (jnp.sqrt(plain_sq) + epsilon)
    new_slab = (own_rows - learn_rate * (direction + decay_rate * own_rows)).astype(jnp.bfloat16)
    new_weight = lax.all_gather(new_slab, "dp", axis=0, tiled=True)
    return (grad_latent, new_weight, moment, rotated_sq, plain_sq)


def solution(mesh):
    return jax.shard_map(
        local,
        mesh=mesh,
        in_specs=(
            P("dp", None),
            P("dp", "tensor"),
            P("dp", "tensor"),
            P("dp", None),
            P("dp", "tensor"),
            P("dp"),
            P(None, "tensor", None),
            P(),
            P("dp", "tensor", None),
            P("dp", "tensor", None),
            P("dp", "tensor", None),
        ),
        out_specs=(
            P(("dp", "tensor"), None),
            P(None, "tensor", None),
            P("dp", "tensor", None),
            P("dp", "tensor", None),
            P("dp", "tensor", None),
        ),
        check_vma=False,
    )
```

profile of v0, /device:TPU:0, one launch (start us, length us, event | category | flops | bytes accessed | tf_op | source)
XLA Modules:
  0.0 150.5 jit_solution(15295552792562103967)
XLA Ops:
  7.2 1.2 copy.62
  9.1 0.2 iota_compare_fusion
  9.4 3.3 %fusion.12 = bf16[576,4,256]{2,0,1:T(8,128)(2,1)} fusion(bf16[576,512]{1,0:T(8,128)(2,1)} %param.11, bf16[256,4,512]{2,1,0:T(4,128)(2,1)} %param.17), kind=kOutput, calls=%fused_computation.17 | convolution fusion | flops 604569600 | bytes 2818048 | tf_op jit(solution)/shard_map/tc,rhc->thr/dot_general | solution.py:63
  12.7 3.5 %fusion.55 = f32[576,576,4]{1,0,2:T(8,128)} fusion(bf16[576,4,64]{0,2,1:T(8,128)(2,1)S(1)} %bitcast.112, bf16[576,64]{0,1:T(8,128)(2,1)S(1)} %copy-done.4), kind=kOutput, calls=%fused_computation.67 | convolution fusion | flops 169869312 | bytes 5677056 | tf_op jit(solution)/shard_map/ihe,je->hij/dot_general | solution.py:20
  16.2 8.2 %fusion.66 = (f32[4,576]{1,0:T(4,128)S(1)}, f32[4,576,576]{1,2,0:T(8,128)}) fusion(pred[576,576]{0,1:T(8,128)(4,1)S(1)} %iota_compare_fusion, f32[576,576,4]{1,0,2:T(8,128)} %fusion.55, bf16[576,4,256]{2,0,1:T(8,128)(2,1)} %fusion.12, bf16[576,512]{1,0:T(8,128)(2,1)S(1)} %copy-done.5), kind=kOutput, calls=%fused_computation.76 | convolution fusion | flops 347701824 | bytes 13132800 | tf_op jit(solution)/shard_map/sub | solution.py:24
  24.4 3.3 %fusion.11 = bf16[4,576,576]{1,2,0:T(8,128)(2,1)S(1)} fusion(f32[4,576,576]{1,2,0:T(8,128)} %get-tuple-element.31, f32[4,576]{1,0:T(4,128)S(1)} %get-tuple-element.30), kind=kLoop, calls=%fused_computation.13 | loop fusion | flops 2654208 | bytes 7971840 | tf_op jit(solution)/shard_map/convert_element_type | solution.py:26
  27.6 1.3 fusion.17
  29.0 1.7 %fusion.21 = bf16[576,4,128]{2,0,1:T(8,128)(2,1)} fusion(bf16[4,576,576]{1,2,0:T(8,128)(2,1)S(1)} %fusion.11, bf16[576,512]{1,0:T(8,128)(2,1)S(1)} %copy-done.6), kind=kOutput, calls=%fused_computation.25 | convolution fusion | flops 340033536 | bytes 3833856 | tf_op jit(solution)/shard_map/hij,ihd->jhd/dot_general | solution.py:34
  31.0 5.5 %fusion.18 = bf16[576,4,128]{2,0,1:T(8,128)(2,1)} fusion(f32[4,576]{1,0:T(4,128)S(1)} %copy.67, f32[4,576,576]{1,2,0:T(8,128)} %get-tuple-element.31, f32[4,576]{1,0:T(4,128)S(1)} %get-tuple-element.30, bf16[576,4,256]{2,0,1:T(8,128)(2,1)} %fusion.12, bf16[576,512]{1,0:T(8,128)(2,1)S(1)} %copy-done.6, bf16[576,512]{1,0:T(8,128)(2,1)S(1)} %copy-done.5), kind=kOutput, calls=%fused_computation.24 | convolution fusion | flops 686407680 | bytes 8275968 | tf_op jit(solution)/shard_map/hij,ihd->jhd/dot_general | solution.py:33
  36.5 3.9 %convolution_bitcast_fusion = f32[256,4,512]{2,0,1:T(8,128)} fusion(bf16[576,4,128]{2,0,1:T(8,128)(2,1)} %fusion.21, bf16[576,4,128]{2,0,1:T(8,128)(2,1)} %fusion.18, bf16[576,512]{1,0:T(8,128)(2,1)} %param.11), kind=kOutput, calls=%fused_computation.14 | convolution fusion | flops 606339072 | bytes 3866624 | tf_op jit(solution)/shard_map/thr,tc->rhc/dot_general | solution.py:73
  40.5 2.9 %convolution_bitcast_fusion.2 = f32[576,512]{1,0:T(8,128)} fusion(bf16[576,4,128]{2,0,1:T(8,128)(2,1)S(1)} %copy-done.8, bf16[576,4,128]{2,0,1:T(8,128)(2,1)} %fusion.18, bf16[256,4,512]{2,1,0:T(4,128)(2,1)S(1)} %copy-done.1), kind=kOutput, calls=%fused_computation.20 | convolution fusion | flops 606339072 | bytes 3407872 | tf_op jit(solution)/shard_map/thr,rhc->tc/dot_general | solution.py:78
  43.4 0.2 all-gather.2.cloned.1.call-start
  43.6 0.2 copy.60
  43.8 40.6 %reduce-scatter.5.cloned.1.call-done = f32[32,4,512]{2,0,1:T(8,128)} async-done(((f32[256,4,512]{2,0,1:T(8,128)}), f32[32,4,512]{2,0,1:T(8,128)}) %reduce-scatter.5.cloned.1.call-update) | async-done | bytes 262160 | tf_op jit(solution)/shard_map/reduce_scatter | solution.py:72
  84.5 2.0 %divide_bitcast_fusion = (f32[1,32,4,512]{3,1,2,0:T(8,128)S(1)}, f32[32,4,512]{2,0,1:T(8,128)S(1)}, f32[32,4,512]{2,0,1:T(8,128)S(1)}) fusion(f32[32,4,512]{2,1,0:T(4,128)S(1)} %copy-done.3, f32[32,4,512]{2,1,0:T(4,128)} %param.19, f32[32,4,512]{2,0,1:T(8,128)} %reduce-scatter.5.cloned.1.call-done, f32[512,512]{1,0:T(8,128)S(1)} %copy-done), kind=kOutput, calls=%fused_computation.66 | convolution fusion | flops 403243008 | bytes 2621440 | tf_op jit(solution)/shard_map/rhc,ce->rhe/dot_general | solution.py:85
  86.4 1.1 fusion.22
  87.5 1.8 %fusion.47 = (bf16[32,4,512]{2,0,1:T(8,128)(2,1)}, f32[32,4,512]{2,0,1:T(8,128)S(1)}) fusion(f32[2,32,4,512]{3,1,2,0:T(8,128)S(1)} %fusion.22, bf16[256,4,512]{2,0,1:T(8,128)(2,1)S(1)} %copy.60, s32[]{:T(128)S(6)} %select_n.12, f32[32,4,512]{2,0,1:T(8,128)S(1)} %copy-done.2, f32[32,4,512]{2,1,0:T(4,128)} %param.21), kind=kLoop, calls=%fused_computation.53 | loop fusion | flops 983040 | bytes 1572868 | tf_op jit(solution)/shard_map/convert_element_type | solution.py:92
  89.4 26.7 %reduce-scatter.3.cloned.1.call-done = f32[144,512]{1,0:T(8,128)} async-done(((f32[576,512]{1,0:T(8,128)}), f32[144,512]{1,0:T(8,128)}) %reduce-scatter.3.cloned.1.call-update) | async-done | bytes 294928 | tf_op jit(solution)/shard_map/reduce_scatter | solution.py:79
  116.1 1.6 %convert_element_type.30 = bf16[144,512]{1,0:T(8,128)(2,1)} convert(f32[144,512]{1,0:T(8,128)} %reduce-scatter.3.cloned.1.call-done) | non-fusion elementwise | flops 73728 | bytes 442368 | tf_op jit(solution)/shard_map/convert_element_type | solution.py:79
  117.7 0.9 copy.76
  118.6 0.9 copy.78
  119.5 0.9 copy.77
  120.3 20.6 %all-gather.2.cloned.1.call-done = bf16[256,4,512]{2,0,1:T(8,128)(2,1)} async-done(((bf16[32,4,512]{2,0,1:T(8,128)(2,1)}), bf16[256,4,512]{2,0,1:T(8,128)(2,1)}) %all-gather.2.cloned.1.call-update) | async-done | bytes 1048592 | tf_op jit(solution)/shard_map/all_gather | solution.py:93
  141.0 3.0 %copy.75 = bf16[256,4,512]{2,1,0:T(4,128)(2,1)} copy(bf16[256,4,512]{2,0,1:T(8,128)(2,1)} %all-gather.2.cloned.1.call-done) | data formatting | bytes 2097152
  (26 shorter events, 0.5 us)
Async XLA Ops:
  7.2 77.3 %copy-start = (f32[512,512]{1,0:T(8,128)S(1)}, f32[512,512]{1,0:T(8,128)}, u32[]{:S(2)}) copy-start(f32[512,512]{1,0:T(8,128)} %param.18) | copy-start | bytes 3145732
  7.2 5.5 %copy-start.4 = (bf16[576,64]{0,1:T(8,128)(2,1)S(1)}, bf16[576,64]{0,1:T(8,128)(2,1)}, u32[]{:S(2)}) copy-start(bf16[576,64]{0,1:T(8,128)(2,1)} %param.14) | copy-start | bytes 221188
  7.2 77.3 %reduce-scatter.5.cloned.1.call-start = ((), (), s32[]{:S(2)}) async-start(), calls=%async_computation.3 | async-start | bytes 2359296 | tf_op jit(solution)/shard_map/reduce_scatter | solution.py:72
  12.7 3.5 %copy-start.5 = (bf16[576,512]{1,0:T(8,128)(2,1)S(1)}, bf16[576,512]{1,0:T(8,128)(2,1)}, u32[]{:S(2)}) copy-start(bf16[576,512]{1,0:T(8,128)(2,1)} %param.12) | copy-start | bytes 1769476
  24.4 3.3 %copy-start.6 = (bf16[576,512]{1,0:T(8,128)(2,1)S(1)}, bf16[576,512]{1,0:T(8,128)(2,1)}, u32[]{:S(2)}) copy-start(bf16[576,512]{1,0:T(8,128)(2,1)} %param.15) | copy-start | bytes 1769476
  24.4 3.3 %copy-start.7 = (bf16[576,4,256]{2,0,1:T(8,128)(2,1)S(1)}, bf16[576,4,256]{2,0,1:T(8,128)(2,1)}, u32[]{:S(2)}) copy-start(bf16[576,4,256]{2,0,1:T(8,128)(2,1)} %fusion.12) | copy-start | bytes 3538948
  36.5 4.0 %copy-start.1 = (bf16[256,4,512]{2,1,0:T(4,128)(2,1)S(1)}, bf16[256,4,512]{2,1,0:T(4,128)(2,1)}, u32[]{:S(2)}) copy-start(bf16[256,4,512]{2,1,0:T(4,128)(2,1)} %param.17) | copy-start | bytes 3145732
  36.5 4.0 %copy-start.8 = (bf16[576,4,128]{2,0,1:T(8,128)(2,1)S(1)}, bf16[576,4,128]{2,0,1:T(8,128)(2,1)}, u32[]{:S(2)}) copy-start(bf16[576,4,128]{2,0,1:T(8,128)(2,1)} %fusion.21) | copy-start | bytes 1769476
  40.4 44.1 %copy-start.3 = (f32[32,4,512]{2,1,0:T(4,128)S(1)}, f32[32,4,512]{2,1,0:T(4,128)}, u32[]{:S(2)}) copy-start(f32[32,4,512]{2,1,0:T(4,128)} %param.20) | copy-start | bytes 786436
  40.4 75.7 %reduce-scatter.3.cloned.1.call-start = ((), (), s32[]{:S(2)}) async-start(), calls=%async_computation.2 | async-start | bytes 1474560 | tf_op jit(solution)/shard_map/reduce_scatter | solution.py:79
  43.4 97.6 %all-gather.2.cloned.1.call-start = ((), (), s32[]{:S(2)}) async-start(), calls=%async_computation.4 | async-start | bytes 1179648 | tf_op jit(solution)/shard_map/all_gather | solution.py:93
  84.5 3.0 %copy-start.2 = (f32[32,4,512]{2,0,1:T(8,128)S(1)}, f32[32,4,512]{2,0,1:T(8,128)}, u32[]{:S(2)}) copy-start(f32[32,4,512]{2,0,1:T(8,128)} %reduce-scatter.5.cloned.1.call-done) | copy-start | bytes 786436
Sparse Core Ops, SparseCore 0:
  40.5 43.8 reduce-scatter.4
  86.9 29.1 reduce-scatter.2
  118.7 22.2 all-gather.1
where the time goes:
time: 151 us
  waiting for transfers between devices  88 us (58%)
  matrix products  33.3 us (22%)
  between operations  14.5 us (10%)
  local copies, waits for them, and re-layouts  7.38 us (5%)
  other arithmetic  6.99 us (5%)
    reduce_scatter x1, waiting for transfers between devices, local(): lax.psum_scatter(jnp.einsum('thr,tc->rhc', grad_kv, latent, preferred_ele...  40.6 us
    reduce_scatter x1, waiting for transfers between devices, local(): lax.psum_scatter(partial_value, 'tensor', scatter_dimension=0, tiled=True)  26.7 us
    all_gather x1, waiting for transfers between devices, local(): new_weight = lax.all_gather(new_slab, 'dp', axis=0, tiled=True)  20.6 us
    sub x1, matrix products, attend_back(): exp_terms = jnp.where(visible[None], jnp.exp(masked - row_max), 0.0)  8.17 us
    unnamed x25, local copies, waits for them, and re-layouts  7.25 us
    dot_general x1, matrix products, attend_back(): jnp.einsum('hij,ihd->jhd', grad_scores, query_main, preferred_element_typ...  5.46 us
    dot_general x1, matrix products, local(): jnp.einsum('thr,tc->rhc', grad_kv, latent, preferred_element_type=f32)  3.91 us
    dot_general x1, matrix products, attend_back(): jnp.einsum('ihe,je->hij', query_side, key_side, preferred_element_type=f32)  3.5 us
  transfers between devices with their start and end apart: 3, of which 3 were waited for; matrix products, arithmetic and copies ran while one was open for 8% of the time, Pallas kernels for 0%

commit v1 on v0

v1 whole, which is shorter than its diff:
```python
import functools

import jax
import jax.numpy as jnp
from jax import lax
from jax.experimental import pallas as pl
from jax.experimental.pallas import tpu as pltpu
from jax.sharding import PartitionSpec as P

beta_first = 0.9
beta_second = 0.95
epsilon = 1e-08
learn_rate = 0.002
decay_rate = 0.1
blend_share = 0.5
log2_e = 1.4426950408889634
f32 = jnp.float32
bf16 = jnp.bfloat16
VMEM = pl.BlockSpec(memory_space=pltpu.VMEM)
SMEM = pl.BlockSpec(memory_space=pltpu.SMEM)


def mm(a, b):
    return lax.dot_general(a, b, (((1,), (0,)), ((), ())), preferred_element_type=f32)


def mm_nt(a, b):
    return lax.dot_general(a, b, (((1,), (1,)), ((), ())), preferred_element_type=f32)


def mm_tn(a, b):
    return lax.dot_general(a, b, (((0,), (0,)), ((), ())), preferred_element_type=f32)


def attend_kernel(
    ids, offsets, latent, q_nope, q_rope, k_rope, grad_out, weight, keep, send, glat, key_value, grad_kv, slab
):
    seq_len, latent_dim = latent.shape
    heads, width, _ = weight.shape
    head_dim = width // 2
    rope_dim = k_rope.shape[1]
    chips = keep.shape[0]
    rows = width // (2 * chips)
    parts = glat.shape[0]
    part_rows = seq_len // parts
    scale = float(head_dim + rope_dim) ** (-0.5)
    lat = latent[...]
    wall = weight[...].reshape(heads * width, latent_dim)
    key_value[...] = mm_nt(lat, wall).astype(bf16)
    limit = jnp.maximum(lax.broadcasted_iota(jnp.int32, (1, seq_len), 1), offsets[0] - 1)
    visible = lax.broadcasted_iota(jnp.int32, (seq_len, seq_len), 0) <= limit
    for h in range(heads):
        q_main = q_nope[:, h * head_dim : (h + 1) * head_dim]
        g_out = grad_out[:, h * head_dim : (h + 1) * head_dim]
        q_all = jnp.concatenate([q_main, q_rope[:, h * rope_dim : (h + 1) * rope_dim]], axis=1)
        keys = key_value[:, h * width : h * width + head_dim]
        values = key_value[:, h * width + head_dim : (h + 1) * width]
        k_all = jnp.concatenate([keys, k_rope[...]], axis=1)
        scores = jnp.where(visible, mm_nt(k_all, q_all), -1e30)
        top = jnp.max(scores, axis=0, keepdims=True)
        terms = jnp.exp2((scores - top) * (scale * log2_e))
        inv = 1.0 / jnp.sum(terms, axis=0, keepdims=True)
        probs = terms * inv
        grad_probs = mm_nt(values, g_out)
        delta = jnp.sum(probs * grad_probs, axis=0, keepdims=True)
        grad_scores = (probs * (grad_probs - delta) * scale).astype(bf16)
        grad_kv[:, h * width : h * width + head_dim] = mm(grad_scores, q_main).astype(bf16)
        grad_kv[:, h * width + head_dim : (h + 1) * width] = mm(probs.astype(bf16), g_out).astype(bf16)
    gkv = grad_kv[...]
    slab[...] = mm_tn(gkv, lat).reshape(heads, 2 * chips, rows, latent_dim)
    my_chip, my_core, my_part = ids[0], ids[1], ids[2]
    for k in range(chips):
        chip = lax.rem(my_chip + k, chips) if chips & (chips - 1) else my_chip ^ k
        mine, other = 2 * chip + my_core, 2 * chip + 1 - my_core
        for h in range(heads):
            keep[k, h * rows : (h + 1) * rows, :] = slab[h, mine].astype(bf16)
            send[k, h * rows : (h + 1) * rows, :] = slab[h, other].astype(bf16)
    gl = mm(gkv, wall).astype(bf16)
    for s in range(parts):
        to = lax.rem(s - my_part + parts, parts)
        glat[to] = gl[s * part_rows : (s + 1) * part_rows, :]


def add_kernel(keep, came, *outs):
    for k, out in enumerate(outs):
        total = keep[k].astype(f32) + came[k].astype(f32)
        out[...] = total.astype(out.dtype)


def soap_kernel(ids, weight, basis, first_moment, second_rot, second_plain, *refs):
    slab_out, new_first, new_second, new_plain, direction, grad, stage = refs[-7:]
    parts = refs[:-7]
    rows, heads, latent_dim = first_moment.shape
    grad[...] = functools.reduce(jnp.add, [p[...].astype(f32) for p in parts])
    turn = basis[...].astype(bf16)
    rotated = mm(grad[...].astype(bf16), turn)
    start = (2 * ids[0] + ids[1]) * rows
    for h in range(heads):
        own = slice(h * rows, (h + 1) * rows)
        rot = rotated[own]
        moment = beta_first * first_moment[:, h, :] + (1.0 - beta_first) * rot
        rot_sq = beta_second * second_rot[:, h, :] + (1.0 - beta_second) * rot * rot
        new_first[:, h, :] = moment
        new_second[:, h, :] = rot_sq
        stage[own, :] = (moment / (jnp.sqrt(rot_sq) + epsilon)).astype(bf16)
        stage[(heads + h) * rows : (heads + h + 1) * rows, :] = moment.astype(bf16)
    turned = mm_nt(stage[...], turn)
    for h in range(heads):
        own = slice(h * rows, (h + 1) * rows)
        g = grad[own, :]
        plain = beta_second * second_plain[:, h, :] + (1.0 - beta_second) * g * g
        new_plain[:, h, :] = plain
        back = turned[(heads + h) * rows : (heads + h + 1) * rows]
        direction[:, h, :] = blend_share * turned[own] + blend_share * back / (jnp.sqrt(plain) + epsilon)
    old = weight[pl.ds(start, rows)].astype(f32)
    slab_out[...] = (old - learn_rate * (direction[...] + decay_rate * old)).astype(bf16)


def place_kernel(ids, *refs):
    out = refs[-1]
    rows = refs[0].shape[0]
    chips = (len(refs) - 1) // 2
    for k in range(chips):
        chip = lax.rem(ids[0] - k + chips, chips) if chips & (chips - 1) else ids[0] ^ k
        out[pl.ds((2 * chip + ids[1]) * rows, rows)] = refs[k][...]
        out[pl.ds((2 * chip + 1 - ids[1]) * rows, rows)] = refs[chips + k][...]


def local(latent, q_nope, q_rope, k_rope, grad_out, offsets, weight, basis, first_moment, second_rot, second_plain):
    seq_len, latent_dim = latent.shape
    width, heads, _ = weight.shape
    dp, parts = lax.axis_size("dp"), lax.axis_size("tensor")
    chips = dp // 2
    rows = width // dp
    part_rows = seq_len // parts
    me = lax.axis_index("dp")
    ids = jnp.stack([me // 2, me % 2, lax.axis_index("tensor")]).astype(jnp.int32)

    def core_swap(x):
        return lax.ppermute(x, "dp", [(i, i ^ 1) for i in range(dp)])

    def chip_move(x, k):
        if chips & (chips - 1):
            pairs = [(i, (i + 2 * k) % dp) for i in range(dp)]
        else:
            pairs = [(i, i ^ (2 * k)) for i in range(dp)]
        return lax.ppermute(x, "dp", pairs)

    def part_move(x, s):
        return lax.ppermute(x, "tensor", [(i, (i + s) % parts) for i in range(parts)])

    params = pltpu.CompilerParams(vmem_limit_bytes=40 * 1024 * 1024)
    keep, send, glat = pl.pallas_call(
        attend_kernel,
        out_shape=(
            jax.ShapeDtypeStruct((chips, heads * rows, latent_dim), bf16),
            jax.ShapeDtypeStruct((chips, heads * rows, latent_dim), bf16),
            jax.ShapeDtypeStruct((parts, part_rows, latent_dim), bf16),
        ),
        in_specs=[SMEM, SMEM] + [VMEM] * 6,
        out_specs=(VMEM, VMEM, VMEM),
        scratch_shapes=[
            pltpu.VMEM((seq_len, heads * width), bf16),
            pltpu.VMEM((seq_len, heads * width), bf16),
            pltpu.VMEM((heads, dp, rows, latent_dim), f32),
        ],
        compiler_params=params,
        name="attend",
    )(ids, offsets, latent, q_nope, q_rope, k_rope, grad_out, jnp.transpose(weight, (1, 0, 2)))

    came = core_swap(send)
    sums = pl.pallas_call(
        add_kernel,
        out_shape=[jax.ShapeDtypeStruct((heads * rows, latent_dim), f32 if k == 0 else bf16) for k in range(chips)],
        in_specs=[VMEM, VMEM],
        out_specs=[VMEM] * chips,
        name="pair_sum",
    )(keep, came)
    got = [sums[0]] + [chip_move(sums[k], k) for k in range(1, chips)]
    glat_parts = [glat[0]] + [part_move(glat[s], s) for s in range(1, parts)]

    state = jax.ShapeDtypeStruct((rows, heads, latent_dim), f32)
    stage_rows = heads * rows
    new_slab, new_first, new_second, new_plain = pl.pallas_call(
        soap_kernel,
        out_shape=(jax.ShapeDtypeStruct((rows, heads, latent_dim), bf16), state, state, state),
        in_specs=[SMEM] + [VMEM] * (5 + chips),
        out_specs=(VMEM,) * 4,
        scratch_shapes=[
            pltpu.VMEM((rows, heads, latent_dim), f32),
            pltpu.VMEM((stage_rows, latent_dim), f32),
            pltpu.VMEM((2 * stage_rows, latent_dim), bf16),
        ],
        compiler_params=params,
        name="soap",
    )(ids, weight, basis, first_moment, second_rot, second_plain, *got)

    mine = [new_slab] + [chip_move(new_slab, k) for k in range(1, chips)]
    others = [core_swap(x) for x in mine]
    new_weight = pl.pallas_call(
        place_kernel,
        out_shape=jax.ShapeDtypeStruct((width, heads, latent_dim), bf16),
        in_specs=[SMEM] + [VMEM] * (2 * chips),
        out_specs=VMEM,
        name="place",
    )(ids, *mine, *others)
    grad_latent = functools.reduce(jnp.add, [x.astype(f32) for x in glat_parts]).astype(bf16)
    return (grad_latent, new_weight, new_first, new_second, new_plain)


def solution(mesh):
    state = P("dp", "tensor", None)
    return jax.shard_map(
        local,
        mesh=mesh,
        in_specs=(
            P("dp", None),
            P("dp", "tensor"),
            P("dp", "tensor"),
            P("dp", None),
            P("dp", "tensor"),
            P("dp"),
            P(None, "tensor", None),
            P(),
            state,
            state,
            state,
        ),
        out_specs=(P(("dp", "tensor"), None), P(None, "tensor", None), state, state, state),
        check_vma=False,
    )
```

time: 151 us -> 51.3 us (0.34)
  waiting for transfers between devices: 88 us -> 5.94 us
  matrix products: 33.3 us -> 0 us
  starting transfers between devices: 0.3 us -> 15.5 us
  Pallas kernels: 0 us -> 15 us
  between operations: 14.5 us -> 1.47 us
  other arithmetic: 6.99 us -> 1.72 us
  local copies, waits for them, and re-layouts: 7.38 us -> 11.2 us
    reduce_scatter x2 -> x0, waiting for transfers between devices: 67.3 us -> none  [the longest x1 40.6 us: local(): lax.psum_scatter(jnp.einsum('thr,tc->rhc', grad_kv, latent, preferred_ele...]
    dot_general x9 -> x0, matrix products: 25.1 us -> none  [the longest x1 5.46 us: attend_back(): jnp.einsum('hij,ihd->jhd', grad_scores, query_main, preferred_element_typ...]
    all_gather x1 -> x0, waiting for transfers between devices: 20.6 us -> none  [local(): new_weight = lax.all_gather(new_slab, 'dp', axis=0, tiled=True)]
    ppermute x0 -> x14, starting transfers between devices: none -> 15.5 us  [the longest x3 7.86 us: part_move(): lax.ppermute(x, 'tensor', [(i, (i + s) % parts) for i in range(parts)])]
    pallas_call x0 -> x4, Pallas kernels: none -> 15 us  [the longest x1 8.52 us: local(): pl.pallas_call(attend_kernel, out_shape=(jax.ShapeDtypeStruct((chips, hea...]
    sub x1 -> x0, matrix products: 8.17 us -> none  [attend_back(): exp_terms = jnp.where(visible[None], jnp.exp(masked - row_max), 0.0)]
    ppermute x0 -> x14, waiting for transfers between devices: none -> 5.94 us  [the longest x6 5.92 us: chip_move(): return lax.ppermute(x, 'dp', pairs)]
    convert_element_type x3 -> x1, other arithmetic: 6.76 us -> 1.65 us  [local(): functools.reduce(jnp.add, [x.astype(f32) for x in glat_parts]).astype(bf16)]
  transfers between devices with their start and end apart: 3 -> 14, of which waited for: 3 -> 4; matrix products, arithmetic and copies ran while one was open for 8% -> 5% of each run, Pallas kernels for 0% -> 8%
where the time goes in v1:
time: 51.3 us; the launch traced here: 50.9 us
  starting transfers between devices  15.5 us (30%)
  Pallas kernels  15 us (29%)
  local copies, waits for them, and re-layouts  11.2 us (22%)
  waiting for transfers between devices  5.94 us (12%)
  other arithmetic  1.72 us (3%)
  between operations  1.47 us (3%)
    unnamed x44, local copies, waits for them, and re-layouts  10.5 us
    pallas_call x1, Pallas kernels, local(): pl.pallas_call(attend_kernel, out_shape=(jax.ShapeDtypeStruct((chips, hea...  8.52 us
    ppermute x3, starting transfers between devices, part_move(): lax.ppermute(x, 'tensor', [(i, (i + s) % parts) for i in range(parts)])  7.86 us
    ppermute x6, starting transfers between devices, chip_move(): return lax.ppermute(x, 'dp', pairs)  6.98 us
    ppermute x6, waiting for transfers between devices, chip_move(): return lax.ppermute(x, 'dp', pairs)  5.92 us
    pallas_call x1, Pallas kernels, local(): pl.pallas_call(place_kernel, out_shape=jax.ShapeDtypeStruct((width, heads...  2.33 us
    pallas_call x1, Pallas kernels, local(): pl.pallas_call(add_kernel, out_shape=[jax.ShapeDtypeStruct((heads * rows,...  2.11 us
    pallas_call x1, Pallas kernels, local(): pl.pallas_call(soap_kernel, out_shape=(jax.ShapeDtypeStruct((rows, heads,...  2 us
  transfers between devices with their start and end apart: 14, of which 4 were waited for; matrix products, arithmetic and copies ran while one was open for 5% of the time, Pallas kernels for 8%

profile of v1, /device:TPU:0, one launch (start us, length us, event | category | flops | bytes accessed | tf_op | source)
XLA Modules:
  0.0 50.9 jit_solution(17137294692892066095)
XLA Ops:
  1.3 1.0 %copy.17.k_rope = bf16[576,64]{1,0:T(8,128)(2,1)S(1)} copy(bf16[576,64]{0,1:T(8,128)(2,1)} %param.14) | data formatting | bytes 147456 | tf_op args[3]
  2.3 1.5 %copy.19 = bf16[256,4,512]{2,0,1:T(8,128)(2,1)S(1)} copy(bf16[256,4,512]{2,1,0:T(4,128)(2,1)} %weight.1) | data formatting | bytes 2097152 | tf_op args[6]
  3.9 1.1 %copy-done.3 = bf16[576,512]{1,0:T(8,128)(2,1)S(1)} copy-done((bf16[576,512]{1,0:T(8,128)(2,1)S(1)}, bf16[576,512]{1,0:T(8,128)(2,1)}, u32[]{:S(2)}) %copy-start.3) | copy-done | bytes 589848
  5.0 1.1 %copy-done.4 = bf16[576,512]{1,0:T(8,128)(2,1)S(1)} copy-done((bf16[576,512]{1,0:T(8,128)(2,1)S(1)}, bf16[576,512]{1,0:T(8,128)(2,1)}, u32[]{:S(2)}) %copy-start.4) | copy-done | bytes 589848
  6.1 1.0 %copy-done.6 = bf16[576,256]{1,0:T(8,128)(2,1)S(1)} copy-done((bf16[576,256]{1,0:T(8,128)(2,1)S(1)}, bf16[576,256]{1,0:T(8,128)(2,1)}, u32[]{:S(2)}) %copy-start.6) | copy-done | bytes 294936
  7.0 8.5 %attend.1 = (bf16[4,128,512]{2,1,0:T(8,128)(2,1)S(1)}, bf16[4,128,512]{2,1,0:T(8,128)(2,1)S(1)}, bf16[4,144,512]{2,1,0:T(8,128)(2,1)S(1)}) custom-call(s32[3]{0:T(128)S(1)} %pad_add_fusion.ids, s32[1]{0:T(128)S(6)} %copy.20.offsets, bf16[576,512]{1,0:T(8,128)(2,1)S(1)} %copy-done.2, bf16[576,512]{1,0:T(8,128)(2,1)S(1)} %copy-done.3, ...), custom_call_target="tpu_custom_call" | custom-call | tf_op jit(solution)/shard_map/attend/pallas_call | solution.py:153
  17.6 2.6 %collective-permute-start = (bf16[144,512]{1,0:T(8,128)(2,1)}, bf16[144,512]{1,0:T(8,128)(2,1)}, u32[]{:S(2)}, u32[]{:S(2)}) collective-permute-start(bf16[144,512]{1,0:T(8,128)(2,1)} %get-tuple-element.27), channel_id=1, source_target_pairs={{0,1},{1,2},{2,3},{3,0},{4,5},{5,6},{6,7},{7,4},{8,9},{9,10},{10,1... | collective-permute-start | bytes 442376 | tf_op jit(solution)/shard_map/ppermute | solution.py:150
  20.1 0.8 %copy-done.13 = bf16[4,128,512]{2,1,0:T(8,128)(2,1)} copy-done((bf16[4,128,512]{2,1,0:T(8,128)(2,1)}, bf16[4,128,512]{2,1,0:T(8,128)(2,1)S(1)}, u32[]{:S(2)}) %copy-start.13) | copy-done | bytes 524312
  20.9 2.1 %pair_sum.1 = (f32[128,512]{1,0:T(8,128)}, bf16[128,512]{1,0:T(8,128)(2,1)}, bf16[128,512]{1,0:T(8,128)(2,1)}, bf16[128,512]{1,0:T(8,128)(2,1)}) custom-call(bf16[4,128,512]{2,1,0:T(8,128)(2,1)} %copy-done.5, bf16[4,128,512]{2,1,0:T(8,128)(2,1)} %copy-done.13), custom_call_target="tpu_custom_call" | custom-call | tf_op jit(solution)/shard_map/pair_sum/pallas_call | solution.py:172
  23.0 1.5 %collective-permute-start.4 = (bf16[128,512]{1,0:T(8,128)(2,1)}, bf16[128,512]{1,0:T(8,128)(2,1)S(1)}, u32[]{:S(2)}, u32[]{:S(2)}) collective-permute-start(bf16[128,512]{1,0:T(8,128)(2,1)} %get-tuple-element.20), channel_id=1, source_target_pairs={{0,8},{4,12},{8,0},{12,4},{16,24},{20,28},{24,16},{28,20},{1,9},{5... | collective-permute-start | bytes 393224 | tf_op jit(solution)/shard_map/ppermute | solution.py:147
  24.5 1.5 %collective-permute-start.5 = (bf16[128,512]{1,0:T(8,128)(2,1)}, bf16[128,512]{1,0:T(8,128)(2,1)S(1)}, u32[]{:S(2)}, u32[]{:S(2)}) collective-permute-start(bf16[128,512]{1,0:T(8,128)(2,1)} %get-tuple-element.21), channel_id=1, source_target_pairs={{0,16},{4,20},{8,24},{12,28},{16,0},{20,4},{24,8},{28,12},{1,17},{... | collective-permute-start | bytes 393224 | tf_op jit(solution)/shard_map/ppermute | solution.py:147
  26.5 3.2 %collective-permute-start.2 = (bf16[144,512]{1,0:T(8,128)(2,1)}, bf16[144,512]{1,0:T(8,128)(2,1)S(1)}, u32[]{:S(2)}, u32[]{:S(2)}) collective-permute-start(bf16[144,512]{1,0:T(8,128)(2,1)} %get-tuple-element.28), channel_id=1, source_target_pairs={{0,3},{1,0},{2,1},{3,2},{4,7},{5,4},{6,5},{7,6},{8,11},{9,8},{10,9... | collective-permute-start | bytes 442376 | tf_op jit(solution)/shard_map/ppermute | solution.py:150
  29.7 2.1 %collective-permute-start.1 = (bf16[144,512]{1,0:T(8,128)(2,1)}, bf16[144,512]{1,0:T(8,128)(2,1)S(1)}, u32[]{:S(2)}, u32[]{:S(2)}) collective-permute-start(bf16[144,512]{1,0:T(8,128)(2,1)} %get-tuple-element.29), channel_id=1, source_target_pairs={{0,2},{1,3},{2,0},{3,1},{4,6},{5,7},{6,4},{7,5},{8,10},{9,11},{10,... | collective-permute-start | bytes 442376 | tf_op jit(solution)/shard_map/ppermute | solution.py:150
  31.8 1.1 %collective-permute-done.5.refs_2_ = bf16[128,512]{1,0:T(8,128)(2,1)S(1)} collective-permute-done((bf16[128,512]{1,0:T(8,128)(2,1)}, bf16[128,512]{1,0:T(8,128)(2,1)S(1)}, u32[]{:S(2)}, u32[]{:S(2)}) %collective-permute-start.5) | collective-permute-done | bytes 131104 | tf_op jit(solution)/shard_map/ppermute | solution.py:147
  33.0 0.9 %copy-done.9 = f32[32,4,512]{2,1,0:T(4,128)S(1)} copy-done((f32[32,4,512]{2,1,0:T(4,128)S(1)}, f32[32,4,512]{2,1,0:T(4,128)}, u32[]{:S(2)}) %copy-start.9) | copy-done | bytes 262168
  33.9 0.9 %copy-done.10 = f32[128,512]{1,0:T(8,128)S(1)} copy-done((f32[128,512]{1,0:T(8,128)S(1)}, f32[128,512]{1,0:T(8,128)}, u32[]{:S(2)}) %copy-start.10) | copy-done | bytes 262168
  34.9 2.0 %soap.1 = (bf16[32,4,512]{2,1,0:T(4,128)(2,1)S(1)}, f32[32,4,512]{2,1,0:T(4,128)}, f32[32,4,512]{2,1,0:T(4,128)}, f32[32,4,512]{2,1,0:T(4,128)}) custom-call(s32[3]{0:T(128)S(1)} %pad_add_fusion.ids, bf16[256,4,512]{2,1,0:T(4,128)(2,1)S(1)} %copy-done, f32[512,512]{1,0:T(8,128)S(1)} %copy-done.1, f32[32,4,512]{2,1,0:T(4,128)S(1)} %copy-done.7, ...), custom_call_target="tpu_custom_call" | custom-call | tf_op jit(solution)/shard_map/soap/pallas_call | solution.py:184
  36.9 1.7 %collective-permute-start.9 = (bf16[32,4,512]{2,1,0:T(4,128)(2,1)S(1)}, bf16[32,4,512]{2,1,0:T(4,128)(2,1)S(1)}, u32[]{:S(2)}, u32[]{:S(2)}) collective-permute-start(bf16[32,4,512]{2,1,0:T(4,128)(2,1)S(1)} %get-tuple-element.23.refs_0_), channel_id=1, source_target_pairs={{0,24},{4,28},{8,16},{12,20},{16,8},{20,12},{24,0},{28,4},{1,25},{... | collective-permute-start | bytes 393224 | tf_op jit(solution)/shard_map/ppermute | solution.py:147
  38.6 1.0 %collective-permute-start.8 = (bf16[32,4,512]{2,1,0:T(4,128)(2,1)S(1)}, bf16[32,4,512]{2,1,0:T(4,128)(2,1)S(1)}, u32[]{:S(2)}, u32[]{:S(2)}) collective-permute-start(bf16[32,4,512]{2,1,0:T(4,128)(2,1)S(1)} %get-tuple-element.23.refs_0_), channel_id=1, source_target_pairs={{0,16},{4,20},{8,24},{12,28},{16,0},{20,4},{24,8},{28,12},{1,17},{... | collective-permute-start | bytes 393224 | tf_op jit(solution)/shard_map/ppermute | solution.py:147
  39.5 0.8 %collective-permute-start.7 = (bf16[32,4,512]{2,1,0:T(4,128)(2,1)S(1)}, bf16[32,4,512]{2,1,0:T(4,128)(2,1)S(1)}, u32[]{:S(2)}, u32[]{:S(2)}) collective-permute-start(bf16[32,4,512]{2,1,0:T(4,128)(2,1)S(1)} %get-tuple-element.23.refs_0_), channel_id=1, source_target_pairs={{0,8},{4,12},{8,0},{12,4},{16,24},{20,28},{24,16},{28,20},{1,9},{5... | collective-permute-start | bytes 393224 | tf_op jit(solution)/shard_map/ppermute | solution.py:147
  40.4 3.5 %collective-permute-done.9.refs_3_ = bf16[32,4,512]{2,1,0:T(4,128)(2,1)S(1)} collective-permute-done((bf16[32,4,512]{2,1,0:T(4,128)(2,1)S(1)}, bf16[32,4,512]{2,1,0:T(4,128)(2,1)S(1)}, u32[]{:S(2)}, u32[]{:S(2)}) %collective-permute-start.9) | collective-permute-done | bytes 131104 | tf_op jit(solution)/shard_map/ppermute | solution.py:147
  43.9 1.0 %collective-permute-done.8.refs_2_ = bf16[32,4,512]{2,1,0:T(4,128)(2,1)S(1)} collective-permute-done((bf16[32,4,512]{2,1,0:T(4,128)(2,1)S(1)}, bf16[32,4,512]{2,1,0:T(4,128)(2,1)S(1)}, u32[]{:S(2)}, u32[]{:S(2)}) %collective-permute-start.8) | collective-permute-done | bytes 131104 | tf_op jit(solution)/shard_map/ppermute | solution.py:147
  45.5 1.6 %fusion.2 = bf16[144,512]{1,0:T(8,128)(2,1)} fusion(bf16[144,512]{1,0:T(8,128)(2,1)S(1)} %collective-permute-done.2, bf16[144,512]{1,0:T(8,128)(2,1)S(1)} %collective-permute-done.1, bf16[144,512]{1,0:T(8,128)(2,1)} %collective-permute-done, bf16[4,144,512]{2,1,0:T(8,128)(2,1)S(1)} %get-tuple-element.16), kind=kLoop, calls=%fused_computation.4 | loop fusion | flops 589824 | bytes 737280 | tf_op jit(solution)/shard_map/convert_element_type | solution.py:207
  48.5 2.3 %place.1 = bf16[256,4,512]{2,1,0:T(4,128)(2,1)} custom-call(s32[3]{0:T(128)} %copy-done.12, bf16[32,4,512]{2,1,0:T(4,128)(2,1)} %copy-done.11, bf16[32,4,512]{2,1,0:T(4,128)(2,1)} %copy-done.16, bf16[32,4,512]{2,1,0:T(4,128)(2,1)} %copy-done.15, bf16[32,4,512]{2,1,0:T(4,128)(2,1)} %copy-done.14, bf16[32,4,512]{2,1,0:T(4,128)(2,1)} %copy-done.17, ...), custom_call_target="tpu_custom_call" | custom-call | tf_op jit(solution)/shard_map/place/pallas_call | solution.py:200
  (55 shorter events, 4.5 us)
Async XLA Ops:
  2.3 1.6 %copy-start.2 = (bf16[576,512]{1,0:T(8,128)(2,1)S(1)}, bf16[576,512]{1,0:T(8,128)(2,1)}, u32[]{:S(2)}) copy-start(bf16[576,512]{1,0:T(8,128)(2,1)} %latent.1) | copy-start | bytes 1769476
  3.9 29.0 %copy-start.12 = (s32[3]{0:T(128)}, s32[3]{0:T(128)S(1)}, u32[]{:S(2)}) copy-start(s32[3]{0:T(128)S(1)} %pad_add_fusion.ids) | copy-start | bytes 40
  7.0 25.9 %copy-start.1 = (f32[512,512]{1,0:T(8,128)S(1)}, f32[512,512]{1,0:T(8,128)}, u32[]{:S(2)}) copy-start(f32[512,512]{1,0:T(8,128)} %basis.1) | copy-start | bytes 3145732
  16.3 16.6 %copy-start = (bf16[256,4,512]{2,1,0:T(4,128)(2,1)S(1)}, bf16[256,4,512]{2,1,0:T(4,128)(2,1)}, u32[]{:S(2)}) copy-start(bf16[256,4,512]{2,1,0:T(4,128)(2,1)} %weight.1) | copy-start | bytes 3145732
  16.3 3.8 %collective-permute-start.3 = (bf16[4,128,512]{2,1,0:T(8,128)(2,1)S(1)}, bf16[4,128,512]{2,1,0:T(8,128)(2,1)S(1)}, u32[]{:S(2)}, u32[]{:S(2)}) collective-permute-start(bf16[4,128,512]{2,1,0:T(8,128)(2,1)S(1)} %get-tuple-element.18), channel_id=1, source_target_pairs={{0,4},{4,0},{8,12},{12,8},{16,20},{20,16},{24,28},{28,24},{1,5},{5... | collective-permute-start | bytes 1572872 | tf_op jit(solution)/shard_map/ppermute | solution.py:140
  17.6 22.0 %collective-permute-start = (bf16[144,512]{1,0:T(8,128)(2,1)}, bf16[144,512]{1,0:T(8,128)(2,1)}, u32[]{:S(2)}, u32[]{:S(2)}) collective-permute-start(bf16[144,512]{1,0:T(8,128)(2,1)} %get-tuple-element.27), channel_id=1, source_target_pairs={{0,1},{1,2},{2,3},{3,0},{4,5},{5,6},{6,7},{7,4},{8,9},{9,10},{10,1... | collective-permute-start | bytes 442376 | tf_op jit(solution)/shard_map/ppermute | solution.py:150
  20.9 12.0 %copy-start.7 = (f32[32,4,512]{2,1,0:T(4,128)S(1)}, f32[32,4,512]{2,1,0:T(4,128)}, u32[]{:S(2)}) copy-start(f32[32,4,512]{2,1,0:T(4,128)} %first_moment.1) | copy-start | bytes 786436
  20.9 12.0 %copy-start.8 = (f32[32,4,512]{2,1,0:T(4,128)S(1)}, f32[32,4,512]{2,1,0:T(4,128)}, u32[]{:S(2)}) copy-start(f32[32,4,512]{2,1,0:T(4,128)} %second_rot.1) | copy-start | bytes 786436
  23.0 6.7 %collective-permute-start.4 = (bf16[128,512]{1,0:T(8,128)(2,1)}, bf16[128,512]{1,0:T(8,128)(2,1)S(1)}, u32[]{:S(2)}, u32[]{:S(2)}) collective-permute-start(bf16[128,512]{1,0:T(8,128)(2,1)} %get-tuple-element.20), channel_id=1, source_target_pairs={{0,8},{4,12},{8,0},{12,4},{16,24},{20,28},{24,16},{28,20},{1,9},{5... | collective-permute-start | bytes 393224 | tf_op jit(solution)/shard_map/ppermute | solution.py:147
  24.5 8.4 %collective-permute-start.5 = (bf16[128,512]{1,0:T(8,128)(2,1)}, bf16[128,512]{1,0:T(8,128)(2,1)S(1)}, u32[]{:S(2)}, u32[]{:S(2)}) collective-permute-start(bf16[128,512]{1,0:T(8,128)(2,1)} %get-tuple-element.21), channel_id=1, source_target_pairs={{0,16},{4,20},{8,24},{12,28},{16,0},{20,4},{24,8},{28,12},{1,17},{... | collective-permute-start | bytes 393224 | tf_op jit(solution)/shard_map/ppermute | solution.py:147
  26.1 6.9 %collective-permute-start.6 = (bf16[128,512]{1,0:T(8,128)(2,1)}, bf16[128,512]{1,0:T(8,128)(2,1)S(1)}, u32[]{:S(2)}, u32[]{:S(2)}) collective-permute-start(bf16[128,512]{1,0:T(8,128)(2,1)} %get-tuple-element.22), channel_id=1, source_target_pairs={{0,24},{4,28},{8,16},{12,20},{16,8},{20,12},{24,0},{28,4},{1,25},{... | collective-permute-start | bytes 393224 | tf_op jit(solution)/shard_map/ppermute | solution.py:147
  26.5 13.8 %collective-permute-start.2 = (bf16[144,512]{1,0:T(8,128)(2,1)}, bf16[144,512]{1,0:T(8,128)(2,1)S(1)}, u32[]{:S(2)}, u32[]{:S(2)}) collective-permute-start(bf16[144,512]{1,0:T(8,128)(2,1)} %get-tuple-element.28), channel_id=1, source_target_pairs={{0,3},{1,0},{2,1},{3,2},{4,7},{5,4},{6,5},{7,6},{8,11},{9,8},{10,9... | collective-permute-start | bytes 442376 | tf_op jit(solution)/shard_map/ppermute | solution.py:150
  29.7 15.8 %collective-permute-start.1 = (bf16[144,512]{1,0:T(8,128)(2,1)}, bf16[144,512]{1,0:T(8,128)(2,1)S(1)}, u32[]{:S(2)}, u32[]{:S(2)}) collective-permute-start(bf16[144,512]{1,0:T(8,128)(2,1)} %get-tuple-element.29), channel_id=1, source_target_pairs={{0,2},{1,3},{2,0},{3,1},{4,6},{5,7},{6,4},{7,5},{8,10},{9,11},{10,... | collective-permute-start | bytes 442376 | tf_op jit(solution)/shard_map/ppermute | solution.py:150
  36.9 10.3 %copy-start.11 = (bf16[32,4,512]{2,1,0:T(4,128)(2,1)}, bf16[32,4,512]{2,1,0:T(4,128)(2,1)S(1)}, u32[]{:S(2)}) copy-start(bf16[32,4,512]{2,1,0:T(4,128)(2,1)S(1)} %get-tuple-element.23.refs_0_) | copy-start | bytes 393220
  36.9 7.0 %collective-permute-start.9 = (bf16[32,4,512]{2,1,0:T(4,128)(2,1)S(1)}, bf16[32,4,512]{2,1,0:T(4,128)(2,1)S(1)}, u32[]{:S(2)}, u32[]{:S(2)}) collective-permute-start(bf16[32,4,512]{2,1,0:T(4,128)(2,1)S(1)} %get-tuple-element.23.refs_0_), channel_id=1, source_target_pairs={{0,24},{4,28},{8,16},{12,20},{16,8},{20,12},{24,0},{28,4},{1,25},{... | collective-permute-start | bytes 393224 | tf_op jit(solution)/shard_map/ppermute | solution.py:147
  38.6 6.3 %collective-permute-start.8 = (bf16[32,4,512]{2,1,0:T(4,128)(2,1)S(1)}, bf16[32,4,512]{2,1,0:T(4,128)(2,1)S(1)}, u32[]{:S(2)}, u32[]{:S(2)}) collective-permute-start(bf16[32,4,512]{2,1,0:T(4,128)(2,1)S(1)} %get-tuple-element.23.refs_0_), channel_id=1, source_target_pairs={{0,16},{4,20},{8,24},{12,28},{16,0},{20,4},{24,8},{28,12},{1,17},{... | collective-permute-start | bytes 393224 | tf_op jit(solution)/shard_map/ppermute | solution.py:147
  39.5 5.7 %collective-permute-start.7 = (bf16[32,4,512]{2,1,0:T(4,128)(2,1)S(1)}, bf16[32,4,512]{2,1,0:T(4,128)(2,1)S(1)}, u32[]{:S(2)}, u32[]{:S(2)}) collective-permute-start(bf16[32,4,512]{2,1,0:T(4,128)(2,1)S(1)} %get-tuple-element.23.refs_0_), channel_id=1, source_target_pairs={{0,8},{4,12},{8,0},{12,4},{16,24},{20,28},{24,16},{28,20},{1,9},{5... | collective-permute-start | bytes 393224 | tf_op jit(solution)/shard_map/ppermute | solution.py:147
  40.4 6.8 %collective-permute-start.10 = (bf16[32,4,512]{2,1,0:T(4,128)(2,1)S(1)}, bf16[32,4,512]{2,1,0:T(4,128)(2,1)S(1)}, u32[]{:S(2)}, u32[]{:S(2)}) collective-permute-start(bf16[32,4,512]{2,1,0:T(4,128)(2,1)S(1)} %get-tuple-element.23.refs_0_), channel_id=1, source_target_pairs={{0,4},{4,0},{8,12},{12,8},{16,20},{20,16},{24,28},{28,24},{1,5},{5... | collective-permute-start | bytes 393224 | tf_op jit(solution)/shard_map/ppermute | solution.py:140
  43.9 3.2 %copy-start.14 = (bf16[32,4,512]{2,1,0:T(4,128)(2,1)}, bf16[32,4,512]{2,1,0:T(4,128)(2,1)S(1)}, u32[]{:S(2)}) copy-start(bf16[32,4,512]{2,1,0:T(4,128)(2,1)S(1)} %collective-permute-done.9.refs_3_) | copy-start | bytes 393220
  43.9 3.3 %collective-permute-start.13 = (bf16[32,4,512]{2,1,0:T(4,128)(2,1)S(1)}, bf16[32,4,512]{2,1,0:T(4,128)(2,1)S(1)}, u32[]{:S(2)}, u32[]{:S(2)}) collective-permute-start(bf16[32,4,512]{2,1,0:T(4,128)(2,1)S(1)} %collective-permute-done.9.refs_3_), channel_id=1, source_target_pairs={{0,4},{4,0},{8,12},{12,8},{16,20},{20,16},{24,28},{28,24},{1,5},{5... | collective-permute-start | bytes 393224 | tf_op jit(solution)/shard_map/ppermute | solution.py:140
  44.9 2.2 %copy-start.15 = (bf16[32,4,512]{2,1,0:T(4,128)(2,1)}, bf16[32,4,512]{2,1,0:T(4,128)(2,1)S(1)}, u32[]{:S(2)}) copy-start(bf16[32,4,512]{2,1,0:T(4,128)(2,1)S(1)} %collective-permute-done.8.refs_2_) | copy-start | bytes 393220
  44.9 2.2 %collective-permute-start.12 = (bf16[32,4,512]{2,1,0:T(4,128)(2,1)S(1)}, bf16[32,4,512]{2,1,0:T(4,128)(2,1)S(1)}, u32[]{:S(2)}, u32[]{:S(2)}) collective-permute-start(bf16[32,4,512]{2,1,0:T(4,128)(2,1)S(1)} %collective-permute-done.8.refs_2_), channel_id=1, source_target_pairs={{0,4},{4,0},{8,12},{12,8},{16,20},{20,16},{24,28},{28,24},{1,5},{5... | collective-permute-start | bytes 393224 | tf_op jit(solution)/shard_map/ppermute | solution.py:140
  45.2 1.9 %copy-start.16 = (bf16[32,4,512]{2,1,0:T(4,128)(2,1)}, bf16[32,4,512]{2,1,0:T(4,128)(2,1)S(1)}, u32[]{:S(2)}) copy-start(bf16[32,4,512]{2,1,0:T(4,128)(2,1)S(1)} %collective-permute-done.7.refs_1_) | copy-start | bytes 393220
  45.2 2.0 %collective-permute-start.11 = (bf16[32,4,512]{2,1,0:T(4,128)(2,1)S(1)}, bf16[32,4,512]{2,1,0:T(4,128)(2,1)S(1)}, u32[]{:S(2)}, u32[]{:S(2)}) collective-permute-start(bf16[32,4,512]{2,1,0:T(4,128)(2,1)S(1)} %collective-permute-done.7.refs_1_), channel_id=1, source_target_pairs={{0,4},{4,0},{8,12},{12,8},{16,20},{20,16},{24,28},{28,24},{1,5},{5... | collective-permute-start | bytes 393224 | tf_op jit(solution)/shard_map/ppermute | solution.py:140
  (11 other events, 9.3 us)

commit v2 on v1

v2 whole, which is shorter than its diff:
```python
import functools

import jax
import jax.numpy as jnp
from jax import lax
from jax.experimental import pallas as pl
from jax.experimental.pallas import tpu as pltpu
from jax.sharding import PartitionSpec as P

beta_first = 0.9
beta_second = 0.95
epsilon = 1e-08
learn_rate = 0.002
decay_rate = 0.1
blend_share = 0.5
log2_e = 1.4426950408889634
f32 = jnp.float32
bf16 = jnp.bfloat16
in_vmem = pl.BlockSpec(memory_space=pltpu.VMEM)
in_hbm = pl.BlockSpec(memory_space=pltpu.HBM)


def mm(a, b):
    return lax.dot_general(a, b, (((1,), (0,)), ((), ())), preferred_element_type=f32)


def mm_nt(a, b):
    return lax.dot_general(a, b, (((1,), (1,)), ((), ())), preferred_element_type=f32)


def mm_tn(a, b):
    return lax.dot_general(a, b, (((0,), (0,)), ((), ())), preferred_element_type=f32)


def limit_mib(mib):
    return pltpu.CompilerParams(vmem_limit_bytes=mib * 1024 * 1024)


def other_chip(chip, k, chips):
    return lax.rem(chip + k, chips) if chips & (chips - 1) else chip ^ k


def sender_chip(chip, k, chips):
    return lax.rem(chip - k + chips, chips) if chips & (chips - 1) else chip ^ k


def place_of():
    me = lax.axis_index("dp")
    return lax.div(me, 2), lax.rem(me, 2)


def attend_kernel(
    offsets,
    latent,
    q_nope,
    q_rope,
    k_rope_t,
    grad_out,
    weight,
    basis,
    first_moment,
    second_rot,
    second_plain,
    send,
    keep,
    grad_kv,
    wall,
    own_weight,
    basis_v,
    first_v,
    rot_v,
    plain_v,
    lat,
    q_main_v,
    q_side_v,
    k_side_v,
    g_out_v,
    weight_v,
    key_value,
    slab,
    sems,
):
    seq_len, latent_dim = latent.shape
    width, heads, _ = weight.shape
    head_dim = width // 2
    rope_dim = k_rope_t.shape[0]
    chips, _, rows, _ = keep.shape
    scale = float(head_dim + rope_dim) ** (-0.5)
    pairs = [
        (weight, weight_v),
        (latent, lat),
        (k_rope_t, k_side_v),
        (q_nope, q_main_v),
        (q_rope, q_side_v),
        (grad_out, g_out_v),
        (basis, basis_v),
        (first_moment, first_v),
        (second_rot, rot_v),
        (second_plain, plain_v),
    ]
    copies = [pltpu.make_async_copy(a, b, sems.at[i]) for i, (a, b) in enumerate(pairs)]
    for copy in copies:
        copy.start()
    limit = jnp.maximum(lax.broadcasted_iota(jnp.int32, (1, seq_len), 1), offsets[0] - 1)
    visible = lax.broadcasted_iota(jnp.int32, (seq_len, seq_len), 0) <= limit
    copies[0].wait()
    wall[...] = jnp.swapaxes(weight_v[...], 0, 1).reshape(heads * width, latent_dim)
    copies[1].wait()
    key_value[...] = mm_nt(lat[...], wall[...]).astype(bf16)
    for copy in copies[2:6]:
        copy.wait()
    k_side = k_side_v[...].T
    for h in range(heads):
        q_main = q_main_v[:, h * head_dim : (h + 1) * head_dim]
        g_out = g_out_v[:, h * head_dim : (h + 1) * head_dim]
        q_all = jnp.concatenate([q_main, q_side_v[:, h * rope_dim : (h + 1) * rope_dim]], axis=1)
        keys = key_value[:, h * width : h * width + head_dim]
        values = key_value[:, h * width + head_dim : (h + 1) * width]
        k_all = jnp.concatenate([keys, k_side], axis=1)
        scores = jnp.where(visible, mm_nt(k_all, q_all), -1e30)
        top = jnp.max(scores, axis=0, keepdims=True)
        terms = jnp.exp2((scores - top) * (scale * log2_e))
        inv = 1.0 / jnp.sum(terms, axis=0, keepdims=True)
        probs = terms * inv
        grad_probs = mm_nt(values, g_out)
        delta = jnp.sum(probs * grad_probs, axis=0, keepdims=True)
        grad_scores = (probs * (grad_probs - delta) * scale).astype(bf16)
        grad_kv[:, h * width : h * width + head_dim] = mm(grad_scores, q_main).astype(bf16)
        grad_kv[:, h * width + head_dim : (h + 1) * width] = mm(probs.astype(bf16), g_out).astype(bf16)
    slab[...] = mm_tn(grad_kv[...], lat[...]).reshape(heads, 2 * chips, rows, latent_dim)
    my_chip, my_core = place_of()
    for k in range(chips):
        chip = other_chip(my_chip, k, chips)
        for h in range(heads):
            send[k, h] = slab[h, 2 * chip + 1 - my_core].astype(bf16)
            keep[k, h] = slab[h, 2 * chip + my_core].astype(bf16)
    own_weight[...] = weight_v[pl.ds((2 * my_chip + my_core) * rows, rows)]
    for copy in copies[6:]:
        copy.wait()


def latent_kernel(grad_kv, wall, basis, *refs):
    turn, total, outs = refs[0], refs[-1], refs[1:-1]
    parts = len(outs)
    total[...] = mm(grad_kv[...], wall[...]).astype(bf16).reshape(total.shape)
    for s, out in enumerate(outs):
        out[...] = total[lax.rem(lax.axis_index("tensor") + s, parts)]
    turn[...] = basis[...].astype(bf16)


def pair_kernel(keep, came, *outs):
    for k, out in enumerate(outs):
        out[...] = (keep[k].astype(f32) + came[k].astype(f32)).astype(out.dtype)


def soap_kernel(old, turn, first_moment, second_rot, second_plain, *refs):
    parts, (slab_out, new_first, new_second, new_plain) = refs[:-4], refs[-4:]
    rows, heads, latent_dim = first_moment.shape
    flat = (heads * rows, latent_dim)

    def by_head(x):
        return jnp.swapaxes(x, 0, 1).reshape(flat)

    def by_row(x):
        return jnp.swapaxes(x.reshape(heads, rows, latent_dim), 0, 1)

    grad = functools.reduce(jnp.add, [p[...].astype(f32) for p in parts]).reshape(flat)
    rotated = mm(grad.astype(bf16), turn[...])
    moment = beta_first * by_head(first_moment[...]) + (1.0 - beta_first) * rotated
    rot_sq = beta_second * by_head(second_rot[...]) + (1.0 - beta_second) * rotated * rotated
    plain_sq = beta_second * by_head(second_plain[...]) + (1.0 - beta_second) * grad * grad
    stacked = jnp.concatenate([moment / (jnp.sqrt(rot_sq) + epsilon), moment], axis=0).astype(bf16)
    turned = mm_nt(stacked, turn[...])
    direction = blend_share * turned[: flat[0]] + blend_share * turned[flat[0] :] / (jnp.sqrt(plain_sq) + epsilon)
    before = old[...].astype(f32)
    slab_out[...] = (before - learn_rate * (by_row(direction) + decay_rate * before)).astype(bf16)
    new_first[...] = by_row(moment)
    new_second[...] = by_row(rot_sq)
    new_plain[...] = by_row(plain_sq)


def place_kernel(*refs):
    chips = (len(refs) - 2) // 2
    out, sems = refs[-2:]
    rows = refs[0].shape[0]
    my_chip, my_core = place_of()
    copies = []
    for k in range(chips):
        chip = sender_chip(my_chip, k, chips)
        for side in range(2):
            core = my_core if side == 0 else 1 - my_core
            spot = out.at[pl.ds((2 * chip + core) * rows, rows)]
            copies.append(pltpu.make_async_copy(refs[side * chips + k], spot, sems.at[2 * k + side]))
    for copy in copies:
        copy.start()
    for copy in copies:
        copy.wait()


def part_sum_kernel(*refs):
    refs[-1][...] = functools.reduce(jnp.add, [x[...].astype(f32) for x in refs[:-1]]).astype(bf16)


def local(latent, q_nope, q_rope, k_rope, grad_out, offsets, weight, basis, first_moment, second_rot, second_plain):
    seq_len, latent_dim = latent.shape
    width, heads, _ = weight.shape
    dp, parts = lax.axis_size("dp"), lax.axis_size("tensor")
    chips = dp // 2
    rows = width // dp
    part_rows = seq_len // parts
    rope_dim = k_rope.shape[1]

    def core_swap(x):
        return lax.ppermute(x, "dp", [(i, i ^ 1) for i in range(dp)])

    def chip_move(x, k):
        if chips & (chips - 1):
            pairs = [(i, (i + 2 * k) % dp) for i in range(dp)]
        else:
            pairs = [(i, i ^ (2 * k)) for i in range(dp)]
        return lax.ppermute(x, "dp", pairs)

    def part_move(x, s):
        return lax.ppermute(x, "tensor", [(i, (i + s) % parts) for i in range(parts)])

    piece = (heads, rows, latent_dim)
    state = (rows, heads, latent_dim)
    send, keep, grad_kv, wall, own_weight, basis_v, first_v, rot_v, plain_v = pl.pallas_call(
        attend_kernel,
        out_shape=(
            pltpu.VMEM((chips,) + piece, bf16),
            pltpu.VMEM((chips,) + piece, bf16),
            pltpu.VMEM((seq_len, heads * width), bf16),
            pltpu.VMEM((heads * width, latent_dim), bf16),
            pltpu.VMEM(state, bf16),
            pltpu.VMEM(basis.shape, f32),
            pltpu.VMEM(state, f32),
            pltpu.VMEM(state, f32),
            pltpu.VMEM(state, f32),
        ),
        in_specs=[pl.BlockSpec(memory_space=pltpu.SMEM)] + [in_hbm] * 10,
        out_specs=(in_vmem,) * 9,
        scratch_shapes=[
            pltpu.VMEM(latent.shape, bf16),
            pltpu.VMEM(q_nope.shape, bf16),
            pltpu.VMEM(q_rope.shape, bf16),
            pltpu.VMEM((rope_dim, seq_len), bf16),
            pltpu.VMEM(grad_out.shape, bf16),
            pltpu.VMEM(weight.shape, bf16),
            pltpu.VMEM((seq_len, heads * width), bf16),
            pltpu.VMEM((heads, dp, rows, latent_dim), f32),
            pltpu.SemaphoreType.DMA((10,)),
        ],
        compiler_params=limit_mib(32),
        name="attend",
    )(offsets, *[
        pltpu.with_memory_space_constraint(x, pltpu.HBM)
        for x in (
            latent, q_nope, q_rope, k_rope.T, grad_out, weight, basis, first_moment, second_rot, second_plain
        )
    ])

    came = core_swap(send)
    turn, *glat = pl.pallas_call(
        latent_kernel,
        out_shape=[pltpu.VMEM(basis.shape, bf16)] + [pltpu.VMEM((part_rows, latent_dim), bf16)] * parts,
        in_specs=[in_vmem] * 3,
        out_specs=[in_vmem] * (1 + parts),
        scratch_shapes=[pltpu.VMEM((parts, part_rows, latent_dim), bf16)],
        compiler_params=limit_mib(8),
        name="latent_share",
    )(grad_kv, wall, basis_v)
    sums = pl.pallas_call(
        pair_kernel,
        out_shape=[pltpu.VMEM(piece, f32 if k == 0 else bf16) for k in range(chips)],
        in_specs=[in_vmem] * 2,
        out_specs=[in_vmem] * chips,
        compiler_params=limit_mib(4),
        name="pair_sum",
    )(keep, came)
    sums, glat = lax.optimization_barrier((sums, glat))
    got = [sums[0]] + [chip_move(sums[k], k) for k in range(1, chips)]
    glat = [glat[0]] + [part_move(glat[s], s) for s in range(1, parts)]

    new_slab, new_first, new_second, new_plain = pl.pallas_call(
        soap_kernel,
        out_shape=(pltpu.VMEM(state, bf16),) + (pltpu.VMEM(state, f32),) * 3,
        in_specs=[in_vmem] * (5 + chips),
        out_specs=(in_vmem,) * 4,
        compiler_params=limit_mib(8),
        name="soap",
    )(own_weight, turn, first_v, rot_v, plain_v, *got)

    mine = [new_slab] + [chip_move(new_slab, k) for k in range(1, chips)]
    others = [core_swap(x) for x in mine]
    grad_latent = pl.pallas_call(
        part_sum_kernel,
        out_shape=jax.ShapeDtypeStruct((part_rows, latent_dim), bf16),
        in_specs=[in_vmem] * parts,
        out_specs=in_vmem,
        compiler_params=limit_mib(4),
        name="part_sum",
    )(*glat)
    new_weight = pl.pallas_call(
        place_kernel,
        out_shape=pltpu.HBM((width, heads, latent_dim), bf16),
        in_specs=[in_vmem] * (2 * chips),
        out_specs=in_hbm,
        scratch_shapes=[pltpu.SemaphoreType.DMA((2 * chips,))],
        compiler_params=limit_mib(4),
        name="place",
    )(*mine, *others)
    return (grad_latent, new_weight, new_first, new_second, new_plain)


def solution(mesh):
    state = P("dp", "tensor", None)
    return jax.shard_map(
        local,
        mesh=mesh,
        in_specs=(
            P("dp", None),
            P("dp", "tensor"),
            P("dp", "tensor"),
            P("dp", None),
            P("dp", "tensor"),
            P("dp"),
            P(None, "tensor", None),
            P(),
            state,
            state,
            state,
        ),
        out_specs=(P(("dp", "tensor"), None), P(None, "tensor", None), state, state, state),
        check_vma=False,
    )
```

time: 51.3 us -> 37.1 us (0.72)
  local copies, waits for them, and re-layouts: 11.2 us -> 2.11 us
  waiting for transfers between devices: 5.94 us -> 3.28 us
  Pallas kernels: 15 us -> 12.7 us
  starting transfers between devices: 15.5 us -> 17.5 us
  other arithmetic: 1.72 us -> 0 us
    unnamed x44 -> x3, local copies, waits for them, and re-layouts: 10.5 us -> 2.11 us
    ppermute x6, waiting for transfers between devices: 5.92 us -> 2.55 us  [chip_move(): return lax.ppermute(x, 'dp', pairs)]
    pallas_call x4 -> x6, Pallas kernels: 15 us -> 12.7 us  [the longest x1 9.04 us: local(): pl.pallas_call(attend_kernel, out_shape=(pltpu.VMEM((chips,) + piece, bf1...]
    convert_element_type x1 -> x0, other arithmetic: 1.65 us -> none  [local(): functools.reduce(jnp.add, [x.astype(f32) for x in glat_parts]).astype(bf16)]
    ppermute x6, starting transfers between devices: 6.98 us -> 8.02 us  [chip_move(): return lax.ppermute(x, 'dp', pairs)]
    squeeze x1 -> x0, local copies, waits for them, and re-layouts: 0.77 us -> none  [local(): glat_parts = [glat[0]] + [part_move(glat[s], s) for s in range(1, parts)]]
    ppermute x5, waiting for transfers between devices: 0.01 us -> 0.73 us  [core_swap(): return lax.ppermute(x, 'dp', [(i, i ^ 1) for i in range(dp)])]
    ppermute x5, starting transfers between devices: 0.71 us -> 1.26 us  [core_swap(): return lax.ppermute(x, 'dp', [(i, i ^ 1) for i in range(dp)])]
  transfers between devices with their start and end apart: 14 -> 14, of which waited for: 4 -> 4; matrix products, arithmetic and copies ran while one was open for 5% -> 6% of each run, Pallas kernels for 8% -> 7%
where the time goes in v2:
time: 37.1 us; the launch traced here: 36.9 us
  starting transfers between devices  17.5 us (47%)
  Pallas kernels  12.7 us (34%)
  waiting for transfers between devices  3.28 us (9%)
  local copies, waits for them, and re-layouts  2.11 us (6%)
  between operations  1.34 us (4%)
    pallas_call x1, Pallas kernels, local(): pl.pallas_call(attend_kernel, out_shape=(pltpu.VMEM((chips,) + piece, bf1...  9.04 us
    ppermute x3, starting transfers between devices, part_move(): lax.ppermute(x, 'tensor', [(i, (i + s) % parts) for i in range(parts)])  8.22 us
    ppermute x6, starting transfers between devices, chip_move(): return lax.ppermute(x, 'dp', pairs)  8.02 us
    ppermute x6, waiting for transfers between devices, chip_move(): return lax.ppermute(x, 'dp', pairs)  2.55 us
    unnamed x3, local copies, waits for them, and re-layouts  2.11 us
    ppermute x5, starting transfers between devices, core_swap(): return lax.ppermute(x, 'dp', [(i, i ^ 1) for i in range(dp)])  1.26 us
    pallas_call x1, Pallas kernels, local(): pl.pallas_call(place_kernel, out_shape=pltpu.HBM((width, heads, latent_di...  1.04 us
    pallas_call x1, Pallas kernels, local(): pl.pallas_call(soap_kernel, out_shape=(pltpu.VMEM(state, bf16),) + (pltpu...  0.96 us
  transfers between devices with their start and end apart: 14, of which 4 were waited for; matrix products, arithmetic and copies ran while one was open for 6% of the time, Pallas kernels for 7%

profile of v2, /device:TPU:0, one launch (start us, length us, event | category | flops | bytes accessed | tf_op | source)
XLA Modules:
  0.0 36.9 jit_solution(15080254317223084640)
XLA Ops:
  1.3 9.0 %attend.1 = (bf16[4,4,32,512]{3,2,1,0:T(8,128)(2,1)S(1)}, bf16[4,4,32,512]{3,2,1,0:T(8,128)(2,1)S(1)}, bf16[576,1024]{1,0:T(8,128)(2,1)S(1)}, bf16[1024,512]{1,0...) custom-call(s32[1]{0:T(128)S(6)} %copy.19.offsets, ...), custom_call_target="tpu_custom_call" | custom-call | tf_op jit(solution)/shard_map/attend/pallas_call | solution.py:228
  10.3 0.5 %collective-permute-start = (bf16[4,4,32,512]{3,2,1,0:T(8,128)(2,1)S(1)}, bf16[4,4,32,512]{3,2,1,0:T(8,128)(2,1)S(1)}, u32[]{:S(2)}, u32[]{:S(2)}) collective-permute-start(bf16[4,4,32,512]{3,2,1,0:T(8,128)(2,1)S(1)} %get-tuple-element.36), channel_id=1, source_target_pairs={{0,4},{4,0},{8,12},{12,8},{16,20},{20,16},{24,28},{28,24},{1,5},{5... | collective-permute-start | bytes 1572872 | tf_op jit(solution)/shard_map/ppermute | solution.py:214
  10.8 0.8 %latent_share.1 = (bf16[512,512]{1,0:T(8,128)(2,1)S(1)}, bf16[144,512]{1,0:T(8,128)(2,1)S(1)}, bf16[144,512]{1,0:T(8,128)(2,1)S(1)}, bf16[144,512]{1,0:T(8,128)(2,1)S(1)}, bf16[144,512]{1,0:T(8,128)(2,1)S(1)}) custom-call(bf16[576,1024]{1,0:T(8,128)(2,1)S(1)} %get-tuple-element.41.grad_kv, bf16[1024,512]{1,0:T(8,128)(2,1)S(1)} %get-tuple-element.42.wall, ...), custom_call_target="tpu_custom_call" | custom-call | tf_op jit(solution)/shard_map/latent_share/pallas_call | solution.py:264
  11.7 0.7 %collective-permute-done.came = bf16[4,4,32,512]{3,2,1,0:T(8,128)(2,1)S(1)} collective-permute-done((bf16[4,4,32,512]{3,2,1,0:T(8,128)(2,1)S(1)}, bf16[4,4,32,512]{3,2,1,0:T(8,128)(2,1)S(1)}, u32[]{:S(2)}, u32[]{:S(2)}) %collective-permute-start) | collective-permute-done | bytes 524320 | tf_op jit(solution)/shard_map/ppermute | solution.py:214
  12.4 0.1 pair_sum.1
  12.5 2.9 %collective-permute-start.4 = (bf16[4,32,512]{2,1,0:T(8,128)(2,1)S(1)}, bf16[4,32,512]{2,1,0:T(8,128)(2,1)S(1)}, u32[]{:S(2)}, u32[]{:S(2)}) collective-permute-start(bf16[4,32,512]{2,1,0:T(8,128)(2,1)S(1)} %get-tuple-element.58), channel_id=1, source_target_pairs={{0,8},{4,12},{8,0},{12,4},{16,24},{20,28},{24,16},{28,20},{1,9},{5... | collective-permute-start | bytes 393224 | tf_op jit(solution)/shard_map/ppermute | solution.py:221
  15.4 1.5 %collective-permute-start.5 = (bf16[4,32,512]{2,1,0:T(8,128)(2,1)S(1)}, bf16[4,32,512]{2,1,0:T(8,128)(2,1)S(1)}, u32[]{:S(2)}, u32[]{:S(2)}) collective-permute-start(bf16[4,32,512]{2,1,0:T(8,128)(2,1)S(1)} %get-tuple-element.59), channel_id=1, source_target_pairs={{0,16},{4,20},{8,24},{12,28},{16,0},{20,4},{24,8},{28,12},{1,17},{... | collective-permute-start | bytes 393224 | tf_op jit(solution)/shard_map/ppermute | solution.py:221
  17.0 2.0 %collective-permute-start.1 = (bf16[144,512]{1,0:T(8,128)(2,1)S(1)}, bf16[144,512]{1,0:T(8,128)(2,1)S(1)}, u32[]{:S(2)}, u32[]{:S(2)}) collective-permute-start(bf16[144,512]{1,0:T(8,128)(2,1)S(1)} %get-tuple-element.49), channel_id=1, source_target_pairs={{0,1},{1,2},{2,3},{3,0},{4,5},{5,6},{6,7},{7,4},{8,9},{9,10},{10,1... | collective-permute-start | bytes 442376 | tf_op jit(solution)/shard_map/ppermute | solution.py:224
  19.0 2.6 %collective-permute-start.2 = (bf16[144,512]{1,0:T(8,128)(2,1)S(1)}, bf16[144,512]{1,0:T(8,128)(2,1)S(1)}, u32[]{:S(2)}, u32[]{:S(2)}) collective-permute-start(bf16[144,512]{1,0:T(8,128)(2,1)S(1)} %get-tuple-element.50), channel_id=1, source_target_pairs={{0,2},{1,3},{2,0},{3,1},{4,6},{5,7},{6,4},{7,5},{8,10},{9,11},{10,... | collective-permute-start | bytes 442376 | tf_op jit(solution)/shard_map/ppermute | solution.py:224
  21.6 1.9 %collective-permute-done.5.refs_2_ = bf16[4,32,512]{2,1,0:T(8,128)(2,1)S(1)} collective-permute-done((bf16[4,32,512]{2,1,0:T(8,128)(2,1)S(1)}, bf16[4,32,512]{2,1,0:T(8,128)(2,1)S(1)}, u32[]{:S(2)}, u32[]{:S(2)}) %collective-permute-start.5) | collective-permute-done | bytes 131104 | tf_op jit(solution)/shard_map/ppermute | solution.py:221
  23.5 1.0 %soap.1 = (bf16[32,4,512]{2,1,0:T(4,128)(2,1)S(1)}, f32[32,4,512]{2,1,0:T(4,128)S(1)}, f32[32,4,512]{2,1,0:T(4,128)S(1)}, f32[32,4,512]{2,1,0:T(4,128)S(1)}) custom-call(bf16[32,4,512]{2,1,0:T(4,128)(2,1)S(1)} %get-tuple-element.52.old, bf16[512,512]{1,0:T(8,128)(2,1)S(1)} %get-tuple-element.53.turn, f32[32,4,512]{2,1,0:T(4,128)S(1)} %get-tuple-element.54.first_moment, ...), custom_call_target="tpu_custom_call" | custom-call | tf_op jit(solution)/shard_map/soap/pallas_call | solution.py:285
  24.5 1.6 %collective-permute-start.9 = (bf16[32,4,512]{2,1,0:T(4,128)(2,1)S(1)}, bf16[32,4,512]{2,1,0:T(4,128)(2,1)S(1)}, u32[]{:S(2)}, u32[]{:S(2)}) collective-permute-start(bf16[32,4,512]{2,1,0:T(4,128)(2,1)S(1)} %get-tuple-element.61.refs_0_), channel_id=1, source_target_pairs={{0,24},{4,28},{8,16},{12,20},{16,8},{20,12},{24,0},{28,4},{1,25},{... | collective-permute-start | bytes 393224 | tf_op jit(solution)/shard_map/ppermute | solution.py:221
  26.0 1.2 %collective-permute-start.8 = (bf16[32,4,512]{2,1,0:T(4,128)(2,1)S(1)}, bf16[32,4,512]{2,1,0:T(4,128)(2,1)S(1)}, u32[]{:S(2)}, u32[]{:S(2)}) collective-permute-start(bf16[32,4,512]{2,1,0:T(4,128)(2,1)S(1)} %get-tuple-element.61.refs_0_), channel_id=1, source_target_pairs={{0,16},{4,20},{8,24},{12,28},{16,0},{20,4},{24,8},{28,12},{1,17},{... | collective-permute-start | bytes 393224 | tf_op jit(solution)/shard_map/ppermute | solution.py:221
  27.2 0.8 %collective-permute-start.7 = (bf16[32,4,512]{2,1,0:T(4,128)(2,1)S(1)}, bf16[32,4,512]{2,1,0:T(4,128)(2,1)S(1)}, u32[]{:S(2)}, u32[]{:S(2)}) collective-permute-start(bf16[32,4,512]{2,1,0:T(4,128)(2,1)S(1)} %get-tuple-element.61.refs_0_), channel_id=1, source_target_pairs={{0,8},{4,12},{8,0},{12,4},{16,24},{20,28},{24,16},{28,20},{1,9},{5... | collective-permute-start | bytes 393224 | tf_op jit(solution)/shard_map/ppermute | solution.py:221
  28.0 3.6 %collective-permute-start.3 = (bf16[144,512]{1,0:T(8,128)(2,1)S(1)}, bf16[144,512]{1,0:T(8,128)(2,1)S(1)}, u32[]{:S(2)}, u32[]{:S(2)}) collective-permute-start(bf16[144,512]{1,0:T(8,128)(2,1)S(1)} %get-tuple-element.51), channel_id=1, source_target_pairs={{0,3},{1,0},{2,1},{3,2},{4,7},{5,4},{6,5},{7,6},{8,11},{9,8},{10,9... | collective-permute-start | bytes 442376 | tf_op jit(solution)/shard_map/ppermute | solution.py:224
  31.6 0.5 %collective-permute-start.13 = (bf16[32,4,512]{2,1,0:T(4,128)(2,1)S(1)}, bf16[32,4,512]{2,1,0:T(4,128)(2,1)S(1)}, u32[]{:S(2)}, u32[]{:S(2)}) collective-permute-start(bf16[32,4,512]{2,1,0:T(4,128)(2,1)S(1)} %collective-permute-done.9.refs_3_), channel_id=1, source_target_pairs={{0,4},{4,0},{8,12},{12,8},{16,20},{20,16},{24,28},{28,24},{1,5},{5... | collective-permute-start | bytes 393224 | tf_op jit(solution)/shard_map/ppermute | solution.py:214
  32.1 0.4 collective-permute-done.8.refs_2_
  32.5 0.3 collective-permute-done.7.refs_1_
  32.8 0.2 collective-permute-start.11
  33.0 0.7 %copy.16 = f32[32,4,512]{2,1,0:T(4,128)} copy(f32[32,4,512]{2,1,0:T(4,128)S(1)} %get-tuple-element.67) | data formatting | bytes 524288
  33.7 0.7 %copy.17 = f32[32,4,512]{2,1,0:T(4,128)} copy(f32[32,4,512]{2,1,0:T(4,128)S(1)} %get-tuple-element.68) | data formatting | bytes 524288
  34.4 0.7 %copy.18 = f32[32,4,512]{2,1,0:T(4,128)} copy(f32[32,4,512]{2,1,0:T(4,128)S(1)} %get-tuple-element.69) | data formatting | bytes 524288
  35.1 0.7 %part_sum.1 = bf16[144,512]{1,0:T(8,128)(2,1)} custom-call(bf16[144,512]{1,0:T(8,128)(2,1)S(1)} %get-tuple-element.48.refs_0_, bf16[144,512]{1,0:T(8,128)(2,1)S(1)} %collective-permute-done.1.refs_1_, bf16[144,512]{1,0:T(8,128)(2,1)S(1)} %collective-permute-done.2.refs_2_, bf16[144,512]{1,0:T(8,128)(2,1)S(1)} %collective-permute-done.3.refs_3_), custom_call_target="tpu_custom_call" | custom-call | tf_op jit(solution)/shard_map/part_sum/pallas_call | solution.py:296
  35.9 1.0 %place.1 = bf16[256,4,512]{2,1,0:T(4,128)(2,1)} custom-call(bf16[32,4,512]{2,1,0:T(4,128)(2,1)S(1)} %get-tuple-element.61.refs_0_, bf16[32,4,512]{2,1,0:T(4,128)(2,1)S(1)} %collective-permute-done.7.refs_1_, bf16[32,4,512]{2,1,0:T(4,128)(2,1)S(1)} %collective-permute-done.8.refs_2_, bf16[32,4,512]{2,1,0:T(4,128)(2,1)S(1)} %collective-permute-done.9.refs_3_, ...), custom_call_target="tpu_custom_call" | custom-call | tf_op jit(solution)/shard_map/place/pallas_call | solution.py:304
  (13 shorter events, 0.1 us)
Async XLA Ops:
  10.3 2.1 %collective-permute-start = (bf16[4,4,32,512]{3,2,1,0:T(8,128)(2,1)S(1)}, bf16[4,4,32,512]{3,2,1,0:T(8,128)(2,1)S(1)}, u32[]{:S(2)}, u32[]{:S(2)}) collective-permute-start(bf16[4,4,32,512]{3,2,1,0:T(8,128)(2,1)S(1)} %get-tuple-element.36), channel_id=1, source_target_pairs={{0,4},{4,0},{8,12},{12,8},{16,20},{20,16},{24,28},{28,24},{1,5},{5... | collective-permute-start | bytes 1572872 | tf_op jit(solution)/shard_map/ppermute | solution.py:214
  12.5 9.1 %collective-permute-start.4 = (bf16[4,32,512]{2,1,0:T(8,128)(2,1)S(1)}, bf16[4,32,512]{2,1,0:T(8,128)(2,1)S(1)}, u32[]{:S(2)}, u32[]{:S(2)}) collective-permute-start(bf16[4,32,512]{2,1,0:T(8,128)(2,1)S(1)} %get-tuple-element.58), channel_id=1, source_target_pairs={{0,8},{4,12},{8,0},{12,4},{16,24},{20,28},{24,16},{28,20},{1,9},{5... | collective-permute-start | bytes 393224 | tf_op jit(solution)/shard_map/ppermute | solution.py:221
  15.4 8.1 %collective-permute-start.5 = (bf16[4,32,512]{2,1,0:T(8,128)(2,1)S(1)}, bf16[4,32,512]{2,1,0:T(8,128)(2,1)S(1)}, u32[]{:S(2)}, u32[]{:S(2)}) collective-permute-start(bf16[4,32,512]{2,1,0:T(8,128)(2,1)S(1)} %get-tuple-element.59), channel_id=1, source_target_pairs={{0,16},{4,20},{8,24},{12,28},{16,0},{20,4},{24,8},{28,12},{1,17},{... | collective-permute-start | bytes 393224 | tf_op jit(solution)/shard_map/ppermute | solution.py:221
  17.0 6.5 %collective-permute-start.6 = (bf16[4,32,512]{2,1,0:T(8,128)(2,1)S(1)}, bf16[4,32,512]{2,1,0:T(8,128)(2,1)S(1)}, u32[]{:S(2)}, u32[]{:S(2)}) collective-permute-start(bf16[4,32,512]{2,1,0:T(8,128)(2,1)S(1)} %get-tuple-element.60), channel_id=1, source_target_pairs={{0,24},{4,28},{8,16},{12,20},{16,8},{20,12},{24,0},{28,4},{1,25},{... | collective-permute-start | bytes 393224 | tf_op jit(solution)/shard_map/ppermute | solution.py:221
  17.0 11.1 %collective-permute-start.1 = (bf16[144,512]{1,0:T(8,128)(2,1)S(1)}, bf16[144,512]{1,0:T(8,128)(2,1)S(1)}, u32[]{:S(2)}, u32[]{:S(2)}) collective-permute-start(bf16[144,512]{1,0:T(8,128)(2,1)S(1)} %get-tuple-element.49), channel_id=1, source_target_pairs={{0,1},{1,2},{2,3},{3,0},{4,5},{5,6},{6,7},{7,4},{8,9},{9,10},{10,1... | collective-permute-start | bytes 442376 | tf_op jit(solution)/shard_map/ppermute | solution.py:224
  19.0 12.6 %collective-permute-start.2 = (bf16[144,512]{1,0:T(8,128)(2,1)S(1)}, bf16[144,512]{1,0:T(8,128)(2,1)S(1)}, u32[]{:S(2)}, u32[]{:S(2)}) collective-permute-start(bf16[144,512]{1,0:T(8,128)(2,1)S(1)} %get-tuple-element.50), channel_id=1, source_target_pairs={{0,2},{1,3},{2,0},{3,1},{4,6},{5,7},{6,4},{7,5},{8,10},{9,11},{10,... | collective-permute-start | bytes 442376 | tf_op jit(solution)/shard_map/ppermute | solution.py:224
  24.5 7.2 %collective-permute-start.9 = (bf16[32,4,512]{2,1,0:T(4,128)(2,1)S(1)}, bf16[32,4,512]{2,1,0:T(4,128)(2,1)S(1)}, u32[]{:S(2)}, u32[]{:S(2)}) collective-permute-start(bf16[32,4,512]{2,1,0:T(4,128)(2,1)S(1)} %get-tuple-element.61.refs_0_), channel_id=1, source_target_pairs={{0,24},{4,28},{8,16},{12,20},{16,8},{20,12},{24,0},{28,4},{1,25},{... | collective-permute-start | bytes 393224 | tf_op jit(solution)/shard_map/ppermute | solution.py:221
  26.0 6.5 %collective-permute-start.8 = (bf16[32,4,512]{2,1,0:T(4,128)(2,1)S(1)}, bf16[32,4,512]{2,1,0:T(4,128)(2,1)S(1)}, u32[]{:S(2)}, u32[]{:S(2)}) collective-permute-start(bf16[32,4,512]{2,1,0:T(4,128)(2,1)S(1)} %get-tuple-element.61.refs_0_), channel_id=1, source_target_pairs={{0,16},{4,20},{8,24},{12,28},{16,0},{20,4},{24,8},{28,12},{1,17},{... | collective-permute-start | bytes 393224 | tf_op jit(solution)/shard_map/ppermute | solution.py:221
  27.2 5.6 %collective-permute-start.7 = (bf16[32,4,512]{2,1,0:T(4,128)(2,1)S(1)}, bf16[32,4,512]{2,1,0:T(4,128)(2,1)S(1)}, u32[]{:S(2)}, u32[]{:S(2)}) collective-permute-start(bf16[32,4,512]{2,1,0:T(4,128)(2,1)S(1)} %get-tuple-element.61.refs_0_), channel_id=1, source_target_pairs={{0,8},{4,12},{8,0},{12,4},{16,24},{20,28},{24,16},{28,20},{1,9},{5... | collective-permute-start | bytes 393224 | tf_op jit(solution)/shard_map/ppermute | solution.py:221
  28.0 7.1 %collective-permute-start.3 = (bf16[144,512]{1,0:T(8,128)(2,1)S(1)}, bf16[144,512]{1,0:T(8,128)(2,1)S(1)}, u32[]{:S(2)}, u32[]{:S(2)}) collective-permute-start(bf16[144,512]{1,0:T(8,128)(2,1)S(1)} %get-tuple-element.51), channel_id=1, source_target_pairs={{0,3},{1,0},{2,1},{3,2},{4,7},{5,4},{6,5},{7,6},{8,11},{9,8},{10,9... | collective-permute-start | bytes 442376 | tf_op jit(solution)/shard_map/ppermute | solution.py:224
  31.6 4.2 %collective-permute-start.10 = (bf16[32,4,512]{2,1,0:T(4,128)(2,1)S(1)}, bf16[32,4,512]{2,1,0:T(4,128)(2,1)S(1)}, u32[]{:S(2)}, u32[]{:S(2)}) collective-permute-start(bf16[32,4,512]{2,1,0:T(4,128)(2,1)S(1)} %get-tuple-element.61.refs_0_), channel_id=1, source_target_pairs={{0,4},{4,0},{8,12},{12,8},{16,20},{20,16},{24,28},{28,24},{1,5},{5... | collective-permute-start | bytes 393224 | tf_op jit(solution)/shard_map/ppermute | solution.py:214
  31.6 4.2 %collective-permute-start.13 = (bf16[32,4,512]{2,1,0:T(4,128)(2,1)S(1)}, bf16[32,4,512]{2,1,0:T(4,128)(2,1)S(1)}, u32[]{:S(2)}, u32[]{:S(2)}) collective-permute-start(bf16[32,4,512]{2,1,0:T(4,128)(2,1)S(1)} %collective-permute-done.9.refs_3_), channel_id=1, source_target_pairs={{0,4},{4,0},{8,12},{12,8},{16,20},{20,16},{24,28},{28,24},{1,5},{5... | collective-permute-start | bytes 393224 | tf_op jit(solution)/shard_map/ppermute | solution.py:214
  32.5 3.4 %collective-permute-start.12 = (bf16[32,4,512]{2,1,0:T(4,128)(2,1)S(1)}, bf16[32,4,512]{2,1,0:T(4,128)(2,1)S(1)}, u32[]{:S(2)}, u32[]{:S(2)}) collective-permute-start(bf16[32,4,512]{2,1,0:T(4,128)(2,1)S(1)} %collective-permute-done.8.refs_2_), channel_id=1, source_target_pairs={{0,4},{4,0},{8,12},{12,8},{16,20},{20,16},{24,28},{28,24},{1,5},{5... | collective-permute-start | bytes 393224 | tf_op jit(solution)/shard_map/ppermute | solution.py:214
  32.8 3.1 %collective-permute-start.11 = (bf16[32,4,512]{2,1,0:T(4,128)(2,1)S(1)}, bf16[32,4,512]{2,1,0:T(4,128)(2,1)S(1)}, u32[]{:S(2)}, u32[]{:S(2)}) collective-permute-start(bf16[32,4,512]{2,1,0:T(4,128)(2,1)S(1)} %collective-permute-done.7.refs_1_), channel_id=1, source_target_pairs={{0,4},{4,0},{8,12},{12,8},{16,20},{20,16},{24,28},{28,24},{1,5},{5... | collective-permute-start | bytes 393224 | tf_op jit(solution)/shard_map/ppermute | solution.py:214

commit v3 on v2

--- a/solution.py
+++ b/solution.py
@@ -57,19 +57,11 @@
     k_rope_t,
     grad_out,
     weight,
-    basis,
-    first_moment,
-    second_rot,
-    second_plain,
     send,
     keep,
     grad_kv,
     wall,
     own_weight,
-    basis_v,
-    first_v,
-    rot_v,
-    plain_v,
     lat,
     q_main_v,
     q_side_v,
@@ -93,15 +85,11 @@
         (q_nope, q_main_v),
         (q_rope, q_side_v),
         (grad_out, g_out_v),
-        (basis, basis_v),
-        (first_moment, first_v),
-        (second_rot, rot_v),
-        (second_plain, plain_v),
     ]
     copies = [pltpu.make_async_copy(a, b, sems.at[i]) for i, (a, b) in enumerate(pairs)]
     for copy in copies:
         copy.start()
-    limit = jnp.maximum(lax.broadcasted_iota(jnp.int32, (1, seq_len), 1), offsets[0] - 1)
+    limit = jnp.maximum(lax.broadcasted_iota(jnp.int32, (1, seq_len), 1), offsets[:1, :1] - 1)
     visible = lax.broadcasted_iota(jnp.int32, (seq_len, seq_len), 0) <= limit
     copies[0].wait()
     wall[...] = jnp.swapaxes(weight_v[...], 0, 1).reshape(heads * width, latent_dim)
@@ -135,17 +123,14 @@
             send[k, h] = slab[h, 2 * chip + 1 - my_core].astype(bf16)
             keep[k, h] = slab[h, 2 * chip + my_core].astype(bf16)
     own_weight[...] = weight_v[pl.ds((2 * my_chip + my_core) * rows, rows)]
-    for copy in copies[6:]:
-        copy.wait()
-
-
-def latent_kernel(grad_kv, wall, basis, *refs):
-    turn, total, outs = refs[0], refs[-1], refs[1:-1]
+
+
+def latent_kernel(grad_kv, wall, *refs):
+    total, outs = refs[-1], refs[:-1]
     parts = len(outs)
     total[...] = mm(grad_kv[...], wall[...]).astype(bf16).reshape(total.shape)
     for s, out in enumerate(outs):
         out[...] = total[lax.rem(lax.axis_index("tensor") + s, parts)]
-    turn[...] = basis[...].astype(bf16)
 
 
 def pair_kernel(keep, came, *outs):
@@ -153,7 +138,7 @@
         out[...] = (keep[k].astype(f32) + came[k].astype(f32)).astype(out.dtype)
 
 
-def soap_kernel(old, turn, first_moment, second_rot, second_plain, *refs):
+def soap_kernel(old, basis, first_moment, second_rot, second_plain, *refs):
     parts, (slab_out, new_first, new_second, new_plain) = refs[:-4], refs[-4:]
     rows, heads, latent_dim = first_moment.shape
     flat = (heads * rows, latent_dim)
@@ -164,13 +149,14 @@
     def by_row(x):
         return jnp.swapaxes(x.reshape(heads, rows, latent_dim), 0, 1)
 
+    turn = basis[...].astype(bf16)
     grad = functools.reduce(jnp.add, [p[...].astype(f32) for p in parts]).reshape(flat)
-    rotated = mm(grad.astype(bf16), turn[...])
+    rotated = mm(grad.astype(bf16), turn)
     moment = beta_first * by_head(first_moment[...]) + (1.0 - beta_first) * rotated
     rot_sq = beta_second * by_head(second_rot[...]) + (1.0 - beta_second) * rotated * rotated
     plain_sq = beta_second * by_head(second_plain[...]) + (1.0 - beta_second) * grad * grad
     stacked = jnp.concatenate([moment / (jnp.sqrt(rot_sq) + epsilon), moment], axis=0).astype(bf16)
-    turned = mm_nt(stacked, turn[...])
+    turned = mm_nt(stacked, turn)
     direction = blend_share * turned[: flat[0]] + blend_share * turned[flat[0] :] / (jnp.sqrt(plain_sq) + epsilon)
     before = old[...].astype(f32)
     slab_out[...] = (before - learn_rate * (by_row(direction) + decay_rate * before)).astype(bf16)
@@ -179,26 +165,35 @@
     new_plain[...] = by_row(plain_sq)
 
 
-def place_kernel(*refs):
-    chips = (len(refs) - 2) // 2
-    out, sems = refs[-2:]
-    rows = refs[0].shape[0]
-    my_chip, my_core = place_of()
+def row_copies(slabs, out, sems, core):
+    chips, rows = len(slabs), slabs[0].shape[0]
     copies = []
-    for k in range(chips):
-        chip = sender_chip(my_chip, k, chips)
-        for side in range(2):
-            core = my_core if side == 0 else 1 - my_core
-            spot = out.at[pl.ds((2 * chip + core) * rows, rows)]
-            copies.append(pltpu.make_async_copy(refs[side * chips + k], spot, sems.at[2 * k + side]))
+    for k, slab in enumerate(slabs):
+        chip = sender_chip(place_of()[0], k, chips)
+        copies.append(pltpu.make_async_copy(slab, out.at[pl.ds((2 * chip + core) * rows, rows)], sems.at[k]))
     for copy in copies:
         copy.start()
-    for copy in copies:
+    return copies
+
+
+def place_own_kernel(chips, *refs):
+    slabs, state, (out, *new_state, sems) = refs[:chips], refs[chips : chips + 3], refs[chips + 3 :]
+    copies = row_copies(slabs, out, sems, place_of()[1])
+    more = [pltpu.make_async_copy(a, b, sems.at[chips + i]) for i, (a, b) in enumerate(zip(state, new_state))]
+    for copy in more:
+        copy.start()
+    for copy in copies + more:
         copy.wait()
 
 
-def part_sum_kernel(*refs):
-    refs[-1][...] = functools.reduce(jnp.add, [x[...].astype(f32) for x in refs[:-1]]).astype(bf16)
+def place_rest_kernel(chips, *refs):
+    slabs, shares, (out, grad_latent, total, sems) = refs[1 : 1 + chips], refs[1 + chips : -4], refs[-4:]
+    copies = row_copies(slabs, out, sems, 1 - place_of()[1])
+    total[...] = functools.reduce(jnp.add, [x[...].astype(f32) for x in shares]).astype(bf16)
+    last = pltpu.make_async_copy(total, grad_latent, sems.at[chips])
+    last.start()
+    for copy in copies + [last]:
+        copy.wait()
 
 
 def local(latent, q_nope, q_rope, k_rope, grad_out, offsets, weight, basis, first_moment, second_rot, second_plain):
@@ -225,7 +220,7 @@
 
     piece = (heads, rows, latent_dim)
     state = (rows, heads, latent_dim)
-    send, keep, grad_kv, wall, own_weight, basis_v, first_v, rot_v, plain_v = pl.pallas_call(
+    send, keep, grad_kv, wall, own_weight = pl.pallas_call(
         attend_kernel,
         out_shape=(
             pltpu.VMEM((chips,) + piece, bf16),
@@ -233,13 +228,9 @@
             pltpu.VMEM((seq_len, heads * width), bf16),
             pltpu.VMEM((heads * width, latent_dim), bf16),
             pltpu.VMEM(state, bf16),
-            pltpu.VMEM(basis.shape, f32),
-            pltpu.VMEM(state, f32),
-            pltpu.VMEM(state, f32),
-            pltpu.VMEM(state, f32),
         ),
-        in_specs=[pl.BlockSpec(memory_space=pltpu.SMEM)] + [in_hbm] * 10,
-        out_specs=(in_vmem,) * 9,
+        in_specs=[in_vmem] + [in_hbm] * 6,
+        out_specs=(in_vmem,) * 5,
         scratch_shapes=[
             pltpu.VMEM(latent.shape, bf16),
             pltpu.VMEM(q_nope.shape, bf16),
@@ -249,27 +240,33 @@
             pltpu.VMEM(weight.shape, bf16),
             pltpu.VMEM((seq_len, heads * width), bf16),
             pltpu.VMEM((heads, dp, rows, latent_dim), f32),
-            pltpu.SemaphoreType.DMA((10,)),
+            pltpu.SemaphoreType.DMA((6,)),
         ],
         compiler_params=limit_mib(32),
+        cost_estimate=pl.CostEstimate(
+            flops=12 * seq_len * heads * width * latent_dim, bytes_accessed=32 * 1024 * 1024, transcendentals=0
+        ),
         name="attend",
-    )(offsets, *[
+    )(jnp.broadcast_to(offsets, (8, 128)), *[
         pltpu.with_memory_space_constraint(x, pltpu.HBM)
         for x in (
-            latent, q_nope, q_rope, k_rope.T, grad_out, weight, basis, first_moment, second_rot, second_plain
+            latent, q_nope, q_rope, k_rope.T, grad_out, weight
         )
     ])
 
+    send, basis, first_moment, second_rot, second_plain = lax.optimization_barrier(
+        (send, basis, first_moment, second_rot, second_plain)
+    )
     came = core_swap(send)
-    turn, *glat = pl.pallas_call(
+    glat = pl.pallas_call(
         latent_kernel,
-        out_shape=[pltpu.VMEM(basis.shape, bf16)] + [pltpu.VMEM((part_rows, latent_dim), bf16)] * parts,
-        in_specs=[in_vmem] * 3,
-        out_specs=[in_vmem] * (1 + parts),
+        out_shape=[pltpu.VMEM((part_rows, latent_dim), bf16)] * parts,
+        in_specs=[in_vmem] * 2,
+        out_specs=[in_vmem] * parts,
         scratch_shapes=[pltpu.VMEM((parts, part_rows, latent_dim), bf16)],
         compiler_params=limit_mib(8),
         name="latent_share",
-    )(grad_kv, wall, basis_v)
+    )(grad_kv, wall)
     sums = pl.pallas_call(
         pair_kernel,
         out_shape=[pltpu.VMEM(piece, f32 if k == 0 else bf16) for k in range(chips)],
@@ -289,27 +286,29 @@
         out_specs=(in_vmem,) * 4,
         compiler_params=limit_mib(8),
         name="soap",
-    )(own_weight, turn, first_v, rot_v, plain_v, *got)
+    )(own_weight, basis, first_moment, second_rot, second_plain, *got)
 
     mine = [new_slab] + [chip_move(new_slab, k) for k in range(1, chips)]
     others = [core_swap(x) for x in mine]
-    grad_latent = pl.pallas_call(
-        part_sum_kernel,
-        out_shape=jax.ShapeDtypeStruct((part_rows, latent_dim), bf16),
-        in_specs=[in_vmem] * parts,
-        out_specs=in_vmem,
+    new_weight, new_first, new_second, new_plain = pl.pallas_call(
+        functools.partial(place_own_kernel, chips),
+        out_shape=(pltpu.HBM((width, heads, latent_dim), bf16),) + (pltpu.HBM(state, f32),) * 3,
+        in_specs=[in_vmem] * (chips + 3),
+        out_specs=(in_hbm,) * 4,
+        scratch_shapes=[pltpu.SemaphoreType.DMA((chips + 3,))],
         compiler_params=limit_mib(4),
-        name="part_sum",
-    )(*glat)
-    new_weight = pl.pallas_call(
-        place_kernel,
-        out_shape=pltpu.HBM((width, heads, latent_dim), bf16),
-        in_specs=[in_vmem] * (2 * chips),
-        out_specs=in_hbm,
-        scratch_shapes=[pltpu.SemaphoreType.DMA((2 * chips,))],
+        name="place_own",
+    )(*mine, new_first, new_second, new_plain)
+    new_weight, grad_latent = pl.pallas_call(
+        functools.partial(place_rest_kernel, chips),
+        out_shape=(pltpu.HBM((width, heads, latent_dim), bf16), pltpu.HBM((part_rows, latent_dim), bf16)),
+        in_specs=[in_hbm] + [in_vmem] * (chips + parts),
+        out_specs=(in_hbm, in_hbm),
+        scratch_shapes=[pltpu.VMEM((part_rows, latent_dim), bf16), pltpu.SemaphoreType.DMA((chips + 1,))],
+        input_output_aliases={0: 0},
         compiler_params=limit_mib(4),
-        name="place",
-    )(*mine, *others)
+        name="place_rest",
+    )(new_weight, *others, *glat)
     return (grad_latent, new_weight, new_first, new_second, new_plain)
 
 

time: 37.1 us -> 35.4 us (0.954)
  local copies, waits for them, and re-layouts: 2.11 us -> 0.02 us
    unnamed x3 -> x8, local copies, waits for them, and re-layouts: 2.11 us -> 0.01 us
  transfers between devices with their start and end apart: 14 -> 14, of which waited for: 4 -> 4; matrix products, arithmetic and copies ran while one was open for 6% -> 0% of each run, Pallas kernels for 7% -> 8%
where the time goes in v3:
time: 35.4 us; the launch traced here: 35.3 us
  starting transfers between devices  17.7 us (50%)
  Pallas kernels  12.9 us (36%)
  waiting for transfers between devices  3.23 us (9%)
  between operations  1.4 us (4%)
    pallas_call x1, Pallas kernels, local(): pl.pallas_call(attend_kernel, out_shape=(pltpu.VMEM((chips,) + piece, bf1...  9.03 us
    ppermute x3, starting transfers between devices, part_move(): lax.ppermute(x, 'tensor', [(i, (i + s) % parts) for i in range(parts)])  8.22 us
    ppermute x6, starting transfers between devices, chip_move(): return lax.ppermute(x, 'dp', pairs)  8.02 us
    ppermute x6, waiting for transfers between devices, chip_move(): return lax.ppermute(x, 'dp', pairs)  2.51 us
    ppermute x5, starting transfers between devices, core_swap(): return lax.ppermute(x, 'dp', [(i, i ^ 1) for i in range(dp)])  1.48 us
    pallas_call x1, Pallas kernels, local(): pl.pallas_call(functools.partial(place_own_kernel, chips), out_shape=(plt...  1.11 us
    pallas_call x1, Pallas kernels, local(): pl.pallas_call(soap_kernel, out_shape=(pltpu.VMEM(state, bf16),) + (pltpu...  0.97 us
    pallas_call x1, Pallas kernels, local(): pl.pallas_call(functools.partial(place_rest_kernel, chips), out_shape=(pl...  0.9 us
  transfers between devices with their start and end apart: 14, of which 4 were waited for; matrix products, arithmetic and copies ran while one was open for 0% of the time, Pallas kernels for 8%

profile of v3, /device:TPU:0, one launch (start us, length us, event | category | flops | bytes accessed | tf_op | source)
XLA Modules:
  0.0 35.3 jit_solution(14267176774719973103)
XLA Ops:
  1.3 9.0 %attend.1 = (bf16[4,4,32,512]{3,2,1,0:T(8,128)(2,1)S(1)}, bf16[4,4,32,512]{3,2,1,0:T(8,128)(2,1)S(1)}, bf16[576,1024]{1,0:T(8,128)(2,1)S(1)}, bf16[1024,512]{1,0:T(8,128)(2,1)S(1)}, bf16[32,4,512]{2,1,0:T(4,128)(2,1)S(1)}) custom-call(s32[8,128]{1,0:T(8,128)S(1)} %broadcast_in_dim.2.offsets, bf16[576,512]{1,0:T(8,128)(2,1)} %latent.1, ...), custom_call_target="tpu_custom_call" | custom-call | flops 3623878656 | bytes 33554432 | tf_op jit(solution)/shard_map/attend/pallas_call | solution.py:223
  10.3 0.5 %collective-permute-start = (bf16[4,4,32,512]{3,2,1,0:T(8,128)(2,1)S(1)}, bf16[4,4,32,512]{3,2,1,0:T(8,128)(2,1)S(1)}, u32[]{:S(2)}, u32[]{:S(2)}) collective-permute-start(bf16[4,4,32,512]{3,2,1,0:T(8,128)(2,1)S(1)} %get-tuple-element.48), channel_id=1, source_target_pairs={{0,4},{4,0},{8,12},{12,8},{16,20},{20,16},{24,28},{28,24},{1,5},{5... | collective-permute-start | bytes 1572872 | tf_op jit(solution)/shard_map/ppermute | solution.py:209
  10.9 0.8 %latent_share.1 = (bf16[144,512]{1,0:T(8,128)(2,1)S(1)}, bf16[144,512]{1,0:T(8,128)(2,1)S(1)}, bf16[144,512]{1,0:T(8,128)(2,1)S(1)}, bf16[144,512]{1,0:T(8,128)(2,1)S(1)}) custom-call(bf16[576,1024]{1,0:T(8,128)(2,1)S(1)} %get-tuple-element.53.grad_kv, bf16[1024,512]{1,0:T(8,128)(2,1)S(1)} %get-tuple-element.54.wall), custom_call_target="tpu_custom_call" | custom-call | tf_op jit(solution)/shard_map/latent_share/pallas_call | solution.py:261
  11.7 0.7 %collective-permute-done.came = bf16[4,4,32,512]{3,2,1,0:T(8,128)(2,1)S(1)} collective-permute-done((bf16[4,4,32,512]{3,2,1,0:T(8,128)(2,1)S(1)}, bf16[4,4,32,512]{3,2,1,0:T(8,128)(2,1)S(1)}, u32[]{:S(2)}, u32[]{:S(2)}) %collective-permute-start) | collective-permute-done | bytes 524320 | tf_op jit(solution)/shard_map/ppermute | solution.py:209
  12.4 0.1 pair_sum.1
  12.5 2.9 %collective-permute-start.1 = (bf16[4,32,512]{2,1,0:T(8,128)(2,1)S(1)}, bf16[4,32,512]{2,1,0:T(8,128)(2,1)S(1)}, u32[]{:S(2)}, u32[]{:S(2)}) collective-permute-start(bf16[4,32,512]{2,1,0:T(8,128)(2,1)S(1)} %get-tuple-element.60), channel_id=1, source_target_pairs={{0,8},{4,12},{8,0},{12,4},{16,24},{20,28},{24,16},{28,20},{1,9},{5... | collective-permute-start | bytes 393224 | tf_op jit(solution)/shard_map/ppermute | solution.py:216
  15.4 1.5 %collective-permute-start.2 = (bf16[4,32,512]{2,1,0:T(8,128)(2,1)S(1)}, bf16[4,32,512]{2,1,0:T(8,128)(2,1)S(1)}, u32[]{:S(2)}, u32[]{:S(2)}) collective-permute-start(bf16[4,32,512]{2,1,0:T(8,128)(2,1)S(1)} %get-tuple-element.61), channel_id=1, source_target_pairs={{0,16},{4,20},{8,24},{12,28},{16,0},{20,4},{24,8},{28,12},{1,17},{... | collective-permute-start | bytes 393224 | tf_op jit(solution)/shard_map/ppermute | solution.py:216
  17.0 0.0 collective-permute-start.3
  17.0 2.0 %collective-permute-start.11 = (bf16[144,512]{1,0:T(8,128)(2,1)S(1)}, bf16[144,512]{1,0:T(8,128)(2,1)S(1)}, u32[]{:S(2)}, u32[]{:S(2)}) collective-permute-start(bf16[144,512]{1,0:T(8,128)(2,1)S(1)} %get-tuple-element.69), channel_id=1, source_target_pairs={{0,1},{1,2},{2,3},{3,0},{4,5},{5,6},{6,7},{7,4},{8,9},{9,10},{10,1... | collective-permute-start | bytes 442376 | tf_op jit(solution)/shard_map/ppermute | solution.py:219
  19.0 2.6 %collective-permute-start.12 = (bf16[144,512]{1,0:T(8,128)(2,1)S(1)}, bf16[144,512]{1,0:T(8,128)(2,1)S(1)}, u32[]{:S(2)}, u32[]{:S(2)}) collective-permute-start(bf16[144,512]{1,0:T(8,128)(2,1)S(1)} %get-tuple-element.70), channel_id=1, source_target_pairs={{0,2},{1,3},{2,0},{3,1},{4,6},{5,7},{6,4},{7,5},{8,10},{9,11},{10,... | collective-permute-start | bytes 442376 | tf_op jit(solution)/shard_map/ppermute | solution.py:219
  21.6 1.9 %collective-permute-done.2.refs_2_ = bf16[4,32,512]{2,1,0:T(8,128)(2,1)S(1)} collective-permute-done((bf16[4,32,512]{2,1,0:T(8,128)(2,1)S(1)}, bf16[4,32,512]{2,1,0:T(8,128)(2,1)S(1)}, u32[]{:S(2)}, u32[]{:S(2)}) %collective-permute-start.2) | collective-permute-done | bytes 131104 | tf_op jit(solution)/shard_map/ppermute | solution.py:216
  23.5 0.0 collective-permute-done.3.refs_3_
  23.5 1.0 %soap.1 = (bf16[32,4,512]{2,1,0:T(4,128)(2,1)S(1)}, f32[32,4,512]{2,1,0:T(4,128)S(1)}, f32[32,4,512]{2,1,0:T(4,128)S(1)}, f32[32,4,512]{2,1,0:T(4,128)S(1)}) custom-call(bf16[32,4,512]{2,1,0:T(4,128)(2,1)S(1)} %get-tuple-element.41.old, f32[512,512]{1,0:T(8,128)S(1)} %copy-done, f32[32,4,512]{2,1,0:T(4,128)S(1)} %copy-done.1, f32[32,4,512]{2,1,0:T(4,128)S(1)} %copy-done.2, ...), custom_call_target="tpu_custom_call" | custom-call | tf_op jit(solution)/shard_map/soap/pallas_call | solution.py:282
  24.5 1.6 %collective-permute-start.6 = (bf16[32,4,512]{2,1,0:T(4,128)(2,1)S(1)}, bf16[32,4,512]{2,1,0:T(4,128)(2,1)S(1)}, u32[]{:S(2)}, u32[]{:S(2)}) collective-permute-start(bf16[32,4,512]{2,1,0:T(4,128)(2,1)S(1)} %get-tuple-element.63.refs_0_), channel_id=1, source_target_pairs={{0,24},{4,28},{8,16},{12,20},{16,8},{20,12},{24,0},{28,4},{1,25},{... | collective-permute-start | bytes 393224 | tf_op jit(solution)/shard_map/ppermute | solution.py:216
  26.1 1.5 %collective-permute-start.4 = (bf16[32,4,512]{2,1,0:T(4,128)(2,1)S(1)}, bf16[32,4,512]{2,1,0:T(4,128)(2,1)S(1)}, u32[]{:S(2)}, u32[]{:S(2)}) collective-permute-start(bf16[32,4,512]{2,1,0:T(4,128)(2,1)S(1)} %get-tuple-element.63.refs_0_), channel_id=1, source_target_pairs={{0,8},{4,12},{8,0},{12,4},{16,24},{20,28},{24,16},{28,20},{1,9},{5... | collective-permute-start | bytes 393224 | tf_op jit(solution)/shard_map/ppermute | solution.py:216
  27.6 0.5 %collective-permute-start.5 = (bf16[32,4,512]{2,1,0:T(4,128)(2,1)S(1)}, bf16[32,4,512]{2,1,0:T(4,128)(2,1)S(1)}, u32[]{:S(2)}, u32[]{:S(2)}) collective-permute-start(bf16[32,4,512]{2,1,0:T(4,128)(2,1)S(1)} %get-tuple-element.63.refs_0_), channel_id=1, source_target_pairs={{0,16},{4,20},{8,24},{12,28},{16,0},{20,4},{24,8},{28,12},{1,17},{... | collective-permute-start | bytes 393224 | tf_op jit(solution)/shard_map/ppermute | solution.py:216
  28.1 0.0 collective-permute-done.11.refs_6_
  28.1 3.6 %collective-permute-start.13 = (bf16[144,512]{1,0:T(8,128)(2,1)S(1)}, bf16[144,512]{1,0:T(8,128)(2,1)S(1)}, u32[]{:S(2)}, u32[]{:S(2)}) collective-permute-start(bf16[144,512]{1,0:T(8,128)(2,1)S(1)} %get-tuple-element.71), channel_id=1, source_target_pairs={{0,3},{1,0},{2,1},{3,2},{4,7},{5,4},{6,5},{7,6},{8,11},{9,8},{10,9... | collective-permute-start | bytes 442376 | tf_op jit(solution)/shard_map/ppermute | solution.py:219
  31.7 0.5 %collective-permute-start.10 = (bf16[32,4,512]{2,1,0:T(4,128)(2,1)S(1)}, bf16[32,4,512]{2,1,0:T(4,128)(2,1)S(1)}, u32[]{:S(2)}, u32[]{:S(2)}) collective-permute-start(bf16[32,4,512]{2,1,0:T(4,128)(2,1)S(1)} %collective-permute-done.6.refs_3_), channel_id=1, source_target_pairs={{0,4},{4,0},{8,12},{12,8},{16,20},{20,16},{24,28},{28,24},{1,5},{5... | collective-permute-start | bytes 393224 | tf_op jit(solution)/shard_map/ppermute | solution.py:209
  32.2 0.5 %collective-permute-done.4.refs_1_ = bf16[32,4,512]{2,1,0:T(4,128)(2,1)S(1)} collective-permute-done((bf16[32,4,512]{2,1,0:T(4,128)(2,1)S(1)}, bf16[32,4,512]{2,1,0:T(4,128)(2,1)S(1)}, u32[]{:S(2)}, u32[]{:S(2)}) %collective-permute-start.4) | collective-permute-done | bytes 131104 | tf_op jit(solution)/shard_map/ppermute | solution.py:216
  32.7 0.1 collective-permute-done.5.refs_2_
  32.8 0.5 %collective-permute-start.9 = (bf16[32,4,512]{2,1,0:T(4,128)(2,1)S(1)}, bf16[32,4,512]{2,1,0:T(4,128)(2,1)S(1)}, u32[]{:S(2)}, u32[]{:S(2)}) collective-permute-start(bf16[32,4,512]{2,1,0:T(4,128)(2,1)S(1)} %collective-permute-done.5.refs_2_), channel_id=1, source_target_pairs={{0,4},{4,0},{8,12},{12,8},{16,20},{20,16},{24,28},{28,24},{1,5},{5... | collective-permute-start | bytes 393224 | tf_op jit(solution)/shard_map/ppermute | solution.py:209
  33.2 1.1 %place_own.1 = (bf16[256,4,512]{2,1,0:T(4,128)(2,1)}, f32[32,4,512]{2,1,0:T(4,128)}, f32[32,4,512]{2,1,0:T(4,128)}, f32[32,4,512]{2,1,0:T(4,128)}) custom-call(bf16[32,4,512]{2,1,0:T(4,128)(2,1)S(1)} %get-tuple-element.63.refs_0_, bf16[32,4,512]{2,1,0:T(4,128)(2,1)S(1)} %collective-permute-done.4.refs_1_, ...), custom_call_target="tpu_custom_call" | custom-call | tf_op jit(solution)/shard_map/place_own/pallas_call | solution.py:293
  34.4 0.9 %place_rest.1 = (bf16[256,4,512]{2,1,0:T(4,128)(2,1)}, bf16[144,512]{1,0:T(8,128)(2,1)}) custom-call(bf16[256,4,512]{2,1,0:T(4,128)(2,1)} %get-tuple-element.67.refs_0_, bf16[32,4,512]{2,1,0:T(4,128)(2,1)S(1)} %collective-permute-done.7.refs_1_, bf16[32,4,512]{2,1,0:T(4,128)(2,1)S(1)} %collective-permute-done.8.refs_2_, ...), custom_call_target="tpu_custom_call", output_to_operand_aliasing={{0}: (0, {})} | custom-call | tf_op jit(solution)/shard_map/place_rest/pallas_call | solution.py:302
  (19 shorter events, 0.0 us)
Async XLA Ops:
  10.3 2.1 %collective-permute-start = (bf16[4,4,32,512]{3,2,1,0:T(8,128)(2,1)S(1)}, bf16[4,4,32,512]{3,2,1,0:T(8,128)(2,1)S(1)}, u32[]{:S(2)}, u32[]{:S(2)}) collective-permute-start(bf16[4,4,32,512]{3,2,1,0:T(8,128)(2,1)S(1)} %get-tuple-element.48), channel_id=1, source_target_pairs={{0,4},{4,0},{8,12},{12,8},{16,20},{20,16},{24,28},{28,24},{1,5},{5... | collective-permute-start | bytes 1572872 | tf_op jit(solution)/shard_map/ppermute | solution.py:209
  10.8 12.7 %copy-start = (f32[512,512]{1,0:T(8,128)S(1)}, f32[512,512]{1,0:T(8,128)}, u32[]{:S(2)}) copy-start(f32[512,512]{1,0:T(8,128)} %basis) | copy-start | bytes 3145732
  10.9 12.7 %copy-start.1 = (f32[32,4,512]{2,1,0:T(4,128)S(1)}, f32[32,4,512]{2,1,0:T(4,128)}, u32[]{:S(2)}) copy-start(f32[32,4,512]{2,1,0:T(4,128)} %first_moment) | copy-start | bytes 786436
  10.9 12.7 %copy-start.2 = (f32[32,4,512]{2,1,0:T(4,128)S(1)}, f32[32,4,512]{2,1,0:T(4,128)}, u32[]{:S(2)}) copy-start(f32[32,4,512]{2,1,0:T(4,128)} %second_rot) | copy-start | bytes 786436
  10.9 12.7 %copy-start.3 = (f32[32,4,512]{2,1,0:T(4,128)S(1)}, f32[32,4,512]{2,1,0:T(4,128)}, u32[]{:S(2)}) copy-start(f32[32,4,512]{2,1,0:T(4,128)} %second_plain) | copy-start | bytes 786436
  12.5 9.1 %collective-permute-start.1 = (bf16[4,32,512]{2,1,0:T(8,128)(2,1)S(1)}, bf16[4,32,512]{2,1,0:T(8,128)(2,1)S(1)}, u32[]{:S(2)}, u32[]{:S(2)}) collective-permute-start(bf16[4,32,512]{2,1,0:T(8,128)(2,1)S(1)} %get-tuple-element.60), channel_id=1, source_target_pairs={{0,8},{4,12},{8,0},{12,4},{16,24},{20,28},{24,16},{28,20},{1,9},{5... | collective-permute-start | bytes 393224 | tf_op jit(solution)/shard_map/ppermute | solution.py:216
  15.4 8.1 %collective-permute-start.2 = (bf16[4,32,512]{2,1,0:T(8,128)(2,1)S(1)}, bf16[4,32,512]{2,1,0:T(8,128)(2,1)S(1)}, u32[]{:S(2)}, u32[]{:S(2)}) collective-permute-start(bf16[4,32,512]{2,1,0:T(8,128)(2,1)S(1)} %get-tuple-element.61), channel_id=1, source_target_pairs={{0,16},{4,20},{8,24},{12,28},{16,0},{20,4},{24,8},{28,12},{1,17},{... | collective-permute-start | bytes 393224 | tf_op jit(solution)/shard_map/ppermute | solution.py:216
  17.0 6.6 %collective-permute-start.3 = (bf16[4,32,512]{2,1,0:T(8,128)(2,1)S(1)}, bf16[4,32,512]{2,1,0:T(8,128)(2,1)S(1)}, u32[]{:S(2)}, u32[]{:S(2)}) collective-permute-start(bf16[4,32,512]{2,1,0:T(8,128)(2,1)S(1)} %get-tuple-element.62), channel_id=1, source_target_pairs={{0,24},{4,28},{8,16},{12,20},{16,8},{20,12},{24,0},{28,4},{1,25},{... | collective-permute-start | bytes 393224 | tf_op jit(solution)/shard_map/ppermute | solution.py:216
  17.0 11.1 %collective-permute-start.11 = (bf16[144,512]{1,0:T(8,128)(2,1)S(1)}, bf16[144,512]{1,0:T(8,128)(2,1)S(1)}, u32[]{:S(2)}, u32[]{:S(2)}) collective-permute-start(bf16[144,512]{1,0:T(8,128)(2,1)S(1)} %get-tuple-element.69), channel_id=1, source_target_pairs={{0,1},{1,2},{2,3},{3,0},{4,5},{5,6},{6,7},{7,4},{8,9},{9,10},{10,1... | collective-permute-start | bytes 442376 | tf_op jit(solution)/shard_map/ppermute | solution.py:219
  19.0 12.7 %collective-permute-start.12 = (bf16[144,512]{1,0:T(8,128)(2,1)S(1)}, bf16[144,512]{1,0:T(8,128)(2,1)S(1)}, u32[]{:S(2)}, u32[]{:S(2)}) collective-permute-start(bf16[144,512]{1,0:T(8,128)(2,1)S(1)} %get-tuple-element.70), channel_id=1, source_target_pairs={{0,2},{1,3},{2,0},{3,1},{4,6},{5,7},{6,4},{7,5},{8,10},{9,11},{10,... | collective-permute-start | bytes 442376 | tf_op jit(solution)/shard_map/ppermute | solution.py:219
  24.5 7.2 %collective-permute-start.6 = (bf16[32,4,512]{2,1,0:T(4,128)(2,1)S(1)}, bf16[32,4,512]{2,1,0:T(4,128)(2,1)S(1)}, u32[]{:S(2)}, u32[]{:S(2)}) collective-permute-start(bf16[32,4,512]{2,1,0:T(4,128)(2,1)S(1)} %get-tuple-element.63.refs_0_), channel_id=1, source_target_pairs={{0,24},{4,28},{8,16},{12,20},{16,8},{20,12},{24,0},{28,4},{1,25},{... | collective-permute-start | bytes 393224 | tf_op jit(solution)/shard_map/ppermute | solution.py:216
  26.1 6.7 %collective-permute-start.4 = (bf16[32,4,512]{2,1,0:T(4,128)(2,1)S(1)}, bf16[32,4,512]{2,1,0:T(4,128)(2,1)S(1)}, u32[]{:S(2)}, u32[]{:S(2)}) collective-permute-start(bf16[32,4,512]{2,1,0:T(4,128)(2,1)S(1)} %get-tuple-element.63.refs_0_), channel_id=1, source_target_pairs={{0,8},{4,12},{8,0},{12,4},{16,24},{20,28},{24,16},{28,20},{1,9},{5... | collective-permute-start | bytes 393224 | tf_op jit(solution)/shard_map/ppermute | solution.py:216
  27.6 5.2 %collective-permute-start.5 = (bf16[32,4,512]{2,1,0:T(4,128)(2,1)S(1)}, bf16[32,4,512]{2,1,0:T(4,128)(2,1)S(1)}, u32[]{:S(2)}, u32[]{:S(2)}) collective-permute-start(bf16[32,4,512]{2,1,0:T(4,128)(2,1)S(1)} %get-tuple-element.63.refs_0_), channel_id=1, source_target_pairs={{0,16},{4,20},{8,24},{12,28},{16,0},{20,4},{24,8},{28,12},{1,17},{... | collective-permute-start | bytes 393224 | tf_op jit(solution)/shard_map/ppermute | solution.py:216
  28.1 6.3 %collective-permute-start.13 = (bf16[144,512]{1,0:T(8,128)(2,1)S(1)}, bf16[144,512]{1,0:T(8,128)(2,1)S(1)}, u32[]{:S(2)}, u32[]{:S(2)}) collective-permute-start(bf16[144,512]{1,0:T(8,128)(2,1)S(1)} %get-tuple-element.71), channel_id=1, source_target_pairs={{0,3},{1,0},{2,1},{3,2},{4,7},{5,4},{6,5},{7,6},{8,11},{9,8},{10,9... | collective-permute-start | bytes 442376 | tf_op jit(solution)/shard_map/ppermute | solution.py:219
  31.7 2.7 %collective-permute-start.7 = (bf16[32,4,512]{2,1,0:T(4,128)(2,1)S(1)}, bf16[32,4,512]{2,1,0:T(4,128)(2,1)S(1)}, u32[]{:S(2)}, u32[]{:S(2)}) collective-permute-start(bf16[32,4,512]{2,1,0:T(4,128)(2,1)S(1)} %get-tuple-element.63.refs_0_), channel_id=1, source_target_pairs={{0,4},{4,0},{8,12},{12,8},{16,20},{20,16},{24,28},{28,24},{1,5},{5... | collective-permute-start | bytes 393224 | tf_op jit(solution)/shard_map/ppermute | solution.py:209
  31.7 2.7 %collective-permute-start.10 = (bf16[32,4,512]{2,1,0:T(4,128)(2,1)S(1)}, bf16[32,4,512]{2,1,0:T(4,128)(2,1)S(1)}, u32[]{:S(2)}, u32[]{:S(2)}) collective-permute-start(bf16[32,4,512]{2,1,0:T(4,128)(2,1)S(1)} %collective-permute-done.6.refs_3_), channel_id=1, source_target_pairs={{0,4},{4,0},{8,12},{12,8},{16,20},{20,16},{24,28},{28,24},{1,5},{5... | collective-permute-start | bytes 393224 | tf_op jit(solution)/shard_map/ppermute | solution.py:209
  32.7 1.7 %collective-permute-start.8 = (bf16[32,4,512]{2,1,0:T(4,128)(2,1)S(1)}, bf16[32,4,512]{2,1,0:T(4,128)(2,1)S(1)}, u32[]{:S(2)}, u32[]{:S(2)}) collective-permute-start(bf16[32,4,512]{2,1,0:T(4,128)(2,1)S(1)} %collective-permute-done.4.refs_1_), channel_id=1, source_target_pairs={{0,4},{4,0},{8,12},{12,8},{16,20},{20,16},{24,28},{28,24},{1,5},{5... | collective-permute-start | bytes 393224 | tf_op jit(solution)/shard_map/ppermute | solution.py:209
  32.8 1.6 %collective-permute-start.9 = (bf16[32,4,512]{2,1,0:T(4,128)(2,1)S(1)}, bf16[32,4,512]{2,1,0:T(4,128)(2,1)S(1)}, u32[]{:S(2)}, u32[]{:S(2)}) collective-permute-start(bf16[32,4,512]{2,1,0:T(4,128)(2,1)S(1)} %collective-permute-done.5.refs_2_), channel_id=1, source_target_pairs={{0,4},{4,0},{8,12},{12,8},{16,20},{20,16},{24,28},{28,24},{1,5},{5... | collective-permute-start | bytes 393224 | tf_op jit(solution)/shard_map/ppermute | solution.py:209

commit v4 on v3

--- a/solution.py
+++ b/solution.py
@@ -69,6 +69,7 @@
     g_out_v,
     weight_v,
     key_value,
+    bias,
     slab,
     sems,
 ):
@@ -87,10 +88,13 @@
         (grad_out, g_out_v),
     ]
     copies = [pltpu.make_async_copy(a, b, sems.at[i]) for i, (a, b) in enumerate(pairs)]
-    for copy in copies:
+    for copy in copies[:2]:
         copy.start()
     limit = jnp.maximum(lax.broadcasted_iota(jnp.int32, (1, seq_len), 1), offsets[:1, :1] - 1)
-    visible = lax.broadcasted_iota(jnp.int32, (seq_len, seq_len), 0) <= limit
+    bias[...] = jnp.where(lax.broadcasted_iota(jnp.int32, (seq_len, seq_len), 0) <= limit, 0.0, -1e30)
+    zeros = jnp.zeros((seq_len, head_dim), bf16)
+    for copy in copies[2:]:
+        copy.start(priority=1)
     copies[0].wait()
     wall[...] = jnp.swapaxes(weight_v[...], 0, 1).reshape(heads * width, latent_dim)
     copies[1].wait()
@@ -105,16 +109,25 @@
         keys = key_value[:, h * width : h * width + head_dim]
         values = key_value[:, h * width + head_dim : (h + 1) * width]
         k_all = jnp.concatenate([keys, k_side], axis=1)
-        scores = jnp.where(visible, mm_nt(k_all, q_all), -1e30)
+        scores = mm_nt(k_all, q_all) + bias[...]
         top = jnp.max(scores, axis=0, keepdims=True)
         terms = jnp.exp2((scores - top) * (scale * log2_e))
         inv = 1.0 / jnp.sum(terms, axis=0, keepdims=True)
         probs = terms * inv
+        probs_low = probs.astype(bf16)
         grad_probs = mm_nt(values, g_out)
         delta = jnp.sum(probs * grad_probs, axis=0, keepdims=True)
         grad_scores = (probs * (grad_probs - delta) * scale).astype(bf16)
-        grad_kv[:, h * width : h * width + head_dim] = mm(grad_scores, q_main).astype(bf16)
-        grad_kv[:, h * width + head_dim : (h + 1) * width] = mm(probs.astype(bf16), g_out).astype(bf16)
+        lhs = jnp.concatenate([grad_scores, zeros[:, : -seq_len % 128], probs_low], axis=1)
+        rhs = jnp.concatenate(
+            [
+                jnp.concatenate([q_main, zeros], axis=1),
+                jnp.concatenate([zeros, zeros], axis=1)[: -seq_len % 128],
+                jnp.concatenate([zeros, g_out], axis=1),
+            ],
+            axis=0,
+        )
+        grad_kv[:, h * width : (h + 1) * width] = mm(lhs, rhs).astype(bf16)
     slab[...] = mm_tn(grad_kv[...], lat[...]).reshape(heads, 2 * chips, rows, latent_dim)
     my_chip, my_core = place_of()
     for k in range(chips):
@@ -138,28 +151,36 @@
         out[...] = (keep[k].astype(f32) + came[k].astype(f32)).astype(out.dtype)
 
 
-def soap_kernel(old, basis, first_moment, second_rot, second_plain, *refs):
+def by_head(x):
+    return jnp.swapaxes(x, 0, 1).reshape(x.shape[0] * x.shape[1], x.shape[2])
+
+
+def ready_kernel(old, basis, first_moment, second_rot, second_plain, before, turn, first, rot, plain):
+    before[...] = by_head(old[...].astype(f32))
+    turn[...] = basis[...].astype(bf16)
+    first[...] = by_head(beta_first * first_moment[...])
+    rot[...] = by_head(beta_second * second_rot[...])
+    plain[...] = by_head(beta_second * second_plain[...])
+
+
+def soap_kernel(before, turn, first, rot, plain, *refs):
     parts, (slab_out, new_first, new_second, new_plain) = refs[:-4], refs[-4:]
-    rows, heads, latent_dim = first_moment.shape
-    flat = (heads * rows, latent_dim)
-
-    def by_head(x):
-        return jnp.swapaxes(x, 0, 1).reshape(flat)
+    rows, heads, latent_dim = new_first.shape
+    count = rows * heads
 
     def by_row(x):
         return jnp.swapaxes(x.reshape(heads, rows, latent_dim), 0, 1)
 
-    turn = basis[...].astype(bf16)
-    grad = functools.reduce(jnp.add, [p[...].astype(f32) for p in parts]).reshape(flat)
-    rotated = mm(grad.astype(bf16), turn)
-    moment = beta_first * by_head(first_moment[...]) + (1.0 - beta_first) * rotated
-    rot_sq = beta_second * by_head(second_rot[...]) + (1.0 - beta_second) * rotated * rotated
-    plain_sq = beta_second * by_head(second_plain[...]) + (1.0 - beta_second) * grad * grad
+    grad = functools.reduce(jnp.add, [p[...].astype(f32) for p in parts]).reshape(count, latent_dim)
+    rotated = mm(grad.astype(bf16), turn[...])
+    moment = first[...] + (1.0 - beta_first) * rotated
+    rot_sq = rot[...] + (1.0 - beta_second) * rotated * rotated
+    plain_sq = plain[...] + (1.0 - beta_second) * grad * grad
     stacked = jnp.concatenate([moment / (jnp.sqrt(rot_sq) + epsilon), moment], axis=0).astype(bf16)
-    turned = mm_nt(stacked, turn)
-    direction = blend_share * turned[: flat[0]] + blend_share * turned[flat[0] :] / (jnp.sqrt(plain_sq) + epsilon)
-    before = old[...].astype(f32)
-    slab_out[...] = (before - learn_rate * (by_row(direction) + decay_rate * before)).astype(bf16)
+    turned = mm_nt(stacked, turn[...])
+    direction = blend_share * turned[:count] + blend_share * turned[count:] / (jnp.sqrt(plain_sq) + epsilon)
+    old = before[...]
+    slab_out[...] = by_row(old - learn_rate * (direction + decay_rate * old)).astype(bf16)
     new_first[...] = by_row(moment)
     new_second[...] = by_row(rot_sq)
     new_plain[...] = by_row(plain_sq)
@@ -239,6 +260,7 @@
             pltpu.VMEM(grad_out.shape, bf16),
             pltpu.VMEM(weight.shape, bf16),
             pltpu.VMEM((seq_len, heads * width), bf16),
+            pltpu.VMEM((seq_len, seq_len), f32),
             pltpu.VMEM((heads, dp, rows, latent_dim), f32),
             pltpu.SemaphoreType.DMA((6,)),
         ],
@@ -279,6 +301,15 @@
     got = [sums[0]] + [chip_move(sums[k], k) for k in range(1, chips)]
     glat = [glat[0]] + [part_move(glat[s], s) for s in range(1, parts)]
 
+    flat = (heads * rows, latent_dim)
+    ready = pl.pallas_call(
+        ready_kernel,
+        out_shape=[pltpu.VMEM(flat, f32), pltpu.VMEM(basis.shape, bf16)] + [pltpu.VMEM(flat, f32)] * 3,
+        in_specs=[in_vmem] * 5,
+        out_specs=[in_vmem] * 5,
+        compiler_params=limit_mib(8),
+        name="ready",
+    )(own_weight, basis, first_moment, second_rot, second_plain)
     new_slab, new_first, new_second, new_plain = pl.pallas_call(
         soap_kernel,
         out_shape=(pltpu.VMEM(state, bf16),) + (pltpu.VMEM(state, f32),) * 3,
@@ -286,7 +317,7 @@
         out_specs=(in_vmem,) * 4,
         compiler_params=limit_mib(8),
         name="soap",
-    )(own_weight, basis, first_moment, second_rot, second_plain, *got)
+    )(*ready, *got)
 
     mine = [new_slab] + [chip_move(new_slab, k) for k in range(1, chips)]
     others = [core_swap(x) for x in mine]

time: 35.4 us -> 34.6 us (0.977)
  Pallas kernels: 12.9 us -> 12.4 us
    pallas_call x1, Pallas kernels: 9.03 us -> 8.38 us  [local(): pl.pallas_call(attend_kernel, out_shape=(pltpu.VMEM((chips,) + piece, bf1...]
  transfers between devices with their start and end apart: 14 -> 14, of which waited for: 4 -> 4; matrix products, arithmetic and copies ran while one was open for 0% -> 0% of each run, Pallas kernels for 8% -> 9%
where the time goes in v4:
time: 34.6 us; the launch traced here: 34.5 us
  starting transfers between devices  17.7 us (51%)
  Pallas kernels  12.4 us (36%)
  waiting for transfers between devices  2.95 us (9%)
  between operations  1.39 us (4%)
    pallas_call x1, Pallas kernels, local(): pl.pallas_call(attend_kernel, out_shape=(pltpu.VMEM((chips,) + piece, bf1...  8.38 us
    ppermute x3, starting transfers between devices, part_move(): lax.ppermute(x, 'tensor', [(i, (i + s) % parts) for i in range(parts)])  8.22 us
    ppermute x6, starting transfers between devices, chip_move(): return lax.ppermute(x, 'dp', pairs)  8.02 us
    ppermute x6, waiting for transfers between devices, chip_move(): return lax.ppermute(x, 'dp', pairs)  2.22 us
    ppermute x5, starting transfers between devices, core_swap(): return lax.ppermute(x, 'dp', [(i, i ^ 1) for i in range(dp)])  1.49 us
    pallas_call x1, Pallas kernels, local(): pl.pallas_call(functools.partial(place_own_kernel, chips), out_shape=(plt...  1.11 us
    pallas_call x1, Pallas kernels, local(): pl.pallas_call(functools.partial(place_rest_kernel, chips), out_shape=(pl...  0.9 us
    pallas_call x1, Pallas kernels, local(): pl.pallas_call(latent_kernel, out_shape=[pltpu.VMEM((part_rows, latent_di...  0.81 us
  transfers between devices with their start and end apart: 14, of which 4 were waited for; matrix products, arithmetic and copies ran while one was open for 0% of the time, Pallas kernels for 9%

profile of v4, /device:TPU:0, one launch (start us, length us, event | category | flops | bytes accessed | tf_op | source)
XLA Modules:
  0.0 34.5 jit_solution(12640634297160264407)
XLA Ops:
  1.3 8.4 %attend.1 = (bf16[4,4,32,512]{3,2,1,0:T(8,128)(2,1)S(1)}, bf16[4,4,32,512]{3,2,1,0:T(8,128)(2,1)S(1)}, bf16[576,1024]{1,0:T(8,128)(2,1)S(1)}, bf16[1024,512]{1,0:T(8,128)(2,1)S(1)}, bf16[32,4,512]{2,1,0:T(4,128)(2,1)S(1)}) custom-call(s32[8,128]{1,0:T(8,128)S(1)} %broadcast_in_dim.2.offsets, bf16[576,512]{1,0:T(8,128)(2,1)} %latent.1, ...), custom_call_target="tpu_custom_call" | custom-call | flops 3623878656 | bytes 33554432 | tf_op jit(solution)/shard_map/attend/pallas_call | solution.py:244
  9.7 0.5 %collective-permute-start = (bf16[4,4,32,512]{3,2,1,0:T(8,128)(2,1)S(1)}, bf16[4,4,32,512]{3,2,1,0:T(8,128)(2,1)S(1)}, u32[]{:S(2)}, u32[]{:S(2)}) collective-permute-start(bf16[4,4,32,512]{3,2,1,0:T(8,128)(2,1)S(1)} %get-tuple-element.58), channel_id=1, source_target_pairs={{0,4},{4,0},{8,12},{12,8},{16,20},{20,16},{24,28},{28,24},{1,5},{5... | collective-permute-start | bytes 1572872 | tf_op jit(solution)/shard_map/ppermute | solution.py:230
  10.2 0.8 %latent_share.1 = (bf16[144,512]{1,0:T(8,128)(2,1)S(1)}, bf16[144,512]{1,0:T(8,128)(2,1)S(1)}, bf16[144,512]{1,0:T(8,128)(2,1)S(1)}, bf16[144,512]{1,0:T(8,128)(2,1)S(1)}) custom-call(bf16[576,1024]{1,0:T(8,128)(2,1)S(1)} %get-tuple-element.63.grad_kv, bf16[1024,512]{1,0:T(8,128)(2,1)S(1)} %get-tuple-element.64.wall), custom_call_target="tpu_custom_call" | custom-call | tf_op jit(solution)/shard_map/latent_share/pallas_call | solution.py:283
  11.0 0.7 %collective-permute-done.came = bf16[4,4,32,512]{3,2,1,0:T(8,128)(2,1)S(1)} collective-permute-done((bf16[4,4,32,512]{3,2,1,0:T(8,128)(2,1)S(1)}, bf16[4,4,32,512]{3,2,1,0:T(8,128)(2,1)S(1)}, u32[]{:S(2)}, u32[]{:S(2)}) %collective-permute-start) | collective-permute-done | bytes 524320 | tf_op jit(solution)/shard_map/ppermute | solution.py:230
  11.7 0.1 pair_sum.1
  11.9 2.9 %collective-permute-start.1 = (bf16[4,32,512]{2,1,0:T(8,128)(2,1)S(1)}, bf16[4,32,512]{2,1,0:T(8,128)(2,1)S(1)}, u32[]{:S(2)}, u32[]{:S(2)}) collective-permute-start(bf16[4,32,512]{2,1,0:T(8,128)(2,1)S(1)} %get-tuple-element.70), channel_id=1, source_target_pairs={{0,8},{4,12},{8,0},{12,4},{16,24},{20,28},{24,16},{28,20},{1,9},{5... | collective-permute-start | bytes 393224 | tf_op jit(solution)/shard_map/ppermute | solution.py:237
  14.8 1.5 %collective-permute-start.2 = (bf16[4,32,512]{2,1,0:T(8,128)(2,1)S(1)}, bf16[4,32,512]{2,1,0:T(8,128)(2,1)S(1)}, u32[]{:S(2)}, u32[]{:S(2)}) collective-permute-start(bf16[4,32,512]{2,1,0:T(8,128)(2,1)S(1)} %get-tuple-element.71), channel_id=1, source_target_pairs={{0,16},{4,20},{8,24},{12,28},{16,0},{20,4},{24,8},{28,12},{1,17},{... | collective-permute-start | bytes 393224 | tf_op jit(solution)/shard_map/ppermute | solution.py:237
  16.3 0.0 collective-permute-start.3
  16.3 2.0 %collective-permute-start.11 = (bf16[144,512]{1,0:T(8,128)(2,1)S(1)}, bf16[144,512]{1,0:T(8,128)(2,1)S(1)}, u32[]{:S(2)}, u32[]{:S(2)}) collective-permute-start(bf16[144,512]{1,0:T(8,128)(2,1)S(1)} %get-tuple-element.79), channel_id=1, source_target_pairs={{0,1},{1,2},{2,3},{3,0},{4,5},{5,6},{6,7},{7,4},{8,9},{9,10},{10,1... | collective-permute-start | bytes 442376 | tf_op jit(solution)/shard_map/ppermute | solution.py:240
  18.4 2.6 %collective-permute-start.12 = (bf16[144,512]{1,0:T(8,128)(2,1)S(1)}, bf16[144,512]{1,0:T(8,128)(2,1)S(1)}, u32[]{:S(2)}, u32[]{:S(2)}) collective-permute-start(bf16[144,512]{1,0:T(8,128)(2,1)S(1)} %get-tuple-element.80), channel_id=1, source_target_pairs={{0,2},{1,3},{2,0},{3,1},{4,6},{5,7},{6,4},{7,5},{8,10},{9,11},{10,... | collective-permute-start | bytes 442376 | tf_op jit(solution)/shard_map/ppermute | solution.py:240
  21.0 0.3 ready.1
  21.2 0.0 collective-permute-done.1.refs_1_
  21.2 1.6 %collective-permute-done.2.refs_2_ = bf16[4,32,512]{2,1,0:T(8,128)(2,1)S(1)} collective-permute-done((bf16[4,32,512]{2,1,0:T(8,128)(2,1)S(1)}, bf16[4,32,512]{2,1,0:T(8,128)(2,1)S(1)}, u32[]{:S(2)}, u32[]{:S(2)}) %collective-permute-start.2) | collective-permute-done | bytes 131104 | tf_op jit(solution)/shard_map/ppermute | solution.py:237
  22.9 0.8 %soap.1 = (bf16[32,4,512]{2,1,0:T(4,128)(2,1)S(1)}, f32[32,4,512]{2,1,0:T(4,128)S(1)}, f32[32,4,512]{2,1,0:T(4,128)S(1)}, f32[32,4,512]{2,1,0:T(4,128)S(1)}) custom-call(f32[128,512]{1,0:T(8,128)S(1)} %get-tuple-element.52.before, bf16[512,512]{1,0:T(8,128)(2,1)S(1)} %get-tuple-element.53.turn, f32[128,512]{1,0:T(8,128)S(1)} %get-tuple-element.54.first, ...), custom_call_target="tpu_custom_call" | custom-call | tf_op jit(solution)/shard_map/soap/pallas_call | solution.py:313
  23.7 1.5 %collective-permute-start.6 = (bf16[32,4,512]{2,1,0:T(4,128)(2,1)S(1)}, bf16[32,4,512]{2,1,0:T(4,128)(2,1)S(1)}, u32[]{:S(2)}, u32[]{:S(2)}) collective-permute-start(bf16[32,4,512]{2,1,0:T(4,128)(2,1)S(1)} %get-tuple-element.73.refs_0_), channel_id=1, source_target_pairs={{0,24},{4,28},{8,16},{12,20},{16,8},{20,12},{24,0},{28,4},{1,25},{... | collective-permute-start | bytes 393224 | tf_op jit(solution)/shard_map/ppermute | solution.py:237
  25.2 1.5 %collective-permute-start.4 = (bf16[32,4,512]{2,1,0:T(4,128)(2,1)S(1)}, bf16[32,4,512]{2,1,0:T(4,128)(2,1)S(1)}, u32[]{:S(2)}, u32[]{:S(2)}) collective-permute-start(bf16[32,4,512]{2,1,0:T(4,128)(2,1)S(1)} %get-tuple-element.73.refs_0_), channel_id=1, source_target_pairs={{0,8},{4,12},{8,0},{12,4},{16,24},{20,28},{24,16},{28,20},{1,9},{5... | collective-permute-start | bytes 393224 | tf_op jit(solution)/shard_map/ppermute | solution.py:237
  26.7 0.5 %collective-permute-start.5 = (bf16[32,4,512]{2,1,0:T(4,128)(2,1)S(1)}, bf16[32,4,512]{2,1,0:T(4,128)(2,1)S(1)}, u32[]{:S(2)}, u32[]{:S(2)}) collective-permute-start(bf16[32,4,512]{2,1,0:T(4,128)(2,1)S(1)} %get-tuple-element.73.refs_0_), channel_id=1, source_target_pairs={{0,16},{4,20},{8,24},{12,28},{16,0},{20,4},{24,8},{28,12},{1,17},{... | collective-permute-start | bytes 393224 | tf_op jit(solution)/shard_map/ppermute | solution.py:237
  27.2 3.6 %collective-permute-start.13 = (bf16[144,512]{1,0:T(8,128)(2,1)S(1)}, bf16[144,512]{1,0:T(8,128)(2,1)S(1)}, u32[]{:S(2)}, u32[]{:S(2)}) collective-permute-start(bf16[144,512]{1,0:T(8,128)(2,1)S(1)} %get-tuple-element.81), channel_id=1, source_target_pairs={{0,3},{1,0},{2,1},{3,2},{4,7},{5,4},{6,5},{7,6},{8,11},{9,8},{10,9... | collective-permute-start | bytes 442376 | tf_op jit(solution)/shard_map/ppermute | solution.py:240
  30.8 0.5 %collective-permute-start.10 = (bf16[32,4,512]{2,1,0:T(4,128)(2,1)S(1)}, bf16[32,4,512]{2,1,0:T(4,128)(2,1)S(1)}, u32[]{:S(2)}, u32[]{:S(2)}) collective-permute-start(bf16[32,4,512]{2,1,0:T(4,128)(2,1)S(1)} %collective-permute-done.6.refs_3_), channel_id=1, source_target_pairs={{0,4},{4,0},{8,12},{12,8},{16,20},{20,16},{24,28},{28,24},{1,5},{5... | collective-permute-start | bytes 393224 | tf_op jit(solution)/shard_map/ppermute | solution.py:230
  31.3 0.5 %collective-permute-done.4.refs_1_ = bf16[32,4,512]{2,1,0:T(4,128)(2,1)S(1)} collective-permute-done((bf16[32,4,512]{2,1,0:T(4,128)(2,1)S(1)}, bf16[32,4,512]{2,1,0:T(4,128)(2,1)S(1)}, u32[]{:S(2)}, u32[]{:S(2)}) %collective-permute-start.4) | collective-permute-done | bytes 131104 | tf_op jit(solution)/shard_map/ppermute | solution.py:237
  31.9 0.1 collective-permute-done.5.refs_2_
  32.0 0.5 %collective-permute-start.9 = (bf16[32,4,512]{2,1,0:T(4,128)(2,1)S(1)}, bf16[32,4,512]{2,1,0:T(4,128)(2,1)S(1)}, u32[]{:S(2)}, u32[]{:S(2)}) collective-permute-start(bf16[32,4,512]{2,1,0:T(4,128)(2,1)S(1)} %collective-permute-done.5.refs_2_), channel_id=1, source_target_pairs={{0,4},{4,0},{8,12},{12,8},{16,20},{20,16},{24,28},{28,24},{1,5},{5... | collective-permute-start | bytes 393224 | tf_op jit(solution)/shard_map/ppermute | solution.py:230
  32.4 1.1 %place_own.1 = (bf16[256,4,512]{2,1,0:T(4,128)(2,1)}, f32[32,4,512]{2,1,0:T(4,128)}, f32[32,4,512]{2,1,0:T(4,128)}, f32[32,4,512]{2,1,0:T(4,128)}) custom-call(bf16[32,4,512]{2,1,0:T(4,128)(2,1)S(1)} %get-tuple-element.73.refs_0_, bf16[32,4,512]{2,1,0:T(4,128)(2,1)S(1)} %collective-permute-done.4.refs_1_, ...), custom_call_target="tpu_custom_call" | custom-call | tf_op jit(solution)/shard_map/place_own/pallas_call | solution.py:324
  33.6 0.9 %place_rest.1 = (bf16[256,4,512]{2,1,0:T(4,128)(2,1)}, bf16[144,512]{1,0:T(8,128)(2,1)}) custom-call(bf16[256,4,512]{2,1,0:T(4,128)(2,1)} %get-tuple-element.77.refs_0_, bf16[32,4,512]{2,1,0:T(4,128)(2,1)S(1)} %collective-permute-done.7.refs_1_, bf16[32,4,512]{2,1,0:T(4,128)(2,1)S(1)} %collective-permute-done.8.refs_2_, ...), custom_call_target="tpu_custom_call", output_to_operand_aliasing={{0}: (0, {})} | custom-call | tf_op jit(solution)/shard_map/place_rest/pallas_call | solution.py:333
  (20 shorter events, 0.0 us)
Async XLA Ops:
  9.7 2.1 %collective-permute-start = (bf16[4,4,32,512]{3,2,1,0:T(8,128)(2,1)S(1)}, bf16[4,4,32,512]{3,2,1,0:T(8,128)(2,1)S(1)}, u32[]{:S(2)}, u32[]{:S(2)}) collective-permute-start(bf16[4,4,32,512]{3,2,1,0:T(8,128)(2,1)S(1)} %get-tuple-element.58), channel_id=1, source_target_pairs={{0,4},{4,0},{8,12},{12,8},{16,20},{20,16},{24,28},{28,24},{1,5},{5... | collective-permute-start | bytes 1572872 | tf_op jit(solution)/shard_map/ppermute | solution.py:230
  10.2 10.7 %copy-start = (f32[512,512]{1,0:T(8,128)S(1)}, f32[512,512]{1,0:T(8,128)}, u32[]{:S(2)}) copy-start(f32[512,512]{1,0:T(8,128)} %basis) | copy-start | bytes 3145732
  10.2 10.7 %copy-start.1 = (f32[32,4,512]{2,1,0:T(4,128)S(1)}, f32[32,4,512]{2,1,0:T(4,128)}, u32[]{:S(2)}) copy-start(f32[32,4,512]{2,1,0:T(4,128)} %first_moment) | copy-start | bytes 786436
  10.2 10.7 %copy-start.2 = (f32[32,4,512]{2,1,0:T(4,128)S(1)}, f32[32,4,512]{2,1,0:T(4,128)}, u32[]{:S(2)}) copy-start(f32[32,4,512]{2,1,0:T(4,128)} %second_rot) | copy-start | bytes 786436
  10.2 10.7 %copy-start.3 = (f32[32,4,512]{2,1,0:T(4,128)S(1)}, f32[32,4,512]{2,1,0:T(4,128)}, u32[]{:S(2)}) copy-start(f32[32,4,512]{2,1,0:T(4,128)} %second_plain) | copy-start | bytes 786436
  11.9 9.4 %collective-permute-start.1 = (bf16[4,32,512]{2,1,0:T(8,128)(2,1)S(1)}, bf16[4,32,512]{2,1,0:T(8,128)(2,1)S(1)}, u32[]{:S(2)}, u32[]{:S(2)}) collective-permute-start(bf16[4,32,512]{2,1,0:T(8,128)(2,1)S(1)} %get-tuple-element.70), channel_id=1, source_target_pairs={{0,8},{4,12},{8,0},{12,4},{16,24},{20,28},{24,16},{28,20},{1,9},{5... | collective-permute-start | bytes 393224 | tf_op jit(solution)/shard_map/ppermute | solution.py:237
  14.8 8.1 %collective-permute-start.2 = (bf16[4,32,512]{2,1,0:T(8,128)(2,1)S(1)}, bf16[4,32,512]{2,1,0:T(8,128)(2,1)S(1)}, u32[]{:S(2)}, u32[]{:S(2)}) collective-permute-start(bf16[4,32,512]{2,1,0:T(8,128)(2,1)S(1)} %get-tuple-element.71), channel_id=1, source_target_pairs={{0,16},{4,20},{8,24},{12,28},{16,0},{20,4},{24,8},{28,12},{1,17},{... | collective-permute-start | bytes 393224 | tf_op jit(solution)/shard_map/ppermute | solution.py:237
  16.3 6.6 %collective-permute-start.3 = (bf16[4,32,512]{2,1,0:T(8,128)(2,1)S(1)}, bf16[4,32,512]{2,1,0:T(8,128)(2,1)S(1)}, u32[]{:S(2)}, u32[]{:S(2)}) collective-permute-start(bf16[4,32,512]{2,1,0:T(8,128)(2,1)S(1)} %get-tuple-element.72), channel_id=1, source_target_pairs={{0,24},{4,28},{8,16},{12,20},{16,8},{20,12},{24,0},{28,4},{1,25},{... | collective-permute-start | bytes 393224 | tf_op jit(solution)/shard_map/ppermute | solution.py:237
  16.3 10.9 %collective-permute-start.11 = (bf16[144,512]{1,0:T(8,128)(2,1)S(1)}, bf16[144,512]{1,0:T(8,128)(2,1)S(1)}, u32[]{:S(2)}, u32[]{:S(2)}) collective-permute-start(bf16[144,512]{1,0:T(8,128)(2,1)S(1)} %get-tuple-element.79), channel_id=1, source_target_pairs={{0,1},{1,2},{2,3},{3,0},{4,5},{5,6},{6,7},{7,4},{8,9},{9,10},{10,1... | collective-permute-start | bytes 442376 | tf_op jit(solution)/shard_map/ppermute | solution.py:240
  18.4 12.5 %collective-permute-start.12 = (bf16[144,512]{1,0:T(8,128)(2,1)S(1)}, bf16[144,512]{1,0:T(8,128)(2,1)S(1)}, u32[]{:S(2)}, u32[]{:S(2)}) collective-permute-start(bf16[144,512]{1,0:T(8,128)(2,1)S(1)} %get-tuple-element.80), channel_id=1, source_target_pairs={{0,2},{1,3},{2,0},{3,1},{4,6},{5,7},{6,4},{7,5},{8,10},{9,11},{10,... | collective-permute-start | bytes 442376 | tf_op jit(solution)/shard_map/ppermute | solution.py:240
  23.7 7.2 %collective-permute-start.6 = (bf16[32,4,512]{2,1,0:T(4,128)(2,1)S(1)}, bf16[32,4,512]{2,1,0:T(4,128)(2,1)S(1)}, u32[]{:S(2)}, u32[]{:S(2)}) collective-permute-start(bf16[32,4,512]{2,1,0:T(4,128)(2,1)S(1)} %get-tuple-element.73.refs_0_), channel_id=1, source_target_pairs={{0,24},{4,28},{8,16},{12,20},{16,8},{20,12},{24,0},{28,4},{1,25},{... | collective-permute-start | bytes 393224 | tf_op jit(solution)/shard_map/ppermute | solution.py:237
  25.2 6.7 %collective-permute-start.4 = (bf16[32,4,512]{2,1,0:T(4,128)(2,1)S(1)}, bf16[32,4,512]{2,1,0:T(4,128)(2,1)S(1)}, u32[]{:S(2)}, u32[]{:S(2)}) collective-permute-start(bf16[32,4,512]{2,1,0:T(4,128)(2,1)S(1)} %get-tuple-element.73.refs_0_), channel_id=1, source_target_pairs={{0,8},{4,12},{8,0},{12,4},{16,24},{20,28},{24,16},{28,20},{1,9},{5... | collective-permute-start | bytes 393224 | tf_op jit(solution)/shard_map/ppermute | solution.py:237
  26.7 5.2 %collective-permute-start.5 = (bf16[32,4,512]{2,1,0:T(4,128)(2,1)S(1)}, bf16[32,4,512]{2,1,0:T(4,128)(2,1)S(1)}, u32[]{:S(2)}, u32[]{:S(2)}) collective-permute-start(bf16[32,4,512]{2,1,0:T(4,128)(2,1)S(1)} %get-tuple-element.73.refs_0_), channel_id=1, source_target_pairs={{0,16},{4,20},{8,24},{12,28},{16,0},{20,4},{24,8},{28,12},{1,17},{... | collective-permute-start | bytes 393224 | tf_op jit(solution)/shard_map/ppermute | solution.py:237
  27.2 6.3 %collective-permute-start.13 = (bf16[144,512]{1,0:T(8,128)(2,1)S(1)}, bf16[144,512]{1,0:T(8,128)(2,1)S(1)}, u32[]{:S(2)}, u32[]{:S(2)}) collective-permute-start(bf16[144,512]{1,0:T(8,128)(2,1)S(1)} %get-tuple-element.81), channel_id=1, source_target_pairs={{0,3},{1,0},{2,1},{3,2},{4,7},{5,4},{6,5},{7,6},{8,11},{9,8},{10,9... | collective-permute-start | bytes 442376 | tf_op jit(solution)/shard_map/ppermute | solution.py:240
  30.8 2.7 %collective-permute-start.7 = (bf16[32,4,512]{2,1,0:T(4,128)(2,1)S(1)}, bf16[32,4,512]{2,1,0:T(4,128)(2,1)S(1)}, u32[]{:S(2)}, u32[]{:S(2)}) collective-permute-start(bf16[32,4,512]{2,1,0:T(4,128)(2,1)S(1)} %get-tuple-element.73.refs_0_), channel_id=1, source_target_pairs={{0,4},{4,0},{8,12},{12,8},{16,20},{20,16},{24,28},{28,24},{1,5},{5... | collective-permute-start | bytes 393224 | tf_op jit(solution)/shard_map/ppermute | solution.py:230
  30.8 2.7 %collective-permute-start.10 = (bf16[32,4,512]{2,1,0:T(4,128)(2,1)S(1)}, bf16[32,4,512]{2,1,0:T(4,128)(2,1)S(1)}, u32[]{:S(2)}, u32[]{:S(2)}) collective-permute-start(bf16[32,4,512]{2,1,0:T(4,128)(2,1)S(1)} %collective-permute-done.6.refs_3_), channel_id=1, source_target_pairs={{0,4},{4,0},{8,12},{12,8},{16,20},{20,16},{24,28},{28,24},{1,5},{5... | collective-permute-start | bytes 393224 | tf_op jit(solution)/shard_map/ppermute | solution.py:230
  31.9 1.7 %collective-permute-start.8 = (bf16[32,4,512]{2,1,0:T(4,128)(2,1)S(1)}, bf16[32,4,512]{2,1,0:T(4,128)(2,1)S(1)}, u32[]{:S(2)}, u32[]{:S(2)}) collective-permute-start(bf16[32,4,512]{2,1,0:T(4,128)(2,1)S(1)} %collective-permute-done.4.refs_1_), channel_id=1, source_target_pairs={{0,4},{4,0},{8,12},{12,8},{16,20},{20,16},{24,28},{28,24},{1,5},{5... | collective-permute-start | bytes 393224 | tf_op jit(solution)/shard_map/ppermute | solution.py:230
  32.0 1.6 %collective-permute-start.9 = (bf16[32,4,512]{2,1,0:T(4,128)(2,1)S(1)}, bf16[32,4,512]{2,1,0:T(4,128)(2,1)S(1)}, u32[]{:S(2)}, u32[]{:S(2)}) collective-permute-start(bf16[32,4,512]{2,1,0:T(4,128)(2,1)S(1)} %collective-permute-done.5.refs_2_), channel_id=1, source_target_pairs={{0,4},{4,0},{8,12},{12,8},{16,20},{20,16},{24,28},{28,24},{1,5},{5... | collective-permute-start | bytes 393224 | tf_op jit(solution)/shard_map/ppermute | solution.py:230

commit v5 on v4

--- a/solution.py
+++ b/solution.py
@@ -68,7 +68,6 @@
     k_side_v,
     g_out_v,
     weight_v,
-    key_value,
     bias,
     slab,
     sems,
@@ -98,16 +97,17 @@
     copies[0].wait()
     wall[...] = jnp.swapaxes(weight_v[...], 0, 1).reshape(heads * width, latent_dim)
     copies[1].wait()
-    key_value[...] = mm_nt(lat[...], wall[...]).astype(bf16)
+    kv_all = mm_nt(lat[...], wall[...]).astype(bf16)
     for copy in copies[2:6]:
         copy.wait()
     k_side = k_side_v[...].T
+    found = []
     for h in range(heads):
         q_main = q_main_v[:, h * head_dim : (h + 1) * head_dim]
         g_out = g_out_v[:, h * head_dim : (h + 1) * head_dim]
         q_all = jnp.concatenate([q_main, q_side_v[:, h * rope_dim : (h + 1) * rope_dim]], axis=1)
-        keys = key_value[:, h * width : h * width + head_dim]
-        values = key_value[:, h * width + head_dim : (h + 1) * width]
+        keys = kv_all[:, h * width : h * width + head_dim]
+        values = kv_all[:, h * width + head_dim : (h + 1) * width]
         k_all = jnp.concatenate([keys, k_side], axis=1)
         scores = mm_nt(k_all, q_all) + bias[...]
         top = jnp.max(scores, axis=0, keepdims=True)
@@ -117,7 +117,7 @@
         probs_low = probs.astype(bf16)
         grad_probs = mm_nt(values, g_out)
         delta = jnp.sum(probs * grad_probs, axis=0, keepdims=True)
-        grad_scores = (probs * (grad_probs - delta) * scale).astype(bf16)
+        grad_scores = (probs * (grad_probs - delta)).astype(bf16)
         lhs = jnp.concatenate([grad_scores, zeros[:, : -seq_len % 128], probs_low], axis=1)
         rhs = jnp.concatenate(
             [
@@ -127,14 +127,17 @@
             ],
             axis=0,
         )
-        grad_kv[:, h * width : (h + 1) * width] = mm(lhs, rhs).astype(bf16)
-    slab[...] = mm_tn(grad_kv[...], lat[...]).reshape(heads, 2 * chips, rows, latent_dim)
+        pair = mm(lhs, rhs)
+        found.append(jnp.concatenate([pair[:, :head_dim] * scale, pair[:, head_dim:]], axis=1).astype(bf16))
+    found = jnp.concatenate(found, axis=1)
+    grad_kv[...] = found
+    slab[...] = mm_tn(found, lat[...]).reshape(heads, 2 * chips, rows, latent_dim).astype(bf16)
     my_chip, my_core = place_of()
     for k in range(chips):
         chip = other_chip(my_chip, k, chips)
         for h in range(heads):
-            send[k, h] = slab[h, 2 * chip + 1 - my_core].astype(bf16)
-            keep[k, h] = slab[h, 2 * chip + my_core].astype(bf16)
+            send[k, h] = slab[h, 2 * chip + 1 - my_core]
+            keep[k, h] = slab[h, 2 * chip + my_core]
     own_weight[...] = weight_v[pl.ds((2 * my_chip + my_core) * rows, rows)]
 
 
@@ -259,9 +262,8 @@
             pltpu.VMEM((rope_dim, seq_len), bf16),
             pltpu.VMEM(grad_out.shape, bf16),
             pltpu.VMEM(weight.shape, bf16),
-            pltpu.VMEM((seq_len, heads * width), bf16),
             pltpu.VMEM((seq_len, seq_len), f32),
-            pltpu.VMEM((heads, dp, rows, latent_dim), f32),
+            pltpu.VMEM((heads, dp, rows, latent_dim), bf16),
             pltpu.SemaphoreType.DMA((6,)),
         ],
         compiler_params=limit_mib(32),

time: 34.6 us -> 34.3 us (level)
  no operation moved by 1% of the time
where the time goes in v5:
time: 34.3 us; the launch traced here: 34.2 us
  starting transfers between devices  17.7 us (52%)
  Pallas kernels  12.1 us (35%)
  waiting for transfers between devices  2.95 us (9%)
  between operations  1.39 us (4%)
    ppermute x3, starting transfers between devices, part_move(): lax.ppermute(x, 'tensor', [(i, (i + s) % parts) for i in range(parts)])  8.22 us
    pallas_call x1, Pallas kernels, local(): pl.pallas_call(attend_kernel, out_shape=(pltpu.VMEM((chips,) + piece, bf1...  8.08 us
    ppermute x6, starting transfers between devices, chip_move(): return lax.ppermute(x, 'dp', pairs)  8.02 us
    ppermute x6, waiting for transfers between devices, chip_move(): return lax.ppermute(x, 'dp', pairs)  2.22 us
    ppermute x5, starting transfers between devices, core_swap(): return lax.ppermute(x, 'dp', [(i, i ^ 1) for i in range(dp)])  1.49 us
    pallas_call x1, Pallas kernels, local(): pl.pallas_call(functools.partial(place_own_kernel, chips), out_shape=(plt...  1.11 us
    pallas_call x1, Pallas kernels, local(): pl.pallas_call(functools.partial(place_rest_kernel, chips), out_shape=(pl...  0.9 us
    pallas_call x1, Pallas kernels, local(): pl.pallas_call(latent_kernel, out_shape=[pltpu.VMEM((part_rows, latent_di...  0.81 us
  transfers between devices with their start and end apart: 14, of which 4 were waited for; matrix products, arithmetic and copies ran while one was open for 0% of the time, Pallas kernels for 9%

profile of v5, /device:TPU:0, one launch (start us, length us, event | category | flops | bytes accessed | tf_op | source)
XLA Modules:
  0.0 34.2 jit_solution(14937504042669410584)
XLA Ops:
  1.3 8.1 %attend.1 = (bf16[4,4,32,512]{3,2,1,0:T(8,128)(2,1)S(1)}, bf16[4,4,32,512]{3,2,1,0:T(8,128)(2,1)S(1)}, bf16[576,1024]{1,0:T(8,128)(2,1)S(1)}, bf16[1024,512]{1,0:T(8,128)(2,1)S(1)}, bf16[32,4,512]{2,1,0:T(4,128)(2,1)S(1)}) custom-call(s32[8,128]{1,0:T(8,128)S(1)} %broadcast_in_dim.2.offsets, bf16[576,512]{1,0:T(8,128)(2,1)} %latent.1, ...), custom_call_target="tpu_custom_call" | custom-call | flops 3623878656 | bytes 33554432 | tf_op jit(solution)/shard_map/attend/pallas_call | solution.py:247
  9.4 0.5 %collective-permute-start = (bf16[4,4,32,512]{3,2,1,0:T(8,128)(2,1)S(1)}, bf16[4,4,32,512]{3,2,1,0:T(8,128)(2,1)S(1)}, u32[]{:S(2)}, u32[]{:S(2)}) collective-permute-start(bf16[4,4,32,512]{3,2,1,0:T(8,128)(2,1)S(1)} %get-tuple-element.58), channel_id=1, source_target_pairs={{0,4},{4,0},{8,12},{12,8},{16,20},{20,16},{24,28},{28,24},{1,5},{5... | collective-permute-start | bytes 1572872 | tf_op jit(solution)/shard_map/ppermute | solution.py:233
  9.9 0.8 %latent_share.1 = (bf16[144,512]{1,0:T(8,128)(2,1)S(1)}, bf16[144,512]{1,0:T(8,128)(2,1)S(1)}, bf16[144,512]{1,0:T(8,128)(2,1)S(1)}, bf16[144,512]{1,0:T(8,128)(2,1)S(1)}) custom-call(bf16[576,1024]{1,0:T(8,128)(2,1)S(1)} %get-tuple-element.63.grad_kv, bf16[1024,512]{1,0:T(8,128)(2,1)S(1)} %get-tuple-element.64.wall), custom_call_target="tpu_custom_call" | custom-call | tf_op jit(solution)/shard_map/latent_share/pallas_call | solution.py:285
  10.7 0.7 %collective-permute-done.came = bf16[4,4,32,512]{3,2,1,0:T(8,128)(2,1)S(1)} collective-permute-done((bf16[4,4,32,512]{3,2,1,0:T(8,128)(2,1)S(1)}, bf16[4,4,32,512]{3,2,1,0:T(8,128)(2,1)S(1)}, u32[]{:S(2)}, u32[]{:S(2)}) %collective-permute-start) | collective-permute-done | bytes 524320 | tf_op jit(solution)/shard_map/ppermute | solution.py:233
  11.4 0.1 pair_sum.1
  11.6 2.9 %collective-permute-start.1 = (bf16[4,32,512]{2,1,0:T(8,128)(2,1)S(1)}, bf16[4,32,512]{2,1,0:T(8,128)(2,1)S(1)}, u32[]{:S(2)}, u32[]{:S(2)}) collective-permute-start(bf16[4,32,512]{2,1,0:T(8,128)(2,1)S(1)} %get-tuple-element.70), channel_id=1, source_target_pairs={{0,8},{4,12},{8,0},{12,4},{16,24},{20,28},{24,16},{28,20},{1,9},{5... | collective-permute-start | bytes 393224 | tf_op jit(solution)/shard_map/ppermute | solution.py:240
  14.5 1.5 %collective-permute-start.2 = (bf16[4,32,512]{2,1,0:T(8,128)(2,1)S(1)}, bf16[4,32,512]{2,1,0:T(8,128)(2,1)S(1)}, u32[]{:S(2)}, u32[]{:S(2)}) collective-permute-start(bf16[4,32,512]{2,1,0:T(8,128)(2,1)S(1)} %get-tuple-element.71), channel_id=1, source_target_pairs={{0,16},{4,20},{8,24},{12,28},{16,0},{20,4},{24,8},{28,12},{1,17},{... | collective-permute-start | bytes 393224 | tf_op jit(solution)/shard_map/ppermute | solution.py:240
  16.0 0.0 collective-permute-start.3
  16.0 2.0 %collective-permute-start.11 = (bf16[144,512]{1,0:T(8,128)(2,1)S(1)}, bf16[144,512]{1,0:T(8,128)(2,1)S(1)}, u32[]{:S(2)}, u32[]{:S(2)}) collective-permute-start(bf16[144,512]{1,0:T(8,128)(2,1)S(1)} %get-tuple-element.79), channel_id=1, source_target_pairs={{0,1},{1,2},{2,3},{3,0},{4,5},{5,6},{6,7},{7,4},{8,9},{9,10},{10,1... | collective-permute-start | bytes 442376 | tf_op jit(solution)/shard_map/ppermute | solution.py:243
  18.1 2.6 %collective-permute-start.12 = (bf16[144,512]{1,0:T(8,128)(2,1)S(1)}, bf16[144,512]{1,0:T(8,128)(2,1)S(1)}, u32[]{:S(2)}, u32[]{:S(2)}) collective-permute-start(bf16[144,512]{1,0:T(8,128)(2,1)S(1)} %get-tuple-element.80), channel_id=1, source_target_pairs={{0,2},{1,3},{2,0},{3,1},{4,6},{5,7},{6,4},{7,5},{8,10},{9,11},{10,... | collective-permute-start | bytes 442376 | tf_op jit(solution)/shard_map/ppermute | solution.py:243
  20.7 0.3 ready.1
  20.9 0.0 collective-permute-done.1.refs_1_
  20.9 1.6 %collective-permute-done.2.refs_2_ = bf16[4,32,512]{2,1,0:T(8,128)(2,1)S(1)} collective-permute-done((bf16[4,32,512]{2,1,0:T(8,128)(2,1)S(1)}, bf16[4,32,512]{2,1,0:T(8,128)(2,1)S(1)}, u32[]{:S(2)}, u32[]{:S(2)}) %collective-permute-start.2) | collective-permute-done | bytes 131104 | tf_op jit(solution)/shard_map/ppermute | solution.py:240
  22.6 0.8 %soap.1 = (bf16[32,4,512]{2,1,0:T(4,128)(2,1)S(1)}, f32[32,4,512]{2,1,0:T(4,128)S(1)}, f32[32,4,512]{2,1,0:T(4,128)S(1)}, f32[32,4,512]{2,1,0:T(4,128)S(1)}) custom-call(f32[128,512]{1,0:T(8,128)S(1)} %get-tuple-element.52.before, bf16[512,512]{1,0:T(8,128)(2,1)S(1)} %get-tuple-element.53.turn, f32[128,512]{1,0:T(8,128)S(1)} %get-tuple-element.54.first, ...), custom_call_target="tpu_custom_call" | custom-call | tf_op jit(solution)/shard_map/soap/pallas_call | solution.py:315
  23.4 1.5 %collective-permute-start.6 = (bf16[32,4,512]{2,1,0:T(4,128)(2,1)S(1)}, bf16[32,4,512]{2,1,0:T(4,128)(2,1)S(1)}, u32[]{:S(2)}, u32[]{:S(2)}) collective-permute-start(bf16[32,4,512]{2,1,0:T(4,128)(2,1)S(1)} %get-tuple-element.73.refs_0_), channel_id=1, source_target_pairs={{0,24},{4,28},{8,16},{12,20},{16,8},{20,12},{24,0},{28,4},{1,25},{... | collective-permute-start | bytes 393224 | tf_op jit(solution)/shard_map/ppermute | solution.py:240
  24.9 1.5 %collective-permute-start.4 = (bf16[32,4,512]{2,1,0:T(4,128)(2,1)S(1)}, bf16[32,4,512]{2,1,0:T(4,128)(2,1)S(1)}, u32[]{:S(2)}, u32[]{:S(2)}) collective-permute-start(bf16[32,4,512]{2,1,0:T(4,128)(2,1)S(1)} %get-tuple-element.73.refs_0_), channel_id=1, source_target_pairs={{0,8},{4,12},{8,0},{12,4},{16,24},{20,28},{24,16},{28,20},{1,9},{5... | collective-permute-start | bytes 393224 | tf_op jit(solution)/shard_map/ppermute | solution.py:240
  26.4 0.5 %collective-permute-start.5 = (bf16[32,4,512]{2,1,0:T(4,128)(2,1)S(1)}, bf16[32,4,512]{2,1,0:T(4,128)(2,1)S(1)}, u32[]{:S(2)}, u32[]{:S(2)}) collective-permute-start(bf16[32,4,512]{2,1,0:T(4,128)(2,1)S(1)} %get-tuple-element.73.refs_0_), channel_id=1, source_target_pairs={{0,16},{4,20},{8,24},{12,28},{16,0},{20,4},{24,8},{28,12},{1,17},{... | collective-permute-start | bytes 393224 | tf_op jit(solution)/shard_map/ppermute | solution.py:240
  26.9 3.6 %collective-permute-start.13 = (bf16[144,512]{1,0:T(8,128)(2,1)S(1)}, bf16[144,512]{1,0:T(8,128)(2,1)S(1)}, u32[]{:S(2)}, u32[]{:S(2)}) collective-permute-start(bf16[144,512]{1,0:T(8,128)(2,1)S(1)} %get-tuple-element.81), channel_id=1, source_target_pairs={{0,3},{1,0},{2,1},{3,2},{4,7},{5,4},{6,5},{7,6},{8,11},{9,8},{10,9... | collective-permute-start | bytes 442376 | tf_op jit(solution)/shard_map/ppermute | solution.py:243
  30.5 0.5 %collective-permute-start.10 = (bf16[32,4,512]{2,1,0:T(4,128)(2,1)S(1)}, bf16[32,4,512]{2,1,0:T(4,128)(2,1)S(1)}, u32[]{:S(2)}, u32[]{:S(2)}) collective-permute-start(bf16[32,4,512]{2,1,0:T(4,128)(2,1)S(1)} %collective-permute-done.6.refs_3_), channel_id=1, source_target_pairs={{0,4},{4,0},{8,12},{12,8},{16,20},{20,16},{24,28},{28,24},{1,5},{5... | collective-permute-start | bytes 393224 | tf_op jit(solution)/shard_map/ppermute | solution.py:233
  31.0 0.5 %collective-permute-done.4.refs_1_ = bf16[32,4,512]{2,1,0:T(4,128)(2,1)S(1)} collective-permute-done((bf16[32,4,512]{2,1,0:T(4,128)(2,1)S(1)}, bf16[32,4,512]{2,1,0:T(4,128)(2,1)S(1)}, u32[]{:S(2)}, u32[]{:S(2)}) %collective-permute-start.4) | collective-permute-done | bytes 131104 | tf_op jit(solution)/shard_map/ppermute | solution.py:240
  31.6 0.1 collective-permute-done.5.refs_2_
  31.6 0.5 %collective-permute-start.9 = (bf16[32,4,512]{2,1,0:T(4,128)(2,1)S(1)}, bf16[32,4,512]{2,1,0:T(4,128)(2,1)S(1)}, u32[]{:S(2)}, u32[]{:S(2)}) collective-permute-start(bf16[32,4,512]{2,1,0:T(4,128)(2,1)S(1)} %collective-permute-done.5.refs_2_), channel_id=1, source_target_pairs={{0,4},{4,0},{8,12},{12,8},{16,20},{20,16},{24,28},{28,24},{1,5},{5... | collective-permute-start | bytes 393224 | tf_op jit(solution)/shard_map/ppermute | solution.py:233
  32.1 1.1 %place_own.1 = (bf16[256,4,512]{2,1,0:T(4,128)(2,1)}, f32[32,4,512]{2,1,0:T(4,128)}, f32[32,4,512]{2,1,0:T(4,128)}, f32[32,4,512]{2,1,0:T(4,128)}) custom-call(bf16[32,4,512]{2,1,0:T(4,128)(2,1)S(1)} %get-tuple-element.73.refs_0_, bf16[32,4,512]{2,1,0:T(4,128)(2,1)S(1)} %collective-permute-done.4.refs_1_, ...), custom_call_target="tpu_custom_call" | custom-call | tf_op jit(solution)/shard_map/place_own/pallas_call | solution.py:326
  33.3 0.9 %place_rest.1 = (bf16[256,4,512]{2,1,0:T(4,128)(2,1)}, bf16[144,512]{1,0:T(8,128)(2,1)}) custom-call(bf16[256,4,512]{2,1,0:T(4,128)(2,1)} %get-tuple-element.77.refs_0_, bf16[32,4,512]{2,1,0:T(4,128)(2,1)S(1)} %collective-permute-done.7.refs_1_, bf16[32,4,512]{2,1,0:T(4,128)(2,1)S(1)} %collective-permute-done.8.refs_2_, ...), custom_call_target="tpu_custom_call", output_to_operand_aliasing={{0}: (0, {})} | custom-call | tf_op jit(solution)/shard_map/place_rest/pallas_call | solution.py:335
  (20 shorter events, 0.0 us)
Async XLA Ops:
  9.4 2.1 %collective-permute-start = (bf16[4,4,32,512]{3,2,1,0:T(8,128)(2,1)S(1)}, bf16[4,4,32,512]{3,2,1,0:T(8,128)(2,1)S(1)}, u32[]{:S(2)}, u32[]{:S(2)}) collective-permute-start(bf16[4,4,32,512]{3,2,1,0:T(8,128)(2,1)S(1)} %get-tuple-element.58), channel_id=1, source_target_pairs={{0,4},{4,0},{8,12},{12,8},{16,20},{20,16},{24,28},{28,24},{1,5},{5... | collective-permute-start | bytes 1572872 | tf_op jit(solution)/shard_map/ppermute | solution.py:233
  9.9 10.7 %copy-start = (f32[512,512]{1,0:T(8,128)S(1)}, f32[512,512]{1,0:T(8,128)}, u32[]{:S(2)}) copy-start(f32[512,512]{1,0:T(8,128)} %basis) | copy-start | bytes 3145732
  9.9 10.7 %copy-start.1 = (f32[32,4,512]{2,1,0:T(4,128)S(1)}, f32[32,4,512]{2,1,0:T(4,128)}, u32[]{:S(2)}) copy-start(f32[32,4,512]{2,1,0:T(4,128)} %first_moment) | copy-start | bytes 786436
  9.9 10.7 %copy-start.2 = (f32[32,4,512]{2,1,0:T(4,128)S(1)}, f32[32,4,512]{2,1,0:T(4,128)}, u32[]{:S(2)}) copy-start(f32[32,4,512]{2,1,0:T(4,128)} %second_rot) | copy-start | bytes 786436
  9.9 10.7 %copy-start.3 = (f32[32,4,512]{2,1,0:T(4,128)S(1)}, f32[32,4,512]{2,1,0:T(4,128)}, u32[]{:S(2)}) copy-start(f32[32,4,512]{2,1,0:T(4,128)} %second_plain) | copy-start | bytes 786436
  11.6 9.4 %collective-permute-start.1 = (bf16[4,32,512]{2,1,0:T(8,128)(2,1)S(1)}, bf16[4,32,512]{2,1,0:T(8,128)(2,1)S(1)}, u32[]{:S(2)}, u32[]{:S(2)}) collective-permute-start(bf16[4,32,512]{2,1,0:T(8,128)(2,1)S(1)} %get-tuple-element.70), channel_id=1, source_target_pairs={{0,8},{4,12},{8,0},{12,4},{16,24},{20,28},{24,16},{28,20},{1,9},{5... | collective-permute-start | bytes 393224 | tf_op jit(solution)/shard_map/ppermute | solution.py:240
  14.5 8.1 %collective-permute-start.2 = (bf16[4,32,512]{2,1,0:T(8,128)(2,1)S(1)}, bf16[4,32,512]{2,1,0:T(8,128)(2,1)S(1)}, u32[]{:S(2)}, u32[]{:S(2)}) collective-permute-start(bf16[4,32,512]{2,1,0:T(8,128)(2,1)S(1)} %get-tuple-element.71), channel_id=1, source_target_pairs={{0,16},{4,20},{8,24},{12,28},{16,0},{20,4},{24,8},{28,12},{1,17},{... | collective-permute-start | bytes 393224 | tf_op jit(solution)/shard_map/ppermute | solution.py:240
  16.0 6.6 %collective-permute-start.3 = (bf16[4,32,512]{2,1,0:T(8,128)(2,1)S(1)}, bf16[4,32,512]{2,1,0:T(8,128)(2,1)S(1)}, u32[]{:S(2)}, u32[]{:S(2)}) collective-permute-start(bf16[4,32,512]{2,1,0:T(8,128)(2,1)S(1)} %get-tuple-element.72), channel_id=1, source_target_pairs={{0,24},{4,28},{8,16},{12,20},{16,8},{20,12},{24,0},{28,4},{1,25},{... | collective-permute-start | bytes 393224 | tf_op jit(solution)/shard_map/ppermute | solution.py:240
  16.0 10.9 %collective-permute-start.11 = (bf16[144,512]{1,0:T(8,128)(2,1)S(1)}, bf16[144,512]{1,0:T(8,128)(2,1)S(1)}, u32[]{:S(2)}, u32[]{:S(2)}) collective-permute-start(bf16[144,512]{1,0:T(8,128)(2,1)S(1)} %get-tuple-element.79), channel_id=1, source_target_pairs={{0,1},{1,2},{2,3},{3,0},{4,5},{5,6},{6,7},{7,4},{8,9},{9,10},{10,1... | collective-permute-start | bytes 442376 | tf_op jit(solution)/shard_map/ppermute | solution.py:243
  18.1 12.5 %collective-permute-start.12 = (bf16[144,512]{1,0:T(8,128)(2,1)S(1)}, bf16[144,512]{1,0:T(8,128)(2,1)S(1)}, u32[]{:S(2)}, u32[]{:S(2)}) collective-permute-start(bf16[144,512]{1,0:T(8,128)(2,1)S(1)} %get-tuple-element.80), channel_id=1, source_target_pairs={{0,2},{1,3},{2,0},{3,1},{4,6},{5,7},{6,4},{7,5},{8,10},{9,11},{10,... | collective-permute-start | bytes 442376 | tf_op jit(solution)/shard_map/ppermute | solution.py:243
  23.4 7.2 %collective-permute-start.6 = (bf16[32,4,512]{2,1,0:T(4,128)(2,1)S(1)}, bf16[32,4,512]{2,1,0:T(4,128)(2,1)S(1)}, u32[]{:S(2)}, u32[]{:S(2)}) collective-permute-start(bf16[32,4,512]{2,1,0:T(4,128)(2,1)S(1)} %get-tuple-element.73.refs_0_), channel_id=1, source_target_pairs={{0,24},{4,28},{8,16},{12,20},{16,8},{20,12},{24,0},{28,4},{1,25},{... | collective-permute-start | bytes 393224 | tf_op jit(solution)/shard_map/ppermute | solution.py:240
  24.9 6.7 %collective-permute-start.4 = (bf16[32,4,512]{2,1,0:T(4,128)(2,1)S(1)}, bf16[32,4,512]{2,1,0:T(4,128)(2,1)S(1)}, u32[]{:S(2)}, u32[]{:S(2)}) collective-permute-start(bf16[32,4,512]{2,1,0:T(4,128)(2,1)S(1)} %get-tuple-element.73.refs_0_), channel_id=1, source_target_pairs={{0,8},{4,12},{8,0},{12,4},{16,24},{20,28},{24,16},{28,20},{1,9},{5... | collective-permute-start | bytes 393224 | tf_op jit(solution)/shard_map/ppermute | solution.py:240
  26.4 5.2 %collective-permute-start.5 = (bf16[32,4,512]{2,1,0:T(4,128)(2,1)S(1)}, bf16[32,4,512]{2,1,0:T(4,128)(2,1)S(1)}, u32[]{:S(2)}, u32[]{:S(2)}) collective-permute-start(bf16[32,4,512]{2,1,0:T(4,128)(2,1)S(1)} %get-tuple-element.73.refs_0_), channel_id=1, source_target_pairs={{0,16},{4,20},{8,24},{12,28},{16,0},{20,4},{24,8},{28,12},{1,17},{... | collective-permute-start | bytes 393224 | tf_op jit(solution)/shard_map/ppermute | solution.py:240
  26.9 6.3 %collective-permute-start.13 = (bf16[144,512]{1,0:T(8,128)(2,1)S(1)}, bf16[144,512]{1,0:T(8,128)(2,1)S(1)}, u32[]{:S(2)}, u32[]{:S(2)}) collective-permute-start(bf16[144,512]{1,0:T(8,128)(2,1)S(1)} %get-tuple-element.81), channel_id=1, source_target_pairs={{0,3},{1,0},{2,1},{3,2},{4,7},{5,4},{6,5},{7,6},{8,11},{9,8},{10,9... | collective-permute-start | bytes 442376 | tf_op jit(solution)/shard_map/ppermute | solution.py:243
  30.5 2.7 %collective-permute-start.7 = (bf16[32,4,512]{2,1,0:T(4,128)(2,1)S(1)}, bf16[32,4,512]{2,1,0:T(4,128)(2,1)S(1)}, u32[]{:S(2)}, u32[]{:S(2)}) collective-permute-start(bf16[32,4,512]{2,1,0:T(4,128)(2,1)S(1)} %get-tuple-element.73.refs_0_), channel_id=1, source_target_pairs={{0,4},{4,0},{8,12},{12,8},{16,20},{20,16},{24,28},{28,24},{1,5},{5... | collective-permute-start | bytes 393224 | tf_op jit(solution)/shard_map/ppermute | solution.py:233
  30.5 2.7 %collective-permute-start.10 = (bf16[32,4,512]{2,1,0:T(4,128)(2,1)S(1)}, bf16[32,4,512]{2,1,0:T(4,128)(2,1)S(1)}, u32[]{:S(2)}, u32[]{:S(2)}) collective-permute-start(bf16[32,4,512]{2,1,0:T(4,128)(2,1)S(1)} %collective-permute-done.6.refs_3_), channel_id=1, source_target_pairs={{0,4},{4,0},{8,12},{12,8},{16,20},{20,16},{24,28},{28,24},{1,5},{5... | collective-permute-start | bytes 393224 | tf_op jit(solution)/shard_map/ppermute | solution.py:233
  31.6 1.7 %collective-permute-start.8 = (bf16[32,4,512]{2,1,0:T(4,128)(2,1)S(1)}, bf16[32,4,512]{2,1,0:T(4,128)(2,1)S(1)}, u32[]{:S(2)}, u32[]{:S(2)}) collective-permute-start(bf16[32,4,512]{2,1,0:T(4,128)(2,1)S(1)} %collective-permute-done.4.refs_1_), channel_id=1, source_target_pairs={{0,4},{4,0},{8,12},{12,8},{16,20},{20,16},{24,28},{28,24},{1,5},{5... | collective-permute-start | bytes 393224 | tf_op jit(solution)/shard_map/ppermute | solution.py:233
  31.6 1.6 %collective-permute-start.9 = (bf16[32,4,512]{2,1,0:T(4,128)(2,1)S(1)}, bf16[32,4,512]{2,1,0:T(4,128)(2,1)S(1)}, u32[]{:S(2)}, u32[]{:S(2)}) collective-permute-start(bf16[32,4,512]{2,1,0:T(4,128)(2,1)S(1)} %collective-permute-done.5.refs_2_), channel_id=1, source_target_pairs={{0,4},{4,0},{8,12},{12,8},{16,20},{20,16},{24,28},{28,24},{1,5},{5... | collective-permute-start | bytes 393224 | tf_op jit(solution)/shard_map/ppermute | solution.py:233

commit v6 on v5

--- a/solution.py
+++ b/solution.py
@@ -101,6 +101,15 @@
     for copy in copies[2:6]:
         copy.wait()
     k_side = k_side_v[...].T
+
+    def masked(scores):
+        blocks = []
+        for lo in range(0, seq_len, 128):
+            hi = min(lo + 128, seq_len)
+            part = scores[lo:hi, :hi] + bias[lo:hi, :hi]
+            blocks.append(jnp.concatenate([part, scores[lo:hi, hi:]], axis=1) if hi < seq_len else part)
+        return jnp.concatenate(blocks, axis=0)
+
     found = []
     for h in range(heads):
         q_main = q_main_v[:, h * head_dim : (h + 1) * head_dim]
@@ -109,7 +118,7 @@
         keys = kv_all[:, h * width : h * width + head_dim]
         values = kv_all[:, h * width + head_dim : (h + 1) * width]
         k_all = jnp.concatenate([keys, k_side], axis=1)
-        scores = mm_nt(k_all, q_all) + bias[...]
+        scores = masked(mm_nt(k_all, q_all))
         top = jnp.max(scores, axis=0, keepdims=True)
         terms = jnp.exp2((scores - top) * (scale * log2_e))
         inv = 1.0 / jnp.sum(terms, axis=0, keepdims=True)
@@ -166,13 +175,14 @@
     plain[...] = by_head(beta_second * second_plain[...])
 
 
+def by_row(x, heads):
+    return jnp.swapaxes(x.reshape(heads, x.shape[0] // heads, x.shape[1]), 0, 1)
+
+
 def soap_kernel(before, turn, first, rot, plain, *refs):
     parts, (slab_out, new_first, new_second, new_plain) = refs[:-4], refs[-4:]
-    rows, heads, latent_dim = new_first.shape
+    rows, heads, latent_dim = slab_out.shape
     count = rows * heads
-
-    def by_row(x):
-        return jnp.swapaxes(x.reshape(heads, rows, latent_dim), 0, 1)
 
     grad = functools.reduce(jnp.add, [p[...].astype(f32) for p in parts]).reshape(count, latent_dim)
     rotated = mm(grad.astype(bf16), turn[...])
@@ -183,10 +193,10 @@
     turned = mm_nt(stacked, turn[...])
     direction = blend_share * turned[:count] + blend_share * turned[count:] / (jnp.sqrt(plain_sq) + epsilon)
     old = before[...]
-    slab_out[...] = by_row(old - learn_rate * (direction + decay_rate * old)).astype(bf16)
-    new_first[...] = by_row(moment)
-    new_second[...] = by_row(rot_sq)
-    new_plain[...] = by_row(plain_sq)
+    slab_out[...] = by_row(old - learn_rate * (direction + decay_rate * old), heads).astype(bf16)
+    new_first[...] = moment
+    new_second[...] = rot_sq
+    new_plain[...] = plain_sq
 
 
 def row_copies(slabs, out, sems, core):
@@ -201,12 +211,14 @@
 
 
 def place_own_kernel(chips, *refs):
-    slabs, state, (out, *new_state, sems) = refs[:chips], refs[chips : chips + 3], refs[chips + 3 :]
+    slabs, state, (out, *rest) = refs[:chips], refs[chips : chips + 3], refs[chips + 3 :]
+    new_state, stages, sems = rest[:3], rest[3:6], rest[6]
     copies = row_copies(slabs, out, sems, place_of()[1])
-    more = [pltpu.make_async_copy(a, b, sems.at[chips + i]) for i, (a, b) in enumerate(zip(state, new_state))]
-    for copy in more:
-        copy.start()
-    for copy in copies + more:
+    for i, (held, stage, new) in enumerate(zip(state, stages, new_state)):
+        stage[...] = by_row(held[...], new.shape[1])
+        copies.append(pltpu.make_async_copy(stage, new, sems.at[chips + i]))
+        copies[-1].start()
+    for copy in copies:
         copy.wait()
 
 
@@ -314,7 +326,7 @@
     )(own_weight, basis, first_moment, second_rot, second_plain)
     new_slab, new_first, new_second, new_plain = pl.pallas_call(
         soap_kernel,
-        out_shape=(pltpu.VMEM(state, bf16),) + (pltpu.VMEM(state, f32),) * 3,
+        out_shape=(pltpu.VMEM(state, bf16),) + (pltpu.VMEM(flat, f32),) * 3,
         in_specs=[in_vmem] * (5 + chips),
         out_specs=(in_vmem,) * 4,
         compiler_params=limit_mib(8),
@@ -328,7 +340,7 @@
         out_shape=(pltpu.HBM((width, heads, latent_dim), bf16),) + (pltpu.HBM(state, f32),) * 3,
         in_specs=[in_vmem] * (chips + 3),
         out_specs=(in_hbm,) * 4,
-        scratch_shapes=[pltpu.SemaphoreType.DMA((chips + 3,))],
+        scratch_shapes=[pltpu.VMEM(state, f32)] * 3 + [pltpu.SemaphoreType.DMA((chips + 3,))],
         compiler_params=limit_mib(4),
         name="place_own",
     )(*mine, new_first, new_second, new_plain)

time: 34.3 us -> 34.2 us (level)
  transfers between devices with their start and end apart: 14 -> 14, of which waited for: 4 -> 4; matrix products, arithmetic and copies ran while one was open for 0% -> 0% of each run, Pallas kernels for 9% -> 8%
where the time goes in v6:
time: 34.2 us; the launch traced here: 34 us
  starting transfers between devices  17.7 us (52%)
  Pallas kernels  12 us (35%)
  waiting for transfers between devices  2.95 us (9%)
  between operations  1.4 us (4%)
    ppermute x3, starting transfers between devices, part_move(): lax.ppermute(x, 'tensor', [(i, (i + s) % parts) for i in range(parts)])  8.21 us
    pallas_call x1, Pallas kernels, local(): pl.pallas_call(attend_kernel, out_shape=(pltpu.VMEM((chips,) + piece, bf1...  8.06 us
    ppermute x6, starting transfers between devices, chip_move(): return lax.ppermute(x, 'dp', pairs)  8.02 us
    ppermute x6, waiting for transfers between devices, chip_move(): return lax.ppermute(x, 'dp', pairs)  2.22 us
    ppermute x5, starting transfers between devices, core_swap(): return lax.ppermute(x, 'dp', [(i, i ^ 1) for i in range(dp)])  1.49 us
    pallas_call x1, Pallas kernels, local(): pl.pallas_call(functools.partial(place_own_kernel, chips), out_shape=(plt...  1.12 us
    pallas_call x1, Pallas kernels, local(): pl.pallas_call(functools.partial(place_rest_kernel, chips), out_shape=(pl...  0.9 us
    pallas_call x1, Pallas kernels, local(): pl.pallas_call(latent_kernel, out_shape=[pltpu.VMEM((part_rows, latent_di...  0.81 us
  transfers between devices with their start and end apart: 14, of which 4 were waited for; matrix products, arithmetic and copies ran while one was open for 0% of the time, Pallas kernels for 8%

profile of v6, /device:TPU:0, one launch (start us, length us, event | category | flops | bytes accessed | tf_op | source)
XLA Modules:
  0.0 34.0 jit_solution(15966901534119253145)
XLA Ops:
  1.3 8.1 %attend.1 = (bf16[4,4,32,512]{3,2,1,0:T(8,128)(2,1)S(1)}, bf16[4,4,32,512]{3,2,1,0:T(8,128)(2,1)S(1)}, bf16[576,1024]{1,0:T(8,128)(2,1)S(1)}, bf16[1024,512]{1,0:T(8,128)(2,1)S(1)}, bf16[32,4,512]{2,1,0:T(4,128)(2,1)S(1)}) custom-call(s32[8,128]{1,0:T(8,128)S(1)} %broadcast_in_dim.2.offsets, bf16[576,512]{1,0:T(8,128)(2,1)} %latent.1, ...), custom_call_target="tpu_custom_call" | custom-call | flops 3623878656 | bytes 33554432 | tf_op jit(solution)/shard_map/attend/pallas_call | solution.py:259
  9.4 0.5 %collective-permute-start = (bf16[4,4,32,512]{3,2,1,0:T(8,128)(2,1)S(1)}, bf16[4,4,32,512]{3,2,1,0:T(8,128)(2,1)S(1)}, u32[]{:S(2)}, u32[]{:S(2)}) collective-permute-start(bf16[4,4,32,512]{3,2,1,0:T(8,128)(2,1)S(1)} %get-tuple-element.58), channel_id=1, source_target_pairs={{0,4},{4,0},{8,12},{12,8},{16,20},{20,16},{24,28},{28,24},{1,5},{5... | collective-permute-start | bytes 1572872 | tf_op jit(solution)/shard_map/ppermute | solution.py:245
  9.9 0.8 %latent_share.1 = (bf16[144,512]{1,0:T(8,128)(2,1)S(1)}, bf16[144,512]{1,0:T(8,128)(2,1)S(1)}, bf16[144,512]{1,0:T(8,128)(2,1)S(1)}, bf16[144,512]{1,0:T(8,128)(2,1)S(1)}) custom-call(bf16[576,1024]{1,0:T(8,128)(2,1)S(1)} %get-tuple-element.63.grad_kv, bf16[1024,512]{1,0:T(8,128)(2,1)S(1)} %get-tuple-element.64.wall), custom_call_target="tpu_custom_call" | custom-call | tf_op jit(solution)/shard_map/latent_share/pallas_call | solution.py:297
  10.7 0.7 %collective-permute-done.came = bf16[4,4,32,512]{3,2,1,0:T(8,128)(2,1)S(1)} collective-permute-done((bf16[4,4,32,512]{3,2,1,0:T(8,128)(2,1)S(1)}, bf16[4,4,32,512]{3,2,1,0:T(8,128)(2,1)S(1)}, u32[]{:S(2)}, u32[]{:S(2)}) %collective-permute-start) | collective-permute-done | bytes 524320 | tf_op jit(solution)/shard_map/ppermute | solution.py:245
  11.4 0.1 pair_sum.1
  11.5 2.9 %collective-permute-start.1 = (bf16[4,32,512]{2,1,0:T(8,128)(2,1)S(1)}, bf16[4,32,512]{2,1,0:T(8,128)(2,1)S(1)}, u32[]{:S(2)}, u32[]{:S(2)}) collective-permute-start(bf16[4,32,512]{2,1,0:T(8,128)(2,1)S(1)} %get-tuple-element.70), channel_id=1, source_target_pairs={{0,8},{4,12},{8,0},{12,4},{16,24},{20,28},{24,16},{28,20},{1,9},{5... | collective-permute-start | bytes 393224 | tf_op jit(solution)/shard_map/ppermute | solution.py:252
  14.5 1.5 %collective-permute-start.2 = (bf16[4,32,512]{2,1,0:T(8,128)(2,1)S(1)}, bf16[4,32,512]{2,1,0:T(8,128)(2,1)S(1)}, u32[]{:S(2)}, u32[]{:S(2)}) collective-permute-start(bf16[4,32,512]{2,1,0:T(8,128)(2,1)S(1)} %get-tuple-element.71), channel_id=1, source_target_pairs={{0,16},{4,20},{8,24},{12,28},{16,0},{20,4},{24,8},{28,12},{1,17},{... | collective-permute-start | bytes 393224 | tf_op jit(solution)/shard_map/ppermute | solution.py:252
  16.0 0.0 collective-permute-start.3
  16.0 2.0 %collective-permute-start.11 = (bf16[144,512]{1,0:T(8,128)(2,1)S(1)}, bf16[144,512]{1,0:T(8,128)(2,1)S(1)}, u32[]{:S(2)}, u32[]{:S(2)}) collective-permute-start(bf16[144,512]{1,0:T(8,128)(2,1)S(1)} %get-tuple-element.79), channel_id=1, source_target_pairs={{0,1},{1,2},{2,3},{3,0},{4,5},{5,6},{6,7},{7,4},{8,9},{9,10},{10,1... | collective-permute-start | bytes 442376 | tf_op jit(solution)/shard_map/ppermute | solution.py:255
  18.0 2.6 %collective-permute-start.12 = (bf16[144,512]{1,0:T(8,128)(2,1)S(1)}, bf16[144,512]{1,0:T(8,128)(2,1)S(1)}, u32[]{:S(2)}, u32[]{:S(2)}) collective-permute-start(bf16[144,512]{1,0:T(8,128)(2,1)S(1)} %get-tuple-element.80), channel_id=1, source_target_pairs={{0,2},{1,3},{2,0},{3,1},{4,6},{5,7},{6,4},{7,5},{8,10},{9,11},{10,... | collective-permute-start | bytes 442376 | tf_op jit(solution)/shard_map/ppermute | solution.py:255
  20.6 0.3 ready.1
  20.9 1.6 %collective-permute-done.2.refs_2_ = bf16[4,32,512]{2,1,0:T(8,128)(2,1)S(1)} collective-permute-done((bf16[4,32,512]{2,1,0:T(8,128)(2,1)S(1)}, bf16[4,32,512]{2,1,0:T(8,128)(2,1)S(1)}, u32[]{:S(2)}, u32[]{:S(2)}) %collective-permute-start.2) | collective-permute-done | bytes 131104 | tf_op jit(solution)/shard_map/ppermute | solution.py:252
  22.5 0.0 collective-permute-done.3.refs_3_
  22.5 0.7 %soap.1 = (bf16[32,4,512]{2,1,0:T(4,128)(2,1)S(1)}, f32[128,512]{1,0:T(8,128)S(1)}, f32[128,512]{1,0:T(8,128)S(1)}, f32[128,512]{1,0:T(8,128)S(1)}) custom-call(f32[128,512]{1,0:T(8,128)S(1)} %get-tuple-element.52.before, bf16[512,512]{1,0:T(8,128)(2,1)S(1)} %get-tuple-element.53.turn, f32[128,512]{1,0:T(8,128)S(1)} %get-tuple-element.54.first, ...), custom_call_target="tpu_custom_call" | custom-call | tf_op jit(solution)/shard_map/soap/pallas_call | solution.py:327
  23.2 1.5 %collective-permute-start.6 = (bf16[32,4,512]{2,1,0:T(4,128)(2,1)S(1)}, bf16[32,4,512]{2,1,0:T(4,128)(2,1)S(1)}, u32[]{:S(2)}, u32[]{:S(2)}) collective-permute-start(bf16[32,4,512]{2,1,0:T(4,128)(2,1)S(1)} %get-tuple-element.73.refs_0_), channel_id=1, source_target_pairs={{0,24},{4,28},{8,16},{12,20},{16,8},{20,12},{24,0},{28,4},{1,25},{... | collective-permute-start | bytes 393224 | tf_op jit(solution)/shard_map/ppermute | solution.py:252
  24.8 1.5 %collective-permute-start.4 = (bf16[32,4,512]{2,1,0:T(4,128)(2,1)S(1)}, bf16[32,4,512]{2,1,0:T(4,128)(2,1)S(1)}, u32[]{:S(2)}, u32[]{:S(2)}) collective-permute-start(bf16[32,4,512]{2,1,0:T(4,128)(2,1)S(1)} %get-tuple-element.73.refs_0_), channel_id=1, source_target_pairs={{0,8},{4,12},{8,0},{12,4},{16,24},{20,28},{24,16},{28,20},{1,9},{5... | collective-permute-start | bytes 393224 | tf_op jit(solution)/shard_map/ppermute | solution.py:252
  26.3 0.5 %collective-permute-start.5 = (bf16[32,4,512]{2,1,0:T(4,128)(2,1)S(1)}, bf16[32,4,512]{2,1,0:T(4,128)(2,1)S(1)}, u32[]{:S(2)}, u32[]{:S(2)}) collective-permute-start(bf16[32,4,512]{2,1,0:T(4,128)(2,1)S(1)} %get-tuple-element.73.refs_0_), channel_id=1, source_target_pairs={{0,16},{4,20},{8,24},{12,28},{16,0},{20,4},{24,8},{28,12},{1,17},{... | collective-permute-start | bytes 393224 | tf_op jit(solution)/shard_map/ppermute | solution.py:252
  26.8 3.6 %collective-permute-start.13 = (bf16[144,512]{1,0:T(8,128)(2,1)S(1)}, bf16[144,512]{1,0:T(8,128)(2,1)S(1)}, u32[]{:S(2)}, u32[]{:S(2)}) collective-permute-start(bf16[144,512]{1,0:T(8,128)(2,1)S(1)} %get-tuple-element.81), channel_id=1, source_target_pairs={{0,3},{1,0},{2,1},{3,2},{4,7},{5,4},{6,5},{7,6},{8,11},{9,8},{10,9... | collective-permute-start | bytes 442376 | tf_op jit(solution)/shard_map/ppermute | solution.py:255
  30.4 0.5 %collective-permute-start.10 = (bf16[32,4,512]{2,1,0:T(4,128)(2,1)S(1)}, bf16[32,4,512]{2,1,0:T(4,128)(2,1)S(1)}, u32[]{:S(2)}, u32[]{:S(2)}) collective-permute-start(bf16[32,4,512]{2,1,0:T(4,128)(2,1)S(1)} %collective-permute-done.6.refs_3_), channel_id=1, source_target_pairs={{0,4},{4,0},{8,12},{12,8},{16,20},{20,16},{24,28},{28,24},{1,5},{5... | collective-permute-start | bytes 393224 | tf_op jit(solution)/shard_map/ppermute | solution.py:245
  30.9 0.5 %collective-permute-done.4.refs_1_ = bf16[32,4,512]{2,1,0:T(4,128)(2,1)S(1)} collective-permute-done((bf16[32,4,512]{2,1,0:T(4,128)(2,1)S(1)}, bf16[32,4,512]{2,1,0:T(4,128)(2,1)S(1)}, u32[]{:S(2)}, u32[]{:S(2)}) %collective-permute-start.4) | collective-permute-done | bytes 131104 | tf_op jit(solution)/shard_map/ppermute | solution.py:252
  31.5 0.1 collective-permute-done.5.refs_2_
  31.5 0.5 %collective-permute-start.9 = (bf16[32,4,512]{2,1,0:T(4,128)(2,1)S(1)}, bf16[32,4,512]{2,1,0:T(4,128)(2,1)S(1)}, u32[]{:S(2)}, u32[]{:S(2)}) collective-permute-start(bf16[32,4,512]{2,1,0:T(4,128)(2,1)S(1)} %collective-permute-done.5.refs_2_), channel_id=1, source_target_pairs={{0,4},{4,0},{8,12},{12,8},{16,20},{20,16},{24,28},{28,24},{1,5},{5... | collective-permute-start | bytes 393224 | tf_op jit(solution)/shard_map/ppermute | solution.py:245
  32.0 1.1 %place_own.1 = (bf16[256,4,512]{2,1,0:T(4,128)(2,1)}, f32[32,4,512]{2,1,0:T(4,128)}, f32[32,4,512]{2,1,0:T(4,128)}, f32[32,4,512]{2,1,0:T(4,128)}) custom-call(bf16[32,4,512]{2,1,0:T(4,128)(2,1)S(1)} %get-tuple-element.73.refs_0_, bf16[32,4,512]{2,1,0:T(4,128)(2,1)S(1)} %collective-permute-done.4.refs_1_, ...), custom_call_target="tpu_custom_call" | custom-call | tf_op jit(solution)/shard_map/place_own/pallas_call | solution.py:338
  33.1 0.9 %place_rest.1 = (bf16[256,4,512]{2,1,0:T(4,128)(2,1)}, bf16[144,512]{1,0:T(8,128)(2,1)}) custom-call(bf16[256,4,512]{2,1,0:T(4,128)(2,1)} %get-tuple-element.77.refs_0_, bf16[32,4,512]{2,1,0:T(4,128)(2,1)S(1)} %collective-permute-done.7.refs_1_, bf16[32,4,512]{2,1,0:T(4,128)(2,1)S(1)} %collective-permute-done.8.refs_2_, ...), custom_call_target="tpu_custom_call", output_to_operand_aliasing={{0}: (0, {})} | custom-call | tf_op jit(solution)/shard_map/place_rest/pallas_call | solution.py:347
  (20 shorter events, 0.0 us)
Async XLA Ops:
  9.4 2.1 %collective-permute-start = (bf16[4,4,32,512]{3,2,1,0:T(8,128)(2,1)S(1)}, bf16[4,4,32,512]{3,2,1,0:T(8,128)(2,1)S(1)}, u32[]{:S(2)}, u32[]{:S(2)}) collective-permute-start(bf16[4,4,32,512]{3,2,1,0:T(8,128)(2,1)S(1)} %get-tuple-element.58), channel_id=1, source_target_pairs={{0,4},{4,0},{8,12},{12,8},{16,20},{20,16},{24,28},{28,24},{1,5},{5... | collective-permute-start | bytes 1572872 | tf_op jit(solution)/shard_map/ppermute | solution.py:245
  9.9 10.7 %copy-start = (f32[512,512]{1,0:T(8,128)S(1)}, f32[512,512]{1,0:T(8,128)}, u32[]{:S(2)}) copy-start(f32[512,512]{1,0:T(8,128)} %basis) | copy-start | bytes 3145732
  9.9 10.7 %copy-start.1 = (f32[32,4,512]{2,1,0:T(4,128)S(1)}, f32[32,4,512]{2,1,0:T(4,128)}, u32[]{:S(2)}) copy-start(f32[32,4,512]{2,1,0:T(4,128)} %first_moment) | copy-start | bytes 786436
  9.9 10.7 %copy-start.2 = (f32[32,4,512]{2,1,0:T(4,128)S(1)}, f32[32,4,512]{2,1,0:T(4,128)}, u32[]{:S(2)}) copy-start(f32[32,4,512]{2,1,0:T(4,128)} %second_rot) | copy-start | bytes 786436
  9.9 10.7 %copy-start.3 = (f32[32,4,512]{2,1,0:T(4,128)S(1)}, f32[32,4,512]{2,1,0:T(4,128)}, u32[]{:S(2)}) copy-start(f32[32,4,512]{2,1,0:T(4,128)} %second_plain) | copy-start | bytes 786436
  11.5 9.4 %collective-permute-start.1 = (bf16[4,32,512]{2,1,0:T(8,128)(2,1)S(1)}, bf16[4,32,512]{2,1,0:T(8,128)(2,1)S(1)}, u32[]{:S(2)}, u32[]{:S(2)}) collective-permute-start(bf16[4,32,512]{2,1,0:T(8,128)(2,1)S(1)} %get-tuple-element.70), channel_id=1, source_target_pairs={{0,8},{4,12},{8,0},{12,4},{16,24},{20,28},{24,16},{28,20},{1,9},{5... | collective-permute-start | bytes 393224 | tf_op jit(solution)/shard_map/ppermute | solution.py:252
  14.5 8.1 %collective-permute-start.2 = (bf16[4,32,512]{2,1,0:T(8,128)(2,1)S(1)}, bf16[4,32,512]{2,1,0:T(8,128)(2,1)S(1)}, u32[]{:S(2)}, u32[]{:S(2)}) collective-permute-start(bf16[4,32,512]{2,1,0:T(8,128)(2,1)S(1)} %get-tuple-element.71), channel_id=1, source_target_pairs={{0,16},{4,20},{8,24},{12,28},{16,0},{20,4},{24,8},{28,12},{1,17},{... | collective-permute-start | bytes 393224 | tf_op jit(solution)/shard_map/ppermute | solution.py:252
  16.0 6.6 %collective-permute-start.3 = (bf16[4,32,512]{2,1,0:T(8,128)(2,1)S(1)}, bf16[4,32,512]{2,1,0:T(8,128)(2,1)S(1)}, u32[]{:S(2)}, u32[]{:S(2)}) collective-permute-start(bf16[4,32,512]{2,1,0:T(8,128)(2,1)S(1)} %get-tuple-element.72), channel_id=1, source_target_pairs={{0,24},{4,28},{8,16},{12,20},{16,8},{20,12},{24,0},{28,4},{1,25},{... | collective-permute-start | bytes 393224 | tf_op jit(solution)/shard_map/ppermute | solution.py:252
  16.0 10.8 %collective-permute-start.11 = (bf16[144,512]{1,0:T(8,128)(2,1)S(1)}, bf16[144,512]{1,0:T(8,128)(2,1)S(1)}, u32[]{:S(2)}, u32[]{:S(2)}) collective-permute-start(bf16[144,512]{1,0:T(8,128)(2,1)S(1)} %get-tuple-element.79), channel_id=1, source_target_pairs={{0,1},{1,2},{2,3},{3,0},{4,5},{5,6},{6,7},{7,4},{8,9},{9,10},{10,1... | collective-permute-start | bytes 442376 | tf_op jit(solution)/shard_map/ppermute | solution.py:255
  18.0 12.4 %collective-permute-start.12 = (bf16[144,512]{1,0:T(8,128)(2,1)S(1)}, bf16[144,512]{1,0:T(8,128)(2,1)S(1)}, u32[]{:S(2)}, u32[]{:S(2)}) collective-permute-start(bf16[144,512]{1,0:T(8,128)(2,1)S(1)} %get-tuple-element.80), channel_id=1, source_target_pairs={{0,2},{1,3},{2,0},{3,1},{4,6},{5,7},{6,4},{7,5},{8,10},{9,11},{10,... | collective-permute-start | bytes 442376 | tf_op jit(solution)/shard_map/ppermute | solution.py:255
  23.2 7.2 %collective-permute-start.6 = (bf16[32,4,512]{2,1,0:T(4,128)(2,1)S(1)}, bf16[32,4,512]{2,1,0:T(4,128)(2,1)S(1)}, u32[]{:S(2)}, u32[]{:S(2)}) collective-permute-start(bf16[32,4,512]{2,1,0:T(4,128)(2,1)S(1)} %get-tuple-element.73.refs_0_), channel_id=1, source_target_pairs={{0,24},{4,28},{8,16},{12,20},{16,8},{20,12},{24,0},{28,4},{1,25},{... | collective-permute-start | bytes 393224 | tf_op jit(solution)/shard_map/ppermute | solution.py:252
  24.8 6.7 %collective-permute-start.4 = (bf16[32,4,512]{2,1,0:T(4,128)(2,1)S(1)}, bf16[32,4,512]{2,1,0:T(4,128)(2,1)S(1)}, u32[]{:S(2)}, u32[]{:S(2)}) collective-permute-start(bf16[32,4,512]{2,1,0:T(4,128)(2,1)S(1)} %get-tuple-element.73.refs_0_), channel_id=1, source_target_pairs={{0,8},{4,12},{8,0},{12,4},{16,24},{20,28},{24,16},{28,20},{1,9},{5... | collective-permute-start | bytes 393224 | tf_op jit(solution)/shard_map/ppermute | solution.py:252
  26.3 5.2 %collective-permute-start.5 = (bf16[32,4,512]{2,1,0:T(4,128)(2,1)S(1)}, bf16[32,4,512]{2,1,0:T(4,128)(2,1)S(1)}, u32[]{:S(2)}, u32[]{:S(2)}) collective-permute-start(bf16[32,4,512]{2,1,0:T(4,128)(2,1)S(1)} %get-tuple-element.73.refs_0_), channel_id=1, source_target_pairs={{0,16},{4,20},{8,24},{12,28},{16,0},{20,4},{24,8},{28,12},{1,17},{... | collective-permute-start | bytes 393224 | tf_op jit(solution)/shard_map/ppermute | solution.py:252
  26.8 6.3 %collective-permute-start.13 = (bf16[144,512]{1,0:T(8,128)(2,1)S(1)}, bf16[144,512]{1,0:T(8,128)(2,1)S(1)}, u32[]{:S(2)}, u32[]{:S(2)}) collective-permute-start(bf16[144,512]{1,0:T(8,128)(2,1)S(1)} %get-tuple-element.81), channel_id=1, source_target_pairs={{0,3},{1,0},{2,1},{3,2},{4,7},{5,4},{6,5},{7,6},{8,11},{9,8},{10,9... | collective-permute-start | bytes 442376 | tf_op jit(solution)/shard_map/ppermute | solution.py:255
  30.4 2.7 %collective-permute-start.7 = (bf16[32,4,512]{2,1,0:T(4,128)(2,1)S(1)}, bf16[32,4,512]{2,1,0:T(4,128)(2,1)S(1)}, u32[]{:S(2)}, u32[]{:S(2)}) collective-permute-start(bf16[32,4,512]{2,1,0:T(4,128)(2,1)S(1)} %get-tuple-element.73.refs_0_), channel_id=1, source_target_pairs={{0,4},{4,0},{8,12},{12,8},{16,20},{20,16},{24,28},{28,24},{1,5},{5... | collective-permute-start | bytes 393224 | tf_op jit(solution)/shard_map/ppermute | solution.py:245
  30.4 2.7 %collective-permute-start.10 = (bf16[32,4,512]{2,1,0:T(4,128)(2,1)S(1)}, bf16[32,4,512]{2,1,0:T(4,128)(2,1)S(1)}, u32[]{:S(2)}, u32[]{:S(2)}) collective-permute-start(bf16[32,4,512]{2,1,0:T(4,128)(2,1)S(1)} %collective-permute-done.6.refs_3_), channel_id=1, source_target_pairs={{0,4},{4,0},{8,12},{12,8},{16,20},{20,16},{24,28},{28,24},{1,5},{5... | collective-permute-start | bytes 393224 | tf_op jit(solution)/shard_map/ppermute | solution.py:245
  31.5 1.7 %collective-permute-start.8 = (bf16[32,4,512]{2,1,0:T(4,128)(2,1)S(1)}, bf16[32,4,512]{2,1,0:T(4,128)(2,1)S(1)}, u32[]{:S(2)}, u32[]{:S(2)}) collective-permute-start(bf16[32,4,512]{2,1,0:T(4,128)(2,1)S(1)} %collective-permute-done.4.refs_1_), channel_id=1, source_target_pairs={{0,4},{4,0},{8,12},{12,8},{16,20},{20,16},{24,28},{28,24},{1,5},{5... | collective-permute-start | bytes 393224 | tf_op jit(solution)/shard_map/ppermute | solution.py:245
  31.5 1.6 %collective-permute-start.9 = (bf16[32,4,512]{2,1,0:T(4,128)(2,1)S(1)}, bf16[32,4,512]{2,1,0:T(4,128)(2,1)S(1)}, u32[]{:S(2)}, u32[]{:S(2)}) collective-permute-start(bf16[32,4,512]{2,1,0:T(4,128)(2,1)S(1)} %collective-permute-done.5.refs_2_), channel_id=1, source_target_pairs={{0,4},{4,0},{8,12},{12,8},{16,20},{20,16},{24,28},{28,24},{1,5},{5... | collective-permute-start | bytes 393224 | tf_op jit(solution)/shard_map/ppermute | solution.py:245
